TPU v7x, 32 devices: a whole 2x2x4 slice. The times are simulated.
32 devices in a mesh: blk: 8 (over z, y), dp: 4 (over x, core).
Axes of the slice: x: 2, y: 2, z: 4, core: 2. Of those that a mesh axis runs over, the one named last changes fastest.
Arguments:
- dec_input: bfloat16 [1024, 8, 768], P('blk', 'dp'), may hold values from -6 to 6
- enc_output: bfloat16 [8, 7168, 768], P('dp', 'blk'), may hold values from -6 to 6
- lengths: int32 [8, 16], P('dp'), may hold values from 56 to 448, as said below
- gains: bfloat16 [3, 768], replicated, may hold values from 0.25 to 1.75
- self_qkv: bfloat16 [3, 768, 768], replicated, may hold values from -0.21875 to 0.21875
- self_out: bfloat16 [768, 768], replicated, may hold values from -0.875 to 0.875
- cross_q: bfloat16 [768, 768], replicated, may hold values from -0.21875 to 0.21875
- cross_kv: bfloat16 [2, 768, 768], replicated, may hold values from -0.21875 to 0.21875
- cross_out: bfloat16 [768, 768], replicated, may hold values from -8 to 8
- ffn_in: bfloat16 [768, 3072], replicated, may hold values from -0.21875 to 0.21875
- ffn_out: bfloat16 [3072, 768], replicated, may hold values from -0.109375 to 0.109375
- cotangent: bfloat16 [1024, 8, 768], P('blk', 'dp'), may hold values from -6 to 6
Outputs:
- output: bfloat16 [1024, 8, 768], P('blk', 'dp')
- dec_grad: bfloat16 [1024, 8, 768], P('blk', 'dp')
- enc_grad: bfloat16 [8, 7168, 768], P('dp', 'blk')
- gains_grad: float32 [3, 768], replicated
- self_qkv_grad: float32 [3, 768, 768], P(None, 'blk', 'dp')
- self_out_grad: float32 [768, 768], P('blk', 'dp')
- cross_q_grad: float32 [768, 768], P('blk', 'dp')
- cross_kv_grad: float32 [2, 768, 768], P(None, 'blk', 'dp')
- cross_out_grad: float32 [768, 768], P('blk', 'dp')
- ffn_in_grad: float32 [768, 3072], P('blk', 'dp')
- ffn_out_grad: float32 [3072, 768], P('blk', 'dp')
Inputs may be any that keep to these rules, and one draw needn't show every extreme that they name: `lengths`: in every aligned group of 2 queries (those of one dp index) the query at one seed-drawn place has all 16 passages full, and the first passage of the other query holds 56 tokens.
All inputs are finite; a program needn't handle non-finite values.
Results may differ from a plain program's by a relative error of at most 0.04.
Values may be sent and summed in bfloat16 or wider, within the bound.
No kernel may reach another device: no remote copies, remote signals or barrier semaphores. Data moves between devices by JAX's collectives and lax.ppermute only.
A program may use at most 256 MiB of HBM per device.

v0:
```python
import jax
import jax.numpy as jnp
from jax import lax
from jax.sharding import PartitionSpec as P

HEAD_DIM = 64
SLOTS = 448


epsilon = 1e-06
negative_fill = -1e30


def merged(array, axis, join):
    gathered = jax.tree.map(
        lambda a, kind: lax.all_gather(a.astype(kind), axis), array, (jnp.bfloat16, jnp.bfloat16)
    )

    def take(source):
        return jax.tree.map(
            lambda a, own: lax.dynamic_index_in_dim(a, source, 0, False).astype(own.dtype),
            gathered,
            array,
        )

    return lax.fori_loop(
        1, lax.axis_size(axis), lambda source, state: join(state, take(source)), take(0)
    )


def normed(values, gain):
    return values * lax.rsqrt(jnp.mean(values * values, axis=-1, keepdims=True) + epsilon) * gain


def product(left, right):
    return jnp.einsum("...k,kn->...n", left, right, preferred_element_type=jnp.float32)


def pulled(grad, weight):
    return jnp.einsum("...n,kn->...k", grad, weight, preferred_element_type=jnp.float32)


def outer(left, right):
    flat_left = left.reshape(-1, left.shape[-1])
    flat_right = right.reshape(-1, right.shape[-1])
    return lax.dot_general(
        flat_left, flat_right, (((0,), (0,)), ((), ())), preferred_element_type=jnp.float32
    )


def norm_pull(values, gain, grad):
    unused, pull = jax.vjp(normed, values, gain)
    return pull(grad)


def body(
    dec_input,
    enc_output,
    lengths,
    gains,
    self_qkv,
    self_out,
    cross_q,
    cross_kv,
    cross_out,
    ffn_in,
    ffn_out,
    cotangent,
):
    seg, seqs, width = dec_input.shape
    heads = width // HEAD_DIM
    blocks = lax.axis_size("blk")
    place = lax.axis_index("blk")
    length = seg * blocks
    enc_rows = enc_output.shape[1]
    gain_values = gains.astype(jnp.float32)
    inputs = dec_input.astype(jnp.float32)
    first_low = normed(inputs, gain_values[0]).astype(jnp.bfloat16)
    projected = jnp.einsum(
        "tsk,ckn->ctsn", first_low, self_qkv, preferred_element_type=jnp.float32
    ).astype(jnp.bfloat16)
    self_query, self_key, self_value = (projected[0], projected[1], projected[2])
    all_keys, all_values = (
        lax.all_gather(self_key, "blk", axis=0, tiled=True),
        lax.all_gather(self_value, "blk", axis=0, tiled=True),
    )
    split_query = self_query.reshape(seg, seqs, heads, HEAD_DIM)
    split_keys_all = all_keys.reshape(length, seqs, heads, HEAD_DIM)
    split_values_all = all_values.reshape(length, seqs, heads, HEAD_DIM)
    query_pos = place * seg + jnp.arange(seg)
    causal = jnp.arange(length)[None, :] <= query_pos[:, None]

    def self_scores():
        raw = (
            jnp.einsum(
                "tshe,ushe->shtu", split_query, split_keys_all, preferred_element_type=jnp.float32
            )
            * 0.125
        )
        return jnp.where(causal[None, None], raw, negative_fill)

    scores = self_scores()
    top = jnp.max(scores, axis=-1, keepdims=True)
    self_lse = top + jnp.log(jnp.sum(jnp.exp(scores - top), axis=-1, keepdims=True))
    self_low = jnp.exp(scores - self_lse).astype(jnp.bfloat16)
    self_mix = jnp.einsum(
        "shtu,ushe->tshe", self_low, split_values_all, preferred_element_type=jnp.float32
    )
    self_mix = self_mix.reshape(seg, seqs, width).astype(jnp.bfloat16)
    after_self = inputs + product(self_mix, self_out)
    second_low = normed(after_self, gain_values[1]).astype(jnp.bfloat16)
    cross_query = product(second_low, cross_q).astype(jnp.bfloat16)
    key_value = jnp.einsum(
        "sek,ckn->csen", enc_output, cross_kv, preferred_element_type=jnp.float32
    ).astype(jnp.bfloat16)
    cross_key, cross_value = (key_value[0], key_value[1])
    split_keys = cross_key.reshape(seqs, enc_rows, heads, HEAD_DIM)
    split_values = cross_value.reshape(seqs, enc_rows, heads, HEAD_DIM)
    slot = place * enc_rows + jnp.arange(enc_rows)
    match = (slot // SLOTS)[None, :, None] == jnp.arange(lengths.shape[1])[None, None, :]
    filled = jnp.sum(jnp.where(match, lengths[:, None, :], 0), axis=-1)
    valid = (slot % SLOTS)[None, :] < filled

    def cross_raw(query_block):
        split_block = query_block.reshape(-1, seqs, heads, HEAD_DIM)
        raw = (
            jnp.einsum(
                "tshe,sxhe->shtx", split_block, split_keys, preferred_element_type=jnp.float32
            )
            * 0.125
        )
        return jnp.where(valid[:, None, None, :], raw, negative_fill)

    all_queries = lax.all_gather(cross_query, "blk", axis=0, tiled=True)
    count_blocks = length // seg
    query_blocks = all_queries.reshape(count_blocks, seg, seqs, width)

    def block_stats(query_block):
        raw = cross_raw(query_block)
        block_top = jnp.max(raw, axis=-1)
        return (block_top, jnp.sum(jnp.exp(raw - block_top[..., None]), axis=-1))

    local_top, local_total = lax.map(block_stats, query_blocks)

    def combine(earlier, later):
        joint = jnp.maximum(earlier[0], later[0])
        return (
            joint,
            earlier[1] * jnp.exp(earlier[0] - joint) + later[1] * jnp.exp(later[0] - joint),
        )

    global_top, global_total = merged((local_top, local_total), "blk", combine)
    log_total = global_top + jnp.log(global_total)
    count = seg * lax.axis_size("blk")
    part_queries = all_queries.reshape(count // seg, seg, seqs, width)

    def one_block(pack):
        query_block, log_block = pack
        prob = jnp.exp(cross_raw(query_block) - log_block[..., None]).astype(jnp.bfloat16)
        mixed = jnp.einsum(
            "shtx,sxhe->tshe", prob, split_values, preferred_element_type=jnp.float32
        )
        return mixed.reshape(seg, seqs, width)

    cross_mix = lax.psum_scatter(
        lax.map(one_block, (part_queries, log_total))
        .reshape(count, seqs, width)
        .astype(jnp.bfloat16),
        "blk",
        scatter_dimension=0,
        tiled=True,
    )
    after_cross = after_self + product(cross_mix, cross_out)
    third_low = normed(after_cross, gain_values[2]).astype(jnp.bfloat16)
    hidden_pre = product(third_low, ffn_in)
    hidden_low = jax.nn.gelu(hidden_pre).astype(jnp.bfloat16)
    output = (after_cross + product(hidden_low, ffn_out)).astype(jnp.bfloat16)
    upstream = cotangent.astype(jnp.float32)
    ffn_out_grad = outer(hidden_low, cotangent)
    hidden_grad = pulled(cotangent, ffn_out)
    unused, gelu_pull = jax.vjp(jax.nn.gelu, hidden_pre)
    pre_low = gelu_pull(hidden_grad)[0].astype(jnp.bfloat16)
    ffn_in_grad = outer(third_low, pre_low)
    step_grad, gain_three = norm_pull(after_cross, gain_values[2], pulled(pre_low, ffn_in))
    cross_grad = upstream + step_grad
    cross_grad_low = cross_grad.astype(jnp.bfloat16)
    cross_out_grad = outer(cross_mix, cross_grad_low)
    mix_grad = pulled(cross_grad_low, cross_out).astype(jnp.bfloat16)
    all_grads = lax.all_gather(mix_grad, "blk", axis=0, tiled=True)
    grad_blocks = all_grads.reshape(count_blocks, seg, seqs, width)

    def block_rows(pack):
        query_block, log_block, grad_block = pack
        prob = jnp.exp(cross_raw(query_block) - log_block[..., None])
        split_grad = grad_block.reshape(seg, seqs, heads, HEAD_DIM)
        prob_grad = jnp.einsum(
            "tshe,sxhe->shtx", split_grad, split_values, preferred_element_type=jnp.float32
        )
        return jnp.sum(prob * prob_grad, axis=-1)

    row_part = lax.map(block_rows, (query_blocks, log_total, grad_blocks))
    row_blocks = lax.psum(row_part.astype(jnp.bfloat16), "blk").astype(jnp.float32)

    def cross_back(carry, pack):
        key_total, value_total = carry
        query_block, log_block, grad_block, row_block = pack
        prob = jnp.exp(cross_raw(query_block) - log_block[..., None])
        split_grad = grad_block.reshape(seg, seqs, heads, HEAD_DIM)
        prob_grad = jnp.einsum(
            "tshe,sxhe->shtx", split_grad, split_values, preferred_element_type=jnp.float32
        )
        score_low = (prob * (prob_grad - row_block[..., None])).astype(jnp.bfloat16)
        query_term = (
            jnp.einsum("shtx,sxhe->tshe", score_low, split_keys, preferred_element_type=jnp.float32)
            * 0.125
        )
        split_block = query_block.reshape(seg, seqs, heads, HEAD_DIM)
        key_total = (
            key_total
            + jnp.einsum(
                "shtx,tshe->sxhe", score_low, split_block, preferred_element_type=jnp.float32
            )
            * 0.125
        )
        value_total = value_total + jnp.einsum(
            "shtx,tshe->sxhe",
            prob.astype(jnp.bfloat16),
            split_grad,
            preferred_element_type=jnp.float32,
        )
        return ((key_total, value_total), query_term.reshape(seg, seqs, width))

    zeros = jnp.zeros((seqs, enc_rows, heads, HEAD_DIM), jnp.float32)
    (key_total, value_total), query_terms = lax.scan(
        cross_back, (zeros, zeros), (query_blocks, log_total, grad_blocks, row_blocks)
    )
    query_grad = lax.psum_scatter(
        query_terms.reshape(length, seqs, width).astype(jnp.bfloat16),
        "blk",
        scatter_dimension=0,
        tiled=True,
    )
    key_low = key_total.reshape(seqs, enc_rows, width).astype(jnp.bfloat16)
    value_low = value_total.reshape(seqs, enc_rows, width).astype(jnp.bfloat16)
    cross_q_grad = outer(second_low, query_grad)
    cross_kv_grad = jnp.stack([outer(enc_output, key_low), outer(enc_output, value_low)])
    enc_grad = (pulled(key_low, cross_kv[0]) + pulled(value_low, cross_kv[1])).astype(jnp.bfloat16)
    step_grad, gain_two = norm_pull(after_self, gain_values[1], pulled(query_grad, cross_q))
    self_grad = cross_grad + step_grad
    self_grad_low = self_grad.astype(jnp.bfloat16)
    self_out_grad = outer(self_mix, self_grad_low)
    mixed_grad = pulled(self_grad_low, self_out).astype(jnp.bfloat16)
    split_mixed = mixed_grad.reshape(seg, seqs, heads, HEAD_DIM)
    self_prob = jnp.exp(self_scores() - self_lse)
    prob_grad = jnp.einsum(
        "tshe,ushe->shtu", split_mixed, split_values_all, preferred_element_type=jnp.float32
    )
    row_sum = jnp.sum(self_prob * prob_grad, axis=-1, keepdims=True)
    score_low = (self_prob * (prob_grad - row_sum)).astype(jnp.bfloat16)
    self_query_grad = (
        jnp.einsum("shtu,ushe->tshe", score_low, split_keys_all, preferred_element_type=jnp.float32)
        * 0.125
    )
    self_query_grad = self_query_grad.reshape(seg, seqs, width).astype(jnp.bfloat16)
    key_term = (
        jnp.einsum(
            "shtu,tshe->ushe", score_low, split_query, preferred_element_type=jnp.float32
        ).reshape(length, seqs, width)
        * 0.125
    )
    value_term = jnp.einsum(
        "shtu,tshe->ushe",
        self_prob.astype(jnp.bfloat16),
        split_mixed,
        preferred_element_type=jnp.float32,
    ).reshape(length, seqs, width)
    self_key_grad, self_value_grad = (
        lax.psum_scatter(
            key_term.astype(jnp.bfloat16), "blk", scatter_dimension=0, tiled=True
        ).astype(jnp.float32),
        lax.psum_scatter(
            value_term.astype(jnp.bfloat16), "blk", scatter_dimension=0, tiled=True
        ).astype(jnp.float32),
    )
    self_key_low = self_key_grad.astype(jnp.bfloat16)
    self_value_low = self_value_grad.astype(jnp.bfloat16)
    self_qkv_grad = jnp.stack(
        [
            outer(first_low, self_query_grad),
            outer(first_low, self_key_low),
            outer(first_low, self_value_low),
        ]
    )
    first_back = (
        pulled(self_query_grad, self_qkv[0])
        + pulled(self_key_low, self_qkv[1])
        + pulled(self_value_low, self_qkv[2])
    )
    step_grad, gain_one = norm_pull(inputs, gain_values[0], first_back)
    dec_grad = (self_grad + step_grad).astype(jnp.bfloat16)
    gain_grads = lax.psum(jnp.stack([gain_one, gain_two, gain_three]), ("blk", "dp"))
    (
        qkv_part,
        self_out_part,
        cross_q_part,
        cross_kv_part,
        cross_out_part,
        ffn_in_part,
        ffn_out_part,
    ) = (
        lax.psum_scatter(
            self_qkv_grad.astype(jnp.bfloat16), "blk", scatter_dimension=1, tiled=True
        ).astype(jnp.float32),
        lax.psum_scatter(
            self_out_grad.astype(jnp.bfloat16), "blk", scatter_dimension=0, tiled=True
        ).astype(jnp.float32),
        lax.psum_scatter(
            cross_q_grad.astype(jnp.bfloat16), "blk", scatter_dimension=0, tiled=True
        ).astype(jnp.float32),
        lax.psum_scatter(
            cross_kv_grad.astype(jnp.bfloat16), "blk", scatter_dimension=1, tiled=True
        ).astype(jnp.float32),
        lax.psum_scatter(
            cross_out_grad.astype(jnp.bfloat16), "blk", scatter_dimension=0, tiled=True
        ).astype(jnp.float32),
        lax.psum_scatter(
            ffn_in_grad.astype(jnp.bfloat16), "blk", scatter_dimension=0, tiled=True
        ).astype(jnp.float32),
        lax.psum_scatter(
            ffn_out_grad.astype(jnp.bfloat16), "blk", scatter_dimension=0, tiled=True
        ).astype(jnp.float32),
    )
    final_grads = (
        lax.psum_scatter(
            qkv_part.astype(jnp.bfloat16), "dp", scatter_dimension=2, tiled=True
        ).astype(jnp.float32),
        lax.psum_scatter(
            self_out_part.astype(jnp.bfloat16), "dp", scatter_dimension=1, tiled=True
        ).astype(jnp.float32),
        lax.psum_scatter(
            cross_q_part.astype(jnp.bfloat16), "dp", scatter_dimension=1, tiled=True
        ).astype(jnp.float32),
        lax.psum_scatter(
            cross_kv_part.astype(jnp.bfloat16), "dp", scatter_dimension=2, tiled=True
        ).astype(jnp.float32),
        lax.psum_scatter(
            cross_out_part.astype(jnp.bfloat16), "dp", scatter_dimension=1, tiled=True
        ).astype(jnp.float32),
        lax.psum_scatter(
            ffn_in_part.astype(jnp.bfloat16), "dp", scatter_dimension=1, tiled=True
        ).astype(jnp.float32),
        lax.psum_scatter(
            ffn_out_part.astype(jnp.bfloat16), "dp", scatter_dimension=1, tiled=True
        ).astype(jnp.float32),
    )
    return (
        output,
        dec_grad,
        enc_grad,
        gain_grads,
        final_grads[0],
        final_grads[1],
        final_grads[2],
        final_grads[3],
        final_grads[4],
        final_grads[5],
        final_grads[6],
    )


def solution(mesh):
    placed = (
        P("blk", "dp", None),
        P("dp", "blk", None),
        P("dp", None),
        P(),
        P(),
        P(),
        P(),
        P(),
        P(),
        P(),
        P(),
        P("blk", "dp", None),
    )
    return jax.shard_map(
        body,
        mesh=mesh,
        in_specs=placed,
        out_specs=(
            P("blk", "dp", None),
            P("blk", "dp", None),
            P("dp", "blk", None),
            P(),
            P(None, "blk", "dp"),
            P("blk", "dp"),
            P("blk", "dp"),
            P(None, "blk", "dp"),
            P("blk", "dp"),
            P("blk", "dp"),
            P("blk", "dp"),
        ),
        check_vma=False,
    )
```

profile of v0, /device:TPU:0, one launch (start us, length us, event | category | flops | bytes accessed | tf_op | source)
XLA Modules:
  0.0 2004.5 jit_solution(15142740395570750294)
XLA Ops:
  15.9 61.1 %all-gather.15.cloned.1.call-done = bf16[1,1024,2,768]{3,1,0,2:T(8,128)(2,1)} async-done(((bf16[1,128,2,768]{3,1,0,2:T(8,128)(2,1)}), bf16[1,1024,2,768]{3,1,0,2:T(8,128)(2,1)}) %all-gather.15.cloned.1.call-update) | async-done | bytes 3145744 | tf_op jit(solution)/shard_map/all_gather | solution.py:84
  90.5 48.4 %all-gather.13.cloned.1.call-done = bf16[1,1024,2,768]{3,1,0,2:T(8,128)(2,1)} async-done(((bf16[1,128,2,768]{3,1,0,2:T(8,128)(2,1)}), bf16[1,1024,2,768]{3,1,0,2:T(8,128)(2,1)}) %all-gather.13.cloned.1.call-update) | async-done | bytes 3145744 | tf_op jit(solution)/shard_map/all_gather | solution.py:85
  166.0 48.6 %all-gather.9.cloned.1.call-done = bf16[1024,2,768]{2,0,1:T(8,128)(2,1)} async-done(((bf16[128,2,768]{2,0,1:T(8,128)(2,1)}), bf16[1024,2,768]{2,0,1:T(8,128)(2,1)}) %all-gather.9.cloned.1.call-update) | async-done | bytes 3145744 | tf_op jit(solution)/shard_map/all_gather | solution.py:134
  219.3 58.3 %while.64 = (s32[]{:T(128)}, bf16[8,2,12,128]{3,1,2,0:T(2,128)(2,1)S(1)}, bf16[8,2,12,128]{3,1,2,0:T(2,128)(2,1)S(1)}, pred[2,896]{1,0:T(4,128)(4,1)S(1)}, bf16[...) while((s32[]{:T(128)}, bf16[8,2,12,128]{3,1,2,0:T(2,128)(2,1)S(1)}, ...), condition=%wide.region_8.9_spmd, body=%wide.region_5.8_spmd.sunk | while | flops 371582976 | bytes 26023508 | solution.py:143
  277.6 31.2 %all-gather.2 = bf16[64,2,12,128]{3,1,2,0:T(2,128)(2,1)S(1)} all-gather(bf16[8,2,12,128]{3,1,2,0:T(2,128)(2,1)S(1)} %get-tuple-element.315), channel_id=4, replica_groups=mesh['blk'=8,'dp'=4] {'blk'}, dimensions={0}, use_global_device_ids=true | all-gather | bytes 442368 | tf_op jit(solution)/shard_map/all_gather | solution.py:16
  308.9 31.0 %all-gather.3 = bf16[64,2,12,128]{3,1,2,0:T(2,128)(2,1)S(1)} all-gather(bf16[8,2,12,128]{3,1,2,0:T(2,128)(2,1)S(1)} %get-tuple-element.316), channel_id=5, replica_groups=mesh['blk'=8,'dp'=4] {'blk'}, dimensions={0}, use_global_device_ids=true | all-gather | bytes 442368 | tf_op jit(solution)/shard_map/all_gather | solution.py:16
  350.4 82.1 %while.66 = (s32[]{:T(128)}, bf16[8,128,2,768]{3,1,0,2:T(8,128)(2,1)}, pred[2,896]{1,0:T(4,128)(4,1)S(1)}, bf16[8,128,2,768]{1,3,2,0:T(8,128)(2,1)}, bf16[2,896,...) while((s32[]{:T(128)}, ...), condition=%wide.region_12.13_spmd, body=%wide.region_11.12_spmd.sunk | while | flops 715653120 | bytes 8690013 | solution.py:166
  432.7 72.9 %reduce-scatter.30.cloned.1.call-done = bf16[128,2,768]{2,0,1:T(8,128)(2,1)} async-done(((bf16[1024,2,768]{2,0,1:T(8,128)(2,1)}), bf16[128,2,768]{2,0,1:T(8,128)(2,1)}) %reduce-scatter.30.cloned.1.call-update) | async-done | bytes 393232 | tf_op jit(solution)/shard_map/reduce_scatter | solution.py:165
  523.0 59.8 %all-gather.11.cloned.1.call-done = bf16[1024,2,768]{2,0,1:T(8,128)(2,1)} async-done(((bf16[128,2,768]{2,0,1:T(8,128)(2,1)}), bf16[1024,2,768]{2,0,1:T(8,128)(2,1)}) %all-gather.11.cloned.1.call-update) | async-done | bytes 3145744 | tf_op jit(solution)/shard_map/all_gather | solution.py:189
  587.4 72.8 %while.67 = (s32[]{:T(128)}, bf16[8,2,12,128]{3,2,1,0:T(8,128)(2,1)S(1)}, pred[2,896]{1,0:T(4,128)(4,1)S(1)}, bf16[8,128,2,768]{1,3,2,0:T(8,128)(2,1)}, bf16[2,8...) while((s32[]{:T(128)}, ...), condition=%wide.region_18.19_spmd, body=%wide.region_16.18_spmd.sunk | while | flops 718402560 | bytes 40955780 | solution.py:201
  660.3 35.5 %psum.14 = bf16[8,2,12,128]{3,2,1,0:T(8,128)(2,1)S(1)} all-reduce(bf16[8,2,12,128]{3,2,1,0:T(8,128)(2,1)S(1)} %get-tuple-element.320), channel_id=1, replica_groups=mesh['blk'=8,'dp'=4] {'blk'}, use_global_device_ids=true, to_apply=%region_19.20 | all-reduce | flops 24576 | bytes 98304 | tf_op jit(solution)/shard_map/psum | solution.py:202
  697.8 287.8 %while.68 = (s32[]{:T(128)}, f32[2,896,12,64]{1,3,2,0:T(8,128)}, f32[2,896,12,64]{1,3,2,0:T(8,128)}, bf16[8,128,2,768]{3,1,0,2:T(8,128)(2,1)}, bf16[8,128,2,768]...) while((s32[]{:T(128)}, f32[2,896,12,64]{1,3,2,0:T(8,128)}, ...), condition=%wide.region_21.22_spmd.clone, body=%wide.region_20.21_spmd.clone.sunk | while | flops 1796407296 | bytes 175513968 | solution.py:234
  1022.9 34.4 %reduce-scatter.32.cloned.1.call-done = bf16[128,2,768]{2,0,1:T(8,128)(2,1)} async-done(((bf16[1024,2,768]{2,0,1:T(8,128)(2,1)}), bf16[128,2,768]{2,0,1:T(8,128)(2,1)}) %reduce-scatter.32.cloned.1.call-update) | async-done | bytes 393232 | tf_op jit(solution)/shard_map/reduce_scatter | solution.py:237
  1127.2 108.2 %all-reduce.3.cloned.1.call-done = bf16[2,768,768]{2,0,1:T(2,128)(2,1)} async-done(((bf16[2,768,768]{2,0,1:T(2,128)(2,1)}), bf16[2,768,768]{2,0,1:T(2,128)(2,1)}) %all-reduce.3.cloned.1.call-update) | async-done | bytes 2359312
  1236.6 29.6 %copy.245 = bf16[2,96,768]{0,1,2:T(8,128)(2,1)} copy(bf16[2,96,768]{2,0,1:T(2,128)(2,1)S(1)} %constant_dynamic-slice_fusion.8) | data formatting | bytes 589824
  1266.2 29.1 %reshape.324 = bf16[768,192]{1,0:T(8,128)(2,1)} reshape(bf16[768,96,2]{2,1,0:T(8,128)(2,1)} %bitcast.331) | data formatting | bytes 589824
  1295.6 38.4 %reduce-scatter.50.cloned.1.call-done = bf16[384,768]{1,0:T(8,128)(2,1)} async-done(((bf16[3072,768]{1,0:T(8,128)(2,1)}), bf16[384,768]{1,0:T(8,128)(2,1)}) %reduce-scatter.50.cloned.1.call-update) | async-done | bytes 589840 | tf_op jit(solution)/shard_map/reduce_scatter | solution.py:329
  1336.3 96.9 %reduce-scatter.46.cloned.1.call-done = bf16[96,3072]{1,0:T(8,128)(2,1)} async-done(((bf16[768,3072]{1,0:T(8,128)(2,1)}), bf16[96,3072]{1,0:T(8,128)(2,1)}) %reduce-scatter.46.cloned.1.call-update) | async-done | bytes 589840 | tf_op jit(solution)/shard_map/reduce_scatter | solution.py:326
  1433.3 67.7 %reduce-scatter.42.cloned.1.call-done = bf16[96,768]{1,0:T(8,128)(2,1)} async-done(((bf16[768,768]{1,0:T(8,128)(2,1)}), bf16[96,768]{1,0:T(8,128)(2,1)}) %reduce-scatter.42.cloned.1.call-update) | async-done | bytes 147472 | tf_op jit(solution)/shard_map/reduce_scatter | solution.py:317
  1511.2 56.5 %reduce-scatter.40.cloned.1.call-done = bf16[96,768]{1,0:T(8,128)(2,1)} async-done(((bf16[768,768]{1,0:T(8,128)(2,1)}), bf16[96,768]{1,0:T(8,128)(2,1)}) %reduce-scatter.40.cloned.1.call-update) | async-done | bytes 147472 | tf_op jit(solution)/shard_map/reduce_scatter | solution.py:314
  1569.5 75.6 %reduce-scatter.36.cloned.1.call-done = bf16[128,2,768]{2,0,1:T(8,128)(2,1)} async-done(((bf16[1024,2,768]{2,0,1:T(8,128)(2,1)}), bf16[128,2,768]{2,0,1:T(8,128)(2,1)}) %reduce-scatter.36.cloned.1.call-update) | async-done | bytes 393232 | tf_op jit(solution)/shard_map/reduce_scatter | solution.py:281
  1647.8 74.8 %reduce-scatter.34.cloned.1.call-done = bf16[128,2,768]{2,0,1:T(8,128)(2,1)} async-done(((bf16[1024,2,768]{2,0,1:T(8,128)(2,1)}), bf16[128,2,768]{2,0,1:T(8,128)(2,1)}) %reduce-scatter.34.cloned.1.call-update) | async-done | bytes 393232 | tf_op jit(solution)/shard_map/reduce_scatter | solution.py:278
  1866.8 78.7 %reduce-scatter.38.cloned.1.call-done = bf16[3,96,768]{2,1,0:T(8,128)(2,1)} async-done(((bf16[3,768,768]{2,1,0:T(8,128)(2,1)}), bf16[3,96,768]{2,1,0:T(8,128)(2,1)}) %reduce-scatter.38.cloned.1.call-update) | async-done | bytes 442384 | tf_op jit(solution)/shard_map/reduce_scatter | solution.py:311
  1954.8 40.5 %psum.15 = f32[3,768]{1,0:T(4,128)} all-reduce(f32[3,768]{1,0:T(4,128)S(1)} %pad_maximum_fusion.2), channel_id=1, replica_groups=mesh['blk'=8,'dp'=4] {'blk','dp'}, use_global_device_ids=true, to_apply=%region_31.32 | all-reduce | flops 2304 | bytes 18432 | tf_op jit(solution)/shard_map/psum | solution.py:301
  (630 shorter events, 874.8 us)
Async XLA Ops:
  7.2 149.0 %copy-start = (bf16[2,896,768]{2,1,0:T(8,128)(2,1)S(1)}, bf16[2,896,768]{2,1,0:T(8,128)(2,1)}, u32[]{:S(2)}) copy-start(bf16[2,896,768]{2,1,0:T(8,128)(2,1)} %param.23) | copy-start | bytes 8257540
  7.2 69.8 %all-gather.15.cloned.1.call-start = ((), (), s32[]{:S(2)}) async-start(), calls=%async_computation.31 | async-start | bytes 3538944 | tf_op jit(solution)/shard_map/all_gather | solution.py:84
  8.1 512.1 %copy-start.42 = (f32[768]{0:T(1024)}, f32[768]{0:T(1024)S(1)}, u32[]{:S(2)}) copy-start(f32[768]{0:T(1024)S(1)} %get-tuple-element.596) | copy-start | bytes 9220
  13.7 125.2 %all-gather.13.cloned.1.call-start = ((), (), s32[]{:S(2)}) async-start(), calls=%async_computation.30 | async-start | bytes 3538944 | tf_op jit(solution)/shard_map/all_gather | solution.py:85
  14.5 200.2 %all-gather.9.cloned.1.call-start = ((), (), s32[]{:S(2)}) async-start(), calls=%async_computation.17 | async-start | bytes 3538944 | tf_op jit(solution)/shard_map/all_gather | solution.py:134
  155.4 350.2 %reduce-scatter.30.cloned.1.call-start = ((), (), s32[]{:S(2)}) async-start(), calls=%async_computation.18 | async-start | bytes 3538944 | tf_op jit(solution)/shard_map/reduce_scatter | solution.py:165
  432.5 150.3 %all-gather.11.cloned.1.call-start = ((), (), s32[]{:S(2)}) async-start(), calls=%async_computation.19 | async-start | bytes 3538944 | tf_op jit(solution)/shard_map/all_gather | solution.py:189
  522.9 534.4 %reduce-scatter.32.cloned.1.call-start = ((), (), s32[]{:S(2)}) async-start(), calls=%async_computation.20 | async-start | bytes 3538944 | tf_op jit(solution)/shard_map/reduce_scatter | solution.py:237
  985.6 138.5 %reduce-scatter.44.cloned.1.call-start = ((), (), s32[]{:S(2)}) async-start(), calls=%async_computation.26 | async-start | bytes 1327104 | tf_op jit(solution)/shard_map/reduce_scatter | solution.py:323
  989.2 246.2 %all-reduce.3.cloned.1.call-start = ((), (), s32[]{:S(2)}) async-start(), calls=%async_computation.38 | async-start | bytes 4718592
  1010.1 324.0 %reduce-scatter.50.cloned.1.call-start = ((), (), s32[]{:S(2)}) async-start(), calls=%async_computation.29 | async-start | bytes 5308416 | tf_op jit(solution)/shard_map/reduce_scatter | solution.py:329
  1016.5 416.7 %reduce-scatter.46.cloned.1.call-start = ((), (), s32[]{:S(2)}) async-start(), calls=%async_computation.27 | async-start | bytes 5308416 | tf_op jit(solution)/shard_map/reduce_scatter | solution.py:326
  1022.8 478.1 %reduce-scatter.42.cloned.1.call-start = ((), (), s32[]{:S(2)}) async-start(), calls=%async_computation.25 | async-start | bytes 1327104 | tf_op jit(solution)/shard_map/reduce_scatter | solution.py:317
  1060.0 507.8 %reduce-scatter.40.cloned.1.call-start = ((), (), s32[]{:S(2)}) async-start(), calls=%async_computation.24 | async-start | bytes 1327104 | tf_op jit(solution)/shard_map/reduce_scatter | solution.py:314
  1064.9 580.3 %reduce-scatter.36.cloned.1.call-start = ((), (), s32[]{:S(2)}) async-start(), calls=%async_computation.22 | async-start | bytes 3538944 | tf_op jit(solution)/shard_map/reduce_scatter | solution.py:281
  1083.5 639.1 %reduce-scatter.34.cloned.1.call-start = ((), (), s32[]{:S(2)}) async-start(), calls=%async_computation.21 | async-start | bytes 3538944 | tf_op jit(solution)/shard_map/reduce_scatter | solution.py:278
  1107.3 637.3 %reduce-scatter.60.cloned.1.call-start = ((), (), s32[]{:S(2)}) async-start(), calls=%async_computation.36 | async-start | bytes 245760
  1125.9 642.1 %reduce-scatter.58.cloned.1.call-start = ((), (), s32[]{:S(2)}) async-start(), calls=%async_computation.35 | async-start | bytes 491520
  1295.4 497.2 %reduce-scatter.62.cloned.1.call-start = ((), (), s32[]{:S(2)}) async-start(), calls=%async_computation.37 | async-start | bytes 737280
  1336.2 481.0 %reduce-scatter.48.cloned.1.call-start = ((), (), s32[]{:S(2)}) async-start(), calls=%async_computation.28 | async-start | bytes 737280 | tf_op jit(solution)/shard_map/reduce_scatter | solution.py:349
  1433.2 406.4 %reduce-scatter.56.cloned.1.call-start = ((), (), s32[]{:S(2)}) async-start(), calls=%async_computation.34 | async-start | bytes 245760
  1502.7 359.7 %reduce-scatter.54.cloned.1.call-start = ((), (), s32[]{:S(2)}) async-start(), calls=%async_computation.33 | async-start | bytes 245760
  1569.5 376.1 %reduce-scatter.38.cloned.1.call-start = ((), (), s32[]{:S(2)}) async-start(), calls=%async_computation.23 | async-start | bytes 3981312 | tf_op jit(solution)/shard_map/reduce_scatter | solution.py:311
  1727.5 267.8 %reduce-scatter.52.cloned.1.call-start = ((), (), s32[]{:S(2)}) async-start(), calls=%async_computation.32 | async-start | bytes 737280
  (131 other events, 1609.4 us)
Sparse Core Ops, SparseCore 0:
  13.8 63.1 all-gather.14
  79.8 59.0 all-gather.12
  155.5 59.0 all-gather.8
  432.6 72.9 reduce-scatter.29
  523.0 59.7 all-gather.10
  985.7 71.5 reduce-scatter.31
  1060.7 63.3 reduce-scatter.43
  1127.7 107.6 all-reduce.2
  1239.5 94.4 reduce-scatter.49
  1338.0 95.1 reduce-scatter.45
  1437.0 63.9 reduce-scatter.41
  1504.5 63.1 reduce-scatter.39
  1571.7 73.3 reduce-scatter.35
  1649.0 73.5 reduce-scatter.33
  1725.6 18.9 reduce-scatter.59
  1747.1 20.8 reduce-scatter.57
  1770.5 22.0 reduce-scatter.61
  1795.1 22.0 reduce-scatter.47
  1819.8 19.6 reduce-scatter.55
  1842.6 19.7 reduce-scatter.53
  1866.4 79.0 reduce-scatter.37
  1950.6 21.7 reduce-scatter.51
where the time goes:
time: 2020 us; the launch traced here: 2000 us
  waiting for transfers between devices  1030 us (51%)
  matrix products  502 us (25%)
  local copies, waits for them, and re-layouts  264 us (13%)
  blocking collectives  138 us (7%)
  other arithmetic  53.3 us (3%)
    unnamed x29, waiting for transfers between devices  175 us
    unnamed x145, local copies, waits for them, and re-layouts  116 us
    reduce_scatter x1, waiting for transfers between devices, body(): lax.psum_scatter(ffn_in_grad.astype(jnp.bfloat16), 'blk', scatter_dimensi...  96.9 us
    dot_general x8, matrix products, cross_back(): jnp.einsum('shtx,tshe->sxhe', prob.astype(jnp.bfloat16), split_grad, pref...  88.1 us
    dot_general x24, matrix products, cross_raw(): jnp.einsum('tshe,sxhe->shtx', split_block, split_keys, preferred_element_...  85.4 us
    reduce_scatter x1, waiting for transfers between devices, body(): lax.psum_scatter(self_qkv_grad.astype(jnp.bfloat16), 'blk', scatter_dimen...  78.7 us
    reduce_scatter x1, waiting for transfers between devices, body(): lax.psum_scatter(value_term.astype(jnp.bfloat16), 'blk', scatter_dimensio...  75.6 us
    reduce_scatter x1, waiting for transfers between devices, body(): lax.psum_scatter(key_term.astype(jnp.bfloat16), 'blk', scatter_dimension=...  74.8 us
  transfers between devices with their start and end apart: 22, of which 21 were waited for; matrix products, arithmetic and copies ran while one was open for 12% of the time, Pallas kernels for 0%

commit v1 on v0

v1 whole, which is shorter than its diff:
```python
import functools

import jax
import jax.numpy as jnp
from jax import lax
from jax.experimental import pallas as pl
from jax.experimental.pallas import tpu as pltpu
from jax.sharding import PartitionSpec as P

HEAD_DIM = 64
SLOTS = 448
F32 = jnp.float32
BF16 = jnp.bfloat16
epsilon = 1e-06
negative_fill = -1e30
safe_score = 60.0
VMEM_LIMIT = 60 * 1024 * 1024


def dot(left, right, left_dim, right_dim):
    return lax.dot_general(
        left, right, (((left_dim,), (right_dim,)), ((), ())), preferred_element_type=F32
    )


def split_low(value):
    high = value.astype(BF16)
    return high, (value - high.astype(F32)).astype(BF16)


def split_sent(value):
    high = lax.reduce_precision(value, 8, 7)
    return high.astype(BF16), (value - high).astype(BF16)


def normed(values, gain):
    return values * lax.rsqrt(jnp.mean(values * values, axis=-1, keepdims=True) + epsilon) * gain


def norm_pull(values, gain, grad):
    unused, pull = jax.vjp(normed, values, gain)
    return pull(grad)


def params():
    return pltpu.CompilerParams(vmem_limit_bytes=VMEM_LIMIT)


def cross_forward(query, keys, values, bias, width, groups):
    heads = width // HEAD_DIM
    length = query.shape[1]
    tokens = length // groups
    parts = len(keys)
    rows = [k.shape[1] for k in keys]
    starts = [sum(rows[:i]) for i in range(parts)]
    total = sum(rows)
    stat_rows = 16 * ((heads + 15) // 16)

    def kernel(*refs):
        q_ref = refs[0]
        k_refs = refs[1 : 1 + parts]
        v_refs = refs[1 + parts : 1 + 2 * parts]
        b_refs = refs[1 + 2 * parts : 1 + 3 * parts]
        o_ref, p_ref, m_ref, lse_ref = refs[1 + 3 * parts :]
        head = pl.program_id(0)
        query = q_ref[...]
        aug_query = jnp.concatenate([query, jnp.ones((16, length), BF16)], axis=0)
        q_norm = jnp.max(jnp.sum(jnp.square(query.astype(F32)), axis=0, keepdims=True))
        k_norm = jnp.float32(0)
        for k_ref in k_refs:
            k_norm = jnp.maximum(
                k_norm, jnp.max(jnp.sum(jnp.square(k_ref[...].astype(F32)), axis=0, keepdims=True))
            )
        small = q_norm * k_norm < safe_score * safe_score

        def score(i):
            return dot(jnp.concatenate([k_refs[i][...], b_refs[i][...]], axis=0), aug_query, 0, 0)

        def finish(probs, top):
            mixed = None
            for i in range(parts):
                aug_value = jnp.concatenate([v_refs[i][...], jnp.ones((16, rows[i]), BF16)], axis=0)
                term = dot(aug_value, probs[i], 1, 0)
                mixed = term if mixed is None else mixed + term
            norm = mixed[HEAD_DIM : HEAD_DIM + 1]
            out = (mixed[:HEAD_DIM] / norm).astype(BF16)
            where = pl.ds(pl.multiple_of(head * HEAD_DIM, HEAD_DIM), HEAD_DIM)
            for g in range(groups):
                o_ref[g, where, :] = out[:, g * tokens : (g + 1) * tokens]
            lse_ref[pl.ds(head, 1), :] = top + jnp.log(norm)
            m_ref[0] = top

        @pl.when(small)
        def plain():
            probs = []
            for i in range(parts):
                prob = jnp.exp(score(i)).astype(BF16)
                p_ref[0, starts[i] : starts[i] + rows[i], :] = prob
                probs.append(prob)
            finish(probs, jnp.zeros((1, length), F32))

        @pl.when(jnp.logical_not(small))
        def shifted():
            raw = [score(i) for i in range(parts)]
            top = jnp.max(raw[0], axis=0, keepdims=True)
            for i in range(1, parts):
                top = jnp.maximum(top, jnp.max(raw[i], axis=0, keepdims=True))
            probs = []
            for i in range(parts):
                prob = jnp.exp(raw[i] - top).astype(BF16)
                p_ref[0, starts[i] : starts[i] + rows[i], :] = prob
                probs.append(prob)
            finish(probs, top)

        @pl.when(head == heads - 1)
        def stats():
            high, low = split_low(lse_ref[...])
            for g in range(groups):
                o_ref[g, width : width + stat_rows, :] = high[:, g * tokens : (g + 1) * tokens]
                o_ref[g, width + stat_rows :, :] = low[:, g * tokens : (g + 1) * tokens]

    payload = width + 2 * stat_rows
    kv_specs = [pl.BlockSpec((HEAD_DIM, r), lambda h: (h, 0)) for r in rows]
    return pl.pallas_call(
        kernel,
        grid=(heads,),
        in_specs=[pl.BlockSpec((HEAD_DIM, length), lambda h: (h, 0))]
        + kv_specs
        + kv_specs
        + [pl.BlockSpec((16, r), lambda h: (0, 0)) for r in rows],
        out_specs=[
            pl.BlockSpec((groups, payload, tokens), lambda h: (0, 0, 0)),
            pl.BlockSpec((1, total, length), lambda h: (h, 0, 0)),
            pl.BlockSpec((1, 1, length), lambda h: (h, 0, 0)),
        ],
        out_shape=[
            jax.ShapeDtypeStruct((groups, payload, tokens), BF16),
            jax.ShapeDtypeStruct((heads, total, length), BF16),
            jax.ShapeDtypeStruct((heads, 1, length), F32),
        ],
        scratch_shapes=[pltpu.VMEM((stat_rows, length), F32)],
        compiler_params=params(),
        cost_estimate=pl.CostEstimate(
            flops=16 * heads * total * length * HEAD_DIM,
            bytes_accessed=2 * heads * total * length,
            transcendentals=heads * total * length,
        ),
        name="cross_forward",
    )(query, *keys, *values, *bias)


def cross_backward(query, keys, values, prob, grads, weight, delta, width, groups):
    heads = width // HEAD_DIM
    length = query.shape[1]
    tokens = length // groups
    parts = len(keys)
    rows = [k.shape[1] for k in keys]
    starts = [sum(rows[:i]) for i in range(parts)]
    total = sum(rows)
    pair = 2

    def kernel(*refs):
        q_ref = refs[0]
        k_refs = refs[1 : 1 + parts]
        v_refs = refs[1 + parts : 1 + 2 * parts]
        p_ref, g_ref, w_ref, d_ref = refs[1 + 2 * parts : 5 + 2 * parts]
        dq_ref = refs[5 + 2 * parts]
        dk_refs = refs[6 + 2 * parts : 6 + 3 * parts]
        dv_refs = refs[6 + 3 * parts :]
        key_out = [[] for _ in range(parts)]
        value_out = [[] for _ in range(parts)]
        for j in range(pair):
            at = slice(j * HEAD_DIM, (j + 1) * HEAD_DIM)
            grad = jnp.concatenate([g_ref[g, at, :] for g in range(groups)], axis=1).astype(F32)
            scaled = grad * w_ref[j]
            high, low = split_low(-d_ref[j])
            scaled_low = scaled.astype(BF16)
            pad = jnp.zeros((14, length), BF16)
            aug = jnp.concatenate([scaled_low, high, low, pad], axis=0)
            scaled_rows = scaled.T.astype(BF16)
            query_rows = q_ref[at, :].astype(F32).T.astype(BF16)
            query_grad = None
            for i in range(parts):
                aug_value = jnp.concatenate(
                    [v_refs[i][at, :], jnp.ones((16, rows[i]), BF16)], axis=0
                )
                prob = p_ref[j, starts[i] : starts[i] + rows[i], :]
                score = (prob.astype(F32) * dot(aug_value, aug, 0, 0)).astype(BF16)
                value_out[i].append(dot(prob, scaled_rows, 1, 0).astype(BF16))
                key_out[i].append(dot(score, query_rows, 1, 0).astype(BF16))
                term = dot(k_refs[i][at, :], score, 1, 0)
                query_grad = term if query_grad is None else query_grad + term
            query_low = (query_grad * 0.125).astype(BF16)
            for g in range(groups):
                dq_ref[g, at, :] = query_low[:, g * tokens : (g + 1) * tokens]
        for i in range(parts):
            dk_refs[i][...] = jnp.concatenate(key_out[i], axis=1)
            dv_refs[i][...] = jnp.concatenate(value_out[i], axis=1)

    size = pair * HEAD_DIM
    kv_specs = [pl.BlockSpec((size, r), lambda h: (h, 0)) for r in rows]
    kv_grads = [pl.BlockSpec((r, size), lambda h: (0, h)) for r in rows]
    outs = pl.pallas_call(
        kernel,
        grid=(heads // pair,),
        in_specs=[pl.BlockSpec((size, length), lambda h: (h, 0))]
        + kv_specs
        + kv_specs
        + [
            pl.BlockSpec((pair, total, length), lambda h: (h, 0, 0)),
            pl.BlockSpec((groups, size, tokens), lambda h: (0, h, 0)),
            pl.BlockSpec((pair, 1, length), lambda h: (h, 0, 0)),
            pl.BlockSpec((pair, 1, length), lambda h: (h, 0, 0)),
        ],
        out_specs=[pl.BlockSpec((groups, size, tokens), lambda h: (0, h, 0))] + kv_grads + kv_grads,
        out_shape=[jax.ShapeDtypeStruct((groups, width, tokens), BF16)]
        + [jax.ShapeDtypeStruct((r, width), BF16) for r in rows] * 2,
        compiler_params=params(),
        cost_estimate=pl.CostEstimate(
            flops=32 * heads * total * length * HEAD_DIM,
            bytes_accessed=2 * heads * total * length,
            transcendentals=0,
        ),
        name="cross_backward",
    )(query, *keys, *values, prob, grads, weight, delta)
    return outs[0], list(outs[1 : 1 + parts]), list(outs[1 + parts :])


def self_forward(projected, key_pos, query_pos):
    own, length = projected.shape[1:]
    heads = own // HEAD_DIM

    def kernel(q_ref, k_ref, v_ref, kp_ref, qp_ref, o_ref, p_ref, w_ref):
        raw = dot(k_ref[0], q_ref[0], 0, 0) * 0.125
        raw = jnp.where(kp_ref[...] <= qp_ref[...], raw, negative_fill)
        top = jnp.max(raw, axis=0, keepdims=True)
        prob = jnp.exp(raw - top).astype(BF16)
        p_ref[0] = prob
        aug_value = jnp.concatenate([v_ref[0], jnp.ones((16, length), BF16)], axis=0)
        mixed = dot(aug_value, prob, 1, 0)
        inverse = 1.0 / mixed[HEAD_DIM : HEAD_DIM + 1]
        o_ref[...] = (mixed[:HEAD_DIM] * inverse).astype(BF16)
        w_ref[0] = inverse

    spec = lambda c: pl.BlockSpec((1, HEAD_DIM, length), lambda h: (c, h, 0))
    return pl.pallas_call(
        kernel,
        grid=(heads,),
        in_specs=[
            spec(0),
            spec(1),
            spec(2),
            pl.BlockSpec((length, 1), lambda h: (0, 0)),
            pl.BlockSpec((1, length), lambda h: (0, 0)),
        ],
        out_specs=[
            pl.BlockSpec((HEAD_DIM, length), lambda h: (h, 0)),
            pl.BlockSpec((1, length, length), lambda h: (h, 0, 0)),
            pl.BlockSpec((1, 1, length), lambda h: (h, 0, 0)),
        ],
        out_shape=[
            jax.ShapeDtypeStruct((own, length), BF16),
            jax.ShapeDtypeStruct((heads, length, length), BF16),
            jax.ShapeDtypeStruct((heads, 1, length), F32),
        ],
        compiler_params=params(),
        cost_estimate=pl.CostEstimate(
            flops=16 * heads * length * length * HEAD_DIM,
            bytes_accessed=2 * heads * length * length,
            transcendentals=heads * length * length,
        ),
        name="self_forward",
    )(projected, projected, projected, key_pos, query_pos)


def self_backward(projected, mixed, grads, prob, weight, groups):
    own, length = projected.shape[1:]
    heads = own // HEAD_DIM
    tokens = length // groups

    def kernel(q_ref, k_ref, v_ref, o_ref, g_ref, p_ref, w_ref, out_ref):
        grad = jnp.concatenate([g_ref[g] for g in range(groups)], axis=1).astype(F32)
        scaled = grad * w_ref[0]
        high, low = split_low(-jnp.sum(scaled * o_ref[...].astype(F32), axis=0, keepdims=True))
        scaled_low = scaled.astype(BF16)
        aug = jnp.concatenate([scaled_low, high, low, jnp.zeros((14, length), BF16)], axis=0)
        aug_value = jnp.concatenate([v_ref[0], jnp.ones((16, length), BF16)], axis=0)
        prob = p_ref[0]
        score = (prob.astype(F32) * dot(aug_value, aug, 0, 0)).astype(BF16)
        results = (
            dot(k_ref[0], score, 1, 0) * 0.125,
            dot(q_ref[0], score, 1, 1) * 0.125,
            dot(scaled_low, prob, 1, 1),
        )
        for c in range(3):
            result = results[c].astype(BF16)
            for g in range(groups):
                out_ref[g, c] = result[:, g * tokens : (g + 1) * tokens]

    spec = lambda c: pl.BlockSpec((1, HEAD_DIM, length), lambda h: (c, h, 0))
    return pl.pallas_call(
        kernel,
        grid=(heads,),
        in_specs=[
            spec(0),
            spec(1),
            spec(2),
            pl.BlockSpec((HEAD_DIM, length), lambda h: (h, 0)),
            pl.BlockSpec((groups, HEAD_DIM, tokens), lambda h: (0, h, 0)),
            pl.BlockSpec((1, length, length), lambda h: (h, 0, 0)),
            pl.BlockSpec((1, 1, length), lambda h: (h, 0, 0)),
        ],
        out_specs=pl.BlockSpec((groups, 3, HEAD_DIM, tokens), lambda h: (0, 0, h, 0)),
        out_shape=jax.ShapeDtypeStruct((groups, 3, own, tokens), BF16),
        compiler_params=params(),
        cost_estimate=pl.CostEstimate(
            flops=32 * heads * length * length * HEAD_DIM,
            bytes_accessed=2 * heads * length * length,
            transcendentals=0,
        ),
        name="self_backward",
    )(projected, projected, projected, mixed, grads, prob, weight)


def body(
    dec_input,
    enc_output,
    lengths,
    gains,
    self_qkv,
    self_out,
    cross_q,
    cross_kv,
    cross_out,
    ffn_in,
    ffn_out,
    cotangent,
):
    seg, seqs, width = dec_input.shape
    heads = width // HEAD_DIM
    blocks = lax.axis_size("blk")
    place = lax.axis_index("blk")
    groups = blocks // seqs
    mine = place // groups
    slot_of = lax.rem(place, groups)
    members = [[s * groups + g for g in range(groups)] for s in range(seqs)]
    own_heads = -(-heads // groups)
    own = own_heads * HEAD_DIM
    padded = own * groups
    tokens = seqs * seg
    length = groups * tokens
    enc_rows = enc_output.shape[1]
    gain_values = gains.astype(F32)

    def shifted(step):
        return [(b, (b + step * groups) % blocks) for b in range(blocks)]

    def exchange(pieces):
        parts = [pieces(mine)]
        for step in range(1, seqs):
            parts.append(lax.ppermute(pieces(lax.rem(mine + step, seqs)), "blk", shifted(step)))
        return parts

    def in_order(parts):
        ordered = []
        for s in range(seqs):
            choice = parts[0]
            for step in range(1, seqs):
                from_there = lax.rem(mine - step + seqs, seqs) == s
                choice = jnp.where(from_there, parts[step], choice)
            ordered.append(choice)
        return ordered

    def spread(array):
        return lax.all_to_all(
            jnp.broadcast_to(array[None], (groups,) + array.shape),
            "blk",
            0,
            0,
            axis_index_groups=members,
        )

    def traded(array):
        return lax.all_to_all(array, "blk", 0, 0, axis_index_groups=members)

    def gathered(array):
        take = lambda s: lax.dynamic_index_in_dim(array, s, 1, False)
        return jnp.concatenate(in_order(exchange(take)), axis=0)

    def returned(array):
        split = array.reshape(seqs, seg, width)
        take = lambda s: lax.dynamic_index_in_dim(split, s, 0, False)
        return jnp.stack(in_order(exchange(take)), axis=1)

    own_inputs = gathered(dec_input)
    all_inputs = spread(own_inputs).reshape(length, width).astype(F32)
    encoded = exchange(lambda s: lax.dynamic_index_in_dim(enc_output, s, 0, False))
    own_cotangent = gathered(cotangent)

    row_lengths = lax.dynamic_index_in_dim(lengths, mine, 0, False)
    bias = []
    for step in range(seqs):
        source = lax.rem(place - step * groups + blocks, blocks)
        slot = source * enc_rows + jnp.arange(enc_rows)
        match = (slot // SLOTS)[:, None] == jnp.arange(lengths.shape[1])[None, :]
        filled = jnp.sum(jnp.where(match, row_lengths[None, :], 0), axis=-1)
        row = jnp.where((slot % SLOTS) < filled, 0.0, negative_fill).astype(BF16)
        bias.append(jnp.concatenate([row[None], jnp.zeros((15, enc_rows), BF16)], axis=0))
    cross_keys = [dot(cross_kv[0], e, 0, 1).astype(BF16) for e in encoded]
    cross_values = [dot(cross_kv[1], e, 0, 1).astype(BF16) for e in encoded]

    first_low = normed(all_inputs, gain_values[0]).astype(BF16)
    extra = [(0, 0), (0, 0), (0, padded - width)]
    own_qkv = lax.dynamic_slice_in_dim(jnp.pad(self_qkv, extra), slot_of * own, own, 2)
    projected = jnp.stack([dot(own_qkv[c], first_low, 0, 1).astype(BF16) for c in range(3)])
    index = jnp.arange(length)
    block = index // seg
    position = ((block % seqs) * groups + block // seqs) * seg + index % seg
    position = position.astype(jnp.int32)
    own_mix, self_prob, self_weight = self_forward(projected, position[:, None], position[None, :])
    self_mix = spread(own_mix).reshape(padded, length)[:width]
    after_self_all = all_inputs + dot(self_mix, self_out, 0, 0)
    second_low_all = normed(after_self_all, gain_values[1]).astype(BF16)
    cross_query = dot(cross_q, second_low_all, 0, 1).astype(BF16) * jnp.asarray(0.125, BF16)

    def own_rows(array):
        return lax.dynamic_slice_in_dim(array, slot_of * tokens, tokens, 0)

    after_self = own_rows(after_self_all)
    second_low = own_rows(second_low_all)
    own_self_mix = lax.dynamic_slice_in_dim(self_mix, slot_of * tokens, tokens, 1)

    part_mix, cross_prob, local_top = cross_forward(
        cross_query, cross_keys, cross_values, bias, width, groups
    )
    stat_rows = (part_mix.shape[1] - width) // 2
    parts = traded(part_mix).astype(F32)
    part_lse = (parts[:, width : width + stat_rows] + parts[:, width + stat_rows :])[:, :heads]
    top = jnp.max(part_lse, axis=0)
    part_weight = jnp.exp(part_lse - top[None])
    weight_sum = jnp.sum(part_weight, axis=0)
    cross_lse = top + jnp.log(weight_sum)
    part_weight = part_weight / weight_sum[None]
    cross_mix = (
        jnp.sum(
            parts[:, :width].reshape(groups, heads, HEAD_DIM, tokens) * part_weight[:, :, None],
            axis=0,
        )
        .reshape(width, tokens)
        .astype(BF16)
    )

    after_cross = after_self + dot(cross_mix, cross_out, 0, 0)
    third_low = normed(after_cross, gain_values[2]).astype(BF16)
    hidden_pre = dot(third_low, ffn_in, 1, 0)
    hidden_low = jax.nn.gelu(hidden_pre).astype(BF16)
    output = returned((after_cross + dot(hidden_low, ffn_out, 1, 0)).astype(BF16))
    upstream = own_cotangent.astype(F32)
    hidden_grad = dot(own_cotangent, ffn_out, 1, 1)
    unused, gelu_pull = jax.vjp(jax.nn.gelu, hidden_pre)
    pre_low = gelu_pull(hidden_grad)[0].astype(BF16)
    step_grad, gain_three = norm_pull(after_cross, gain_values[2], dot(pre_low, ffn_in, 1, 1))
    cross_grad = upstream + step_grad
    cross_grad_low = cross_grad.astype(BF16)
    mix_grad = dot(cross_out, cross_grad_low, 1, 1).astype(BF16)
    row_term = jnp.sum(
        (mix_grad.astype(F32) * cross_mix.astype(F32)).reshape(heads, HEAD_DIM, tokens), axis=1
    )
    stats = jnp.concatenate([*split_sent(cross_lse), *split_sent(row_term)], axis=0)
    fill = jnp.zeros((-stats.shape[0] % 16, tokens), BF16)
    packed = spread(jnp.concatenate([mix_grad, stats, fill], axis=0))

    def whole_rows(start):
        rows = packed[:, start : start + 2 * heads].astype(F32)
        rows = rows[:, :heads] + rows[:, heads:]
        return rows.transpose(1, 0, 2).reshape(heads, 1, length)

    scale = jnp.exp(local_top - whole_rows(width))
    query_parts, key_low, value_low = cross_backward(
        cross_query,
        cross_keys,
        cross_values,
        cross_prob,
        packed,
        scale,
        whole_rows(width + 2 * heads) * scale,
        width,
        groups,
    )
    query_grad = jnp.sum(traded(query_parts).astype(F32), axis=0).astype(BF16)

    ffn_out_grad = dot(hidden_low, own_cotangent, 0, 0)
    ffn_in_grad = dot(third_low, pre_low, 0, 0)
    cross_out_grad = dot(cross_mix, cross_grad_low, 1, 0)
    cross_q_grad = dot(second_low, query_grad, 0, 1)
    key_weight_grad = sum(dot(e, g, 0, 0) for e, g in zip(encoded, key_low))
    value_weight_grad = sum(dot(e, g, 0, 0) for e, g in zip(encoded, value_low))
    enc_parts = [
        (dot(k, cross_kv[0], 1, 1) + dot(v, cross_kv[1], 1, 1)).astype(BF16)
        for k, v in zip(key_low, value_low)
    ]
    enc_back = [enc_parts[0]]
    for step in range(1, seqs):
        enc_back.append(
            lax.ppermute(enc_parts[step], "blk", [(b, a) for a, b in shifted(step)])
        )
    enc_grad = []
    for s in range(seqs):
        choice = enc_back[0]
        for step in range(1, seqs):
            choice = jnp.where(lax.rem(mine + step, seqs) == s, enc_back[step], choice)
        enc_grad.append(choice)
    enc_grad = jnp.stack(enc_grad, axis=0)

    step_grad, gain_two = norm_pull(after_self, gain_values[1], dot(query_grad, cross_q, 0, 1))
    self_grad = cross_grad + step_grad
    self_grad_low = self_grad.astype(BF16)
    self_out_grad = dot(own_self_mix, self_grad_low, 1, 0)
    mixed_grad = dot(self_out, self_grad_low, 1, 1).astype(BF16)
    mixed_grad = jnp.pad(mixed_grad, [(0, padded - width), (0, 0)])
    grads = traded(mixed_grad.reshape(groups, own, tokens))
    own_grads = self_backward(projected, own_mix, grads, self_prob, self_weight, groups)
    back = traded(own_grads)
    back = back.transpose(1, 0, 2, 3).reshape(3, padded, tokens)[:, :width]
    own_first = own_rows(first_low)
    self_qkv_grad = jnp.stack([dot(own_first, back[c], 0, 1) for c in range(3)])
    first_back = sum(dot(back[c], self_qkv[c], 0, 1) for c in range(3))
    step_grad, gain_one = norm_pull(own_rows(all_inputs), gain_values[0], first_back)
    dec_grad = returned((self_grad + step_grad).astype(BF16))

    gain_grads = lax.psum(jnp.stack([gain_one, gain_two, gain_three]), ("blk", "dp"))

    def scattered(grad, axis):
        grad = lax.psum_scatter(grad.astype(BF16), "blk", scatter_dimension=axis, tiled=True)
        return lax.psum_scatter(grad, "dp", scatter_dimension=axis + 1, tiled=True).astype(F32)

    return (
        output,
        dec_grad,
        enc_grad,
        gain_grads,
        scattered(self_qkv_grad, 1),
        scattered(self_out_grad, 0),
        scattered(cross_q_grad, 0),
        scattered(jnp.stack([key_weight_grad, value_weight_grad]), 1),
        scattered(cross_out_grad, 0),
        scattered(ffn_in_grad, 0),
        scattered(ffn_out_grad, 0),
    )


def solution(mesh):
    placed = (
        P("blk", "dp", None),
        P("dp", "blk", None),
        P("dp", None),
        P(),
        P(),
        P(),
        P(),
        P(),
        P(),
        P(),
        P(),
        P("blk", "dp", None),
    )
    return jax.shard_map(
        body,
        mesh=mesh,
        in_specs=placed,
        out_specs=(
            P("blk", "dp", None),
            P("blk", "dp", None),
            P("dp", "blk", None),
            P(),
            P(None, "blk", "dp"),
            P("blk", "dp"),
            P("blk", "dp"),
            P(None, "blk", "dp"),
            P("blk", "dp"),
            P("blk", "dp"),
            P("blk", "dp"),
        ),
        check_vma=False,
    )
```

time: 2020 us -> 1090 us (0.54)
  matrix products: 502 us -> 98.5 us
  waiting for transfers between devices: 1030 us -> 655 us
  local copies, waits for them, and re-layouts: 264 us -> 64.1 us
  Pallas kernels: 0 us -> 95 us
  blocking collectives: 138 us -> 75.3 us
  starting transfers between devices: 2.34 us -> 35.9 us
    dot_general x105 -> x36, matrix products: 502 us -> 98.5 us  [dot(): lax.dot_general(left, right, (((left_dim,), (right_dim,)), ((), ())), pre...]
    all_gather x4 -> x0, waiting for transfers between devices: 218 us -> none  [the longest x1 61.1 us: body(): lax.all_gather(self_key, 'blk', axis=0, tiled=True)]
    reduce_scatter x11 -> x8, waiting for transfers between devices: 634 us -> 493 us  [the longest x7 470 us: scattered(): lax.psum_scatter(grad.astype(BF16), 'blk', scatter_dimension=axis, tiled=...]
    unnamed x29 -> x20, waiting for transfers between devices: 175 us -> 60.7 us
    pallas_call x0 -> x4, Pallas kernels: none -> 95 us  [the longest x1 47.7 us: cross_backward(): pl.pallas_call(kernel, grid=(heads // pair,), in_specs=[pl.BlockSpec((siz...]
    unnamed x145 -> x98, local copies, waits for them, and re-layouts: 116 us -> 31 us
    all_to_all x0 -> x5, waiting for transfers between devices: none -> 63.7 us  [the longest x3 33.5 us: traded(): return lax.all_to_all(array, 'blk', 0, 0, axis_index_groups=members)]
    all_gather x2 -> x0, blocking collectives: 62.1 us -> none  [merged(): lax.all_gather(a.astype(kind), axis)]
  transfers between devices with their start and end apart: 22 -> 25, of which waited for: 21 -> 18; matrix products, arithmetic and copies ran while one was open for 12% -> 13% of each run, Pallas kernels for 0% -> 2%
where the time goes in v1:
time: 1090 us; the launch traced here: 1080 us
  waiting for transfers between devices  655 us (60%)
  matrix products  98.5 us (9%)
  Pallas kernels  95 us (9%)
  blocking collectives  75.3 us (7%)
  local copies, waits for them, and re-layouts  64.1 us (6%)
  other arithmetic  40.1 us (4%)
  starting transfers between devices  35.9 us (3%)
  between operations  15.3 us (1%)
    reduce_scatter x7, waiting for transfers between devices, scattered(): lax.psum_scatter(grad.astype(BF16), 'blk', scatter_dimension=axis, tiled=...  470 us
    dot_general x36, matrix products, dot(): lax.dot_general(left, right, (((left_dim,), (right_dim,)), ((), ())), pre...  98.5 us
    unnamed x20, waiting for transfers between devices  60.7 us
    pallas_call x1, Pallas kernels, cross_backward(): pl.pallas_call(kernel, grid=(heads // pair,), in_specs=[pl.BlockSpec((siz...  47.7 us
    psum x1, blocking collectives, body(): lax.psum(jnp.stack([gain_one, gain_two, gain_three]), ('blk', 'dp'))  39.4 us
    ppermute x5, waiting for transfers between devices, exchange(): lax.ppermute(pieces(lax.rem(mine + step, seqs)), 'blk', shifted(step))  38.3 us
    all_to_all x3, waiting for transfers between devices, traded(): return lax.all_to_all(array, 'blk', 0, 0, axis_index_groups=members)  33.5 us
    unnamed x98, local copies, waits for them, and re-layouts  31 us
  transfers between devices with their start and end apart: 25, of which 18 were waited for; matrix products, arithmetic and copies ran while one was open for 13% of the time, Pallas kernels for 2%

profile of v1, /device:TPU:0, one launch (start us, length us, event | category | flops | bytes accessed | tf_op | source)
XLA Modules:
  0.0 1079.6 jit_solution(2881486094168552657)
XLA Ops:
  15.8 9.4 collective-permute-done
  38.4 30.2 %all-to-all-done = bf16[4,256,768]{2,1,0:T(8,128)(2,1)} async-done(((bf16[4,256,768]{2,1,0:T(8,128)(2,1)}), bf16[4,256,768]{2,1,0:T(8,128)(2,1)}, u32[]{:S(2)}, u32[]{:S(2)}) %all-to-all-start) | async-done | bytes 1572896 | tf_op jit(solution)/shard_map/all_to_all | solution.py:375
  80.1 8.7 self_forward.1
  124.6 28.8 %cross_forward.1 = (bf16[4,800,256]{2,1,0:T(8,128)(2,1)}, bf16[12,1792,1024]{2,1,0:T(8,128)(2,1)}, f32[12,1,1024]{2,1,0:T(1,128)}) custom-call(bf16[768,1024]{1,0:T(8,128)(2,1)} %multiply_bitcast_fusion.refs_0_, bf16[768,896]{1,0:T(8,128)(2,1)} %fusion.8.refs_1_, bf16[768,896]{1,0:T(8,128)(2,1)} %fusion.9.refs_2_, bf16[768,896]{1,0:T(8,128)(2,1)} %fusion.10.refs_3_, ...), custom_call_target="tpu_custom_call" | custom-call | flops 22548578304 | bytes 44040192 | tf_op jit(solution)/shard_map/cross_forward/pallas_call | solution.py:124
  158.8 19.9 %collective-permute-done.3 = bf16[128,768]{1,0:T(8,128)(2,1)S(1)} collective-permute-done((bf16[128,768]{1,0:T(8,128)(2,1)}, bf16[128,768]{1,0:T(8,128)(2,1)S(1)}, u32[]{:S(2)}, u32[]{:S(2)}) %collective-permute-start.3) | collective-permute-done | bytes 196640 | tf_op jit(solution)/shard_map/ppermute | solution.py:361
  215.7 25.4 %all_to_all.35.refs_6_ = bf16[4,816,256]{2,1,0:T(8,128)(2,1)S(1)} all-to-all(bf16[4,816,256]{2,1,0:T(8,128)(2,1)S(1)} %broadcast_in_dim.82), channel_id=1, replica_groups={{0,4,8,12},{16,20,24,28},{1,5,9,13},{17,21,25,29},{2,6,10,14},{18,22,26..., dimensions={0} | all-to-all | bytes 3342336 | tf_op jit(solution)/shard_map/all_to_all | solution.py:375
  249.7 47.7 %cross_backward.1 = (bf16[4,768,256]{2,1,0:T(8,128)(2,1)}, bf16[896,768]{1,0:T(8,128)(2,1)}, bf16[896,768]{1,0:T(8,128)(2,1)}, bf16[896,768]{1,0:T(8,128)(2,1)}, bf16[896,768]{1,0:T(8,128)(2,1)}) custom-call(bf16[768,1024]{1,0:T(8,128)(2,1)} %multiply_bitcast_fusion.refs_0_, bf16[768,896]{1,0:T(8,128)(2,1)} %fusion.8.refs_1_, ...), custom_call_target="tpu_custom_call" | custom-call | flops 45097156608 | bytes 44040192 | tf_op jit(solution)/shard_map/cross_backward/pallas_call | solution.py:203
  304.8 17.9 %all-to-all-done.4 = bf16[4,768,256]{2,1,0:T(8,128)(2,1)} async-done(((bf16[4,768,256]{2,1,0:T(8,128)(2,1)}), bf16[4,768,256]{2,1,0:T(8,128)(2,1)}, u32[]{:S(2)}, u32[]{:S(2)}) %all-to-all-start.4) | async-done | bytes 1572896 | tf_op jit(solution)/shard_map/all_to_all | solution.py:384
  348.6 6.4 convolution_convert_fusion
  364.8 10.6 all_to_all.36.g_ref
  375.4 9.8 self_backward.1
  393.7 13.8 %all-to-all-done.6 = bf16[4,3,192,256]{3,2,1,0:T(8,128)(2,1)} async-done(((bf16[4,3,192,256]{3,2,1,0:T(8,128)(2,1)}), bf16[4,3,192,256]{3,2,1,0:T(8,128)(2,1)}, u32[]{:S(2)}, u32[]{:S(2)}) %all-to-all-start.6) | async-done | bytes 1179680 | tf_op jit(solution)/shard_map/all_to_all | solution.py:384
  417.3 23.2 %reduce-scatter.31.cloned.1.call-done = bf16[96,768]{1,0:T(8,128)(2,1)} async-done(((bf16[768,768]{1,0:T(8,128)(2,1)}), bf16[96,768]{1,0:T(8,128)(2,1)}) %reduce-scatter.31.cloned.1.call-update) | async-done | bytes 147472 | tf_op jit(solution)/shard_map/reduce_scatter | solution.py:534
  442.3 64.6 %reduce-scatter.29.cloned.1.call-done = bf16[96,768]{1,0:T(8,128)(2,1)} async-done(((bf16[768,768]{1,0:T(8,128)(2,1)}), bf16[96,768]{1,0:T(8,128)(2,1)}) %reduce-scatter.29.cloned.1.call-update) | async-done | bytes 147472 | tf_op jit(solution)/shard_map/reduce_scatter | solution.py:534
  508.7 70.3 %reduce-scatter.33.cloned.1.call-done = bf16[2,96,768]{2,1,0:T(8,128)(2,1)} async-done(((bf16[2,768,768]{2,1,0:T(8,128)(2,1)}), bf16[2,96,768]{2,1,0:T(8,128)(2,1)}) %reduce-scatter.33.cloned.1.call-update) | async-done | bytes 294928 | tf_op jit(solution)/shard_map/reduce_scatter | solution.py:534
  583.1 93.8 %reduce-scatter.41.cloned.1.call-done = bf16[384,768]{1,0:T(8,128)(2,1)} async-done(((bf16[3072,768]{1,0:T(8,128)(2,1)}), bf16[384,768]{1,0:T(8,128)(2,1)}) %reduce-scatter.41.cloned.1.call-update) | async-done | bytes 589840 | tf_op jit(solution)/shard_map/reduce_scatter | solution.py:534
  686.8 136.6 %reduce-scatter.37.cloned.1.call-done = bf16[96,3072]{1,0:T(8,128)(2,1)} async-done(((bf16[768,3072]{1,0:T(8,128)(2,1)}), bf16[96,3072]{1,0:T(8,128)(2,1)}) %reduce-scatter.37.cloned.1.call-update) | async-done | bytes 589840 | tf_op jit(solution)/shard_map/reduce_scatter | solution.py:534
  831.7 8.9 collective-permute-done.2
  847.5 81.3 %reduce-scatter.27.cloned.1.call-done = bf16[3,96,768]{2,1,0:T(8,128)(2,1)} async-done(((bf16[3,768,768]{2,1,0:T(8,128)(2,1)}), bf16[3,96,768]{2,1,0:T(8,128)(2,1)}) %reduce-scatter.27.cloned.1.call-update) | async-done | bytes 442384 | tf_op jit(solution)/shard_map/reduce_scatter | solution.py:534
  939.7 39.4 %psum.7 = f32[3,768]{1,0:T(4,128)} all-reduce(f32[3,768]{1,0:T(4,128)S(1)} %pad_maximum_fusion.12), channel_id=1, replica_groups=mesh['blk'=8,'dp'=4] {'blk','dp'}, use_global_device_ids=true, to_apply=%region_18.19 | all-reduce | flops 2304 | bytes 18432 | tf_op jit(solution)/shard_map/psum | solution.py:531
  983.4 13.8 %reduce-scatter.49.cloned.1.call-done = bf16[192,192]{1,0:T(8,128)(2,1)} async-done(((bf16[768,192]{1,0:T(8,128)(2,1)}), bf16[192,192]{1,0:T(8,128)(2,1)}) %reduce-scatter.49.cloned.1.call-update) | async-done | bytes 73744
  999.0 22.6 %reduce-scatter.53.cloned.1.call-done = bf16[192,384]{1,0:T(8,128)(2,1)} async-done(((bf16[768,384]{1,0:T(8,128)(2,1)}), bf16[192,384]{1,0:T(8,128)(2,1)}) %reduce-scatter.53.cloned.1.call-update) | async-done | bytes 147472
  1023.5 22.7 %reduce-scatter.39.cloned.1.call-done = bf16[96,768]{1,0:T(8,128)(2,1)} async-done(((bf16[96,3072]{1,0:T(8,128)(2,1)}), bf16[96,768]{1,0:T(8,128)(2,1)}) %reduce-scatter.39.cloned.1.call-update) | async-done | bytes 147472 | tf_op jit(solution)/shard_map/reduce_scatter | solution.py:535
  1047.9 22.8 %reduce-scatter.43.cloned.1.call-done = bf16[192,288]{1,0:T(8,128)(2,1)} async-done(((bf16[768,288]{1,0:T(8,128)(2,1)}), bf16[192,288]{1,0:T(8,128)(2,1)}) %reduce-scatter.43.cloned.1.call-update) | async-done | bytes 110608
  (268 shorter events, 235.5 us)
Async XLA Ops:
  11.8 13.5 %collective-permute-start = (bf16[128,768]{1,0:T(8,128)(2,1)}, bf16[128,768]{1,0:T(8,128)(2,1)}, u32[]{:S(2)}, u32[]{:S(2)}) collective-permute-start(bf16[128,768]{1,0:T(8,128)(2,1)} %bitcast.206), channel_id=1, source_target_pairs={{0,16},{4,20},{8,24},{12,28},{16,0},{20,4},{24,8},{28,12},{1,17},{... | collective-permute-start | bytes 589832 | tf_op jit(solution)/shard_map/ppermute | solution.py:361
  27.7 40.9 %all-to-all-start = ((bf16[4,256,768]{2,1,0:T(8,128)(2,1)}), bf16[4,256,768]{2,1,0:T(8,128)(2,1)}, u32[]{:S(2)}, u32[]{:S(2)}) async-start(bf16[4,256,768]{2,1,0:T(8,128)(2,1)} %broadcast_in_dim.40), calls=%async_computation | async-start | bytes 3145728 | tf_op jit(solution)/shard_map/all_to_all | solution.py:375
  33.4 70.3 %collective-permute-start.1 = (bf16[896,768]{1,0:T(8,128)(2,1)}, bf16[896,768]{1,0:T(8,128)(2,1)}, u32[]{:S(2)}, u32[]{:S(2)}) collective-permute-start(bf16[896,768]{1,0:T(8,128)(2,1)} %dynamic-slice_bitcast_fusion), channel_id=1, source_target_pairs={{0,16},{4,20},{8,24},{12,28},{16,0},{20,4},{24,8},{28,12},{1,17},{... | collective-permute-start | bytes 4128776 | tf_op jit(solution)/shard_map/ppermute | solution.py:361
  91.1 23.7 %all-to-all-start.1 = ((bf16[4,192,1024]{2,1,0:T(8,128)(2,1)}), bf16[4,192,1024]{2,1,0:T(8,128)(2,1)}, u32[]{:S(2)}, u32[]{:S(2)}) async-start(bf16[4,192,1024]{2,1,0:T(8,128)(2,1)} %broadcast_in_dim.41), calls=%async_computation.1 | async-start | bytes 3145728 | tf_op jit(solution)/shard_map/all_to_all | solution.py:375
  153.4 27.8 %all-to-all-start.2 = ((bf16[4,800,256]{2,1,0:T(8,128)(2,1)}), bf16[4,800,256]{2,1,0:T(8,128)(2,1)}, u32[]{:S(2)}, u32[]{:S(2)}) async-start(bf16[4,800,256]{2,1,0:T(8,128)(2,1)} %get-tuple-element.23), calls=%async_computation.2 | async-start | bytes 3276800 | tf_op jit(solution)/shard_map/all_to_all | solution.py:384
  158.5 20.2 %collective-permute-start.3 = (bf16[128,768]{1,0:T(8,128)(2,1)}, bf16[128,768]{1,0:T(8,128)(2,1)S(1)}, u32[]{:S(2)}, u32[]{:S(2)}) collective-permute-start(bf16[128,768]{1,0:T(8,128)(2,1)} %bitcast.205), channel_id=1, source_target_pairs={{0,16},{4,20},{8,24},{12,28},{16,0},{20,4},{24,8},{28,12},{1,17},{... | collective-permute-start | bytes 589832 | tf_op jit(solution)/shard_map/ppermute | solution.py:361
  297.4 25.3 %all-to-all-start.4 = ((bf16[4,768,256]{2,1,0:T(8,128)(2,1)}), bf16[4,768,256]{2,1,0:T(8,128)(2,1)}, u32[]{:S(2)}, u32[]{:S(2)}) async-start(bf16[4,768,256]{2,1,0:T(8,128)(2,1)} %get-tuple-element.26), calls=%async_computation.4 | async-start | bytes 3145728 | tf_op jit(solution)/shard_map/all_to_all | solution.py:384
  301.8 89.8 %reduce-scatter.35.cloned.1.call-start = ((), (), s32[]{:S(2)}) async-start(), calls=%async_computation.25 | async-start | bytes 1327104 | tf_op jit(solution)/shard_map/reduce_scatter | solution.py:534
  304.8 135.8 %reduce-scatter.31.cloned.1.call-start = ((), (), s32[]{:S(2)}) async-start(), calls=%async_computation.23 | async-start | bytes 1327104 | tf_op jit(solution)/shard_map/reduce_scatter | solution.py:534
  327.9 179.0 %reduce-scatter.29.cloned.1.call-start = ((), (), s32[]{:S(2)}) async-start(), calls=%async_computation.22 | async-start | bytes 1327104 | tf_op jit(solution)/shard_map/reduce_scatter | solution.py:534
  336.4 242.7 %reduce-scatter.33.cloned.1.call-start = ((), (), s32[]{:S(2)}) async-start(), calls=%async_computation.24 | async-start | bytes 2654208 | tf_op jit(solution)/shard_map/reduce_scatter | solution.py:534
  348.6 328.3 %reduce-scatter.41.cloned.1.call-start = ((), (), s32[]{:S(2)}) async-start(), calls=%async_computation.28 | async-start | bytes 5308416 | tf_op jit(solution)/shard_map/reduce_scatter | solution.py:534
  355.0 468.4 %reduce-scatter.37.cloned.1.call-start = ((), (), s32[]{:S(2)}) async-start(), calls=%async_computation.26 | async-start | bytes 5308416 | tf_op jit(solution)/shard_map/reduce_scatter | solution.py:534
  385.2 22.2 %all-to-all-start.6 = ((bf16[4,3,192,256]{3,2,1,0:T(8,128)(2,1)}), bf16[4,3,192,256]{3,2,1,0:T(8,128)(2,1)}, u32[]{:S(2)}, u32[]{:S(2)}) async-start(bf16[4,3,192,256]{3,2,1,0:T(8,128)(2,1)} %self_backward.1), calls=%async_computation.6 | async-start | bytes 2359296 | tf_op jit(solution)/shard_map/all_to_all | solution.py:384
  389.6 456.3 %reduce-scatter.51.cloned.1.call-start = ((), (), s32[]{:S(2)}) async-start(), calls=%async_computation.33 | async-start | bytes 245760
  393.4 535.4 %reduce-scatter.27.cloned.1.call-start = ((), (), s32[]{:S(2)}) async-start(), calls=%async_computation.21 | async-start | bytes 3981312 | tf_op jit(solution)/shard_map/reduce_scatter | solution.py:534
  417.2 563.1 %reduce-scatter.47.cloned.1.call-start = ((), (), s32[]{:S(2)}) async-start(), calls=%async_computation.31 | async-start | bytes 245760
  442.3 539.6 %reduce-scatter.45.cloned.1.call-start = ((), (), s32[]{:S(2)}) async-start(), calls=%async_computation.30 | async-start | bytes 245760
  508.7 488.5 %reduce-scatter.49.cloned.1.call-start = ((), (), s32[]{:S(2)}) async-start(), calls=%async_computation.32 | async-start | bytes 491520
  583.1 438.5 %reduce-scatter.53.cloned.1.call-start = ((), (), s32[]{:S(2)}) async-start(), calls=%async_computation.34 | async-start | bytes 737280
  679.1 367.2 %reduce-scatter.39.cloned.1.call-start = ((), (), s32[]{:S(2)}) async-start(), calls=%async_computation.27 | async-start | bytes 737280 | tf_op jit(solution)/shard_map/reduce_scatter | solution.py:535
  684.6 246.9 %collective-permute-start.5 = (bf16[896,768]{1,0:T(8,128)(2,1)}, bf16[896,768]{1,0:T(8,128)(2,1)}, u32[]{:S(2)}, u32[]{:S(2)}) collective-permute-start(bf16[896,768]{1,0:T(8,128)(2,1)} %add_convert_fusion.1), channel_id=1, source_target_pairs={{16,0},{20,4},{24,8},{28,12},{0,16},{4,20},{8,24},{12,28},{17,1},{... | collective-permute-start | bytes 4128776 | tf_op jit(solution)/shard_map/ppermute | solution.py:505
  823.4 247.2 %reduce-scatter.43.cloned.1.call-start = ((), (), s32[]{:S(2)}) async-start(), calls=%async_computation.29 | async-start | bytes 737280
  935.9 43.2 %collective-permute-start.4 = (bf16[128,768]{1,0:T(8,128)(2,1)S(1)}, bf16[128,768]{1,0:T(8,128)(2,1)S(1)}, u32[]{:S(2)}, u32[]{:S(2)}) collective-permute-start(bf16[128,768]{1,0:T(8,128)(2,1)S(1)} %dynamic-slice_bitcast_fusion.7), channel_id=1, source_target_pairs={{0,16},{4,20},{8,24},{12,28},{16,0},{20,4},{24,8},{28,12},{1,17},{... | collective-permute-start | bytes 589832 | tf_op jit(solution)/shard_map/ppermute | solution.py:361
  (39 other events, 216.6 us)
Sparse Core Ops, SparseCore 0:
  306.0 63.8 reduce-scatter.34
  373.3 67.1 reduce-scatter.30
  443.9 62.9 reduce-scatter.28
  510.9 68.1 reduce-scatter.32
  582.6 94.2 reduce-scatter.40
  680.4 142.9 reduce-scatter.36
  826.4 19.4 reduce-scatter.50
  849.6 79.1 reduce-scatter.26
  931.8 19.2 reduce-scatter.46
  954.0 19.7 reduce-scatter.44
  976.2 20.8 reduce-scatter.48
  999.5 22.0 reduce-scatter.52
  1024.1 22.0 reduce-scatter.38
  1048.6 22.0 reduce-scatter.42

commit v2 on v1

v2 whole, which is shorter than its diff:
```python
import functools

import jax
import jax.numpy as jnp
from jax import lax
from jax.experimental import pallas as pl
from jax.experimental.pallas import tpu as pltpu
from jax.sharding import PartitionSpec as P

HEAD_DIM = 64
SLOTS = 448
F32 = jnp.float32
BF16 = jnp.bfloat16
epsilon = 1e-06
negative_fill = -1e30
safe_score = 60.0
VMEM_LIMIT = 60 * 1024 * 1024


def dot(left, right, left_dim, right_dim):
    return lax.dot_general(
        left, right, (((left_dim,), (right_dim,)), ((), ())), preferred_element_type=F32
    )


def split_low(value):
    high = value.astype(BF16)
    return high, (value - high.astype(F32)).astype(BF16)


def normed(values, gain):
    return values * lax.rsqrt(jnp.mean(values * values, axis=-1, keepdims=True) + epsilon) * gain


def parted(array, axis, dim):
    size = lax.axis_size(axis)
    shape = array.shape
    above = size // shape[dim]
    split = array.reshape(shape[:dim] + (shape[dim] // 2, 2) + shape[dim + 1 :])
    bit = lax.rem(lax.axis_index(axis) // above, 2)
    kept = lax.dynamic_index_in_dim(split, bit, dim + 1, False)
    sent = lax.dynamic_index_in_dim(split, 1 - bit, dim + 1, False)
    return kept, sent, [(i, i ^ above) for i in range(size)]


def added(kept, got):
    return (kept.astype(F32) + got.astype(F32)).astype(BF16)


class Halving:
    def __init__(self, array):
        self.array = array

    def send(self, axis, dim):
        self.kept, sent, pairs = parted(self.array, axis, dim)
        self.got = lax.ppermute(sent, axis, pairs)

    def take(self):
        self.array = added(self.kept, self.got)


def after(value, *halvings):
    value, got = lax.optimization_barrier((value, [h.got for h in halvings]))
    for halving, piece in zip(halvings, got):
        halving.got = piece
        halving.take()
    return value


def halved(array, axis, dim):
    while array.shape[dim] > 1:
        kept, sent, pairs = parted(array, axis, dim)
        array = added(kept, lax.ppermute(sent, axis, pairs))
    return jnp.squeeze(array, dim)


def total_of(array):
    for axis in ("dp", "blk"):
        size = lax.axis_size(axis)
        copies = jnp.broadcast_to(array[None], (size,) + array.shape)
        array = jnp.sum(lax.all_to_all(copies, axis, 0, 0), axis=0)
    return array


def estimate(flops, bytes_accessed, transcendentals):
    scale = 10**9
    return pl.CostEstimate(
        flops=max(flops // scale, 1),
        bytes_accessed=max(bytes_accessed // scale, 1),
        transcendentals=transcendentals // scale,
    )


def params():
    return pltpu.CompilerParams(vmem_limit_bytes=VMEM_LIMIT)


def cross_forward(query, pairs, bias, width, groups):
    heads = width // HEAD_DIM
    length = query.shape[1]
    tokens = length // groups
    parts = len(pairs)
    rows = [p.shape[2] for p in pairs]
    starts = [sum(rows[:i]) for i in range(parts)]
    total = sum(rows)
    stat_rows = 16 * ((heads + 15) // 16)

    def kernel(*refs):
        q_ref = refs[0]
        k_refs = refs[1 : 1 + parts]
        v_refs = refs[1 + parts : 1 + 2 * parts]
        b_refs = refs[1 + 2 * parts : 1 + 3 * parts]
        o_ref, p_ref, m_ref, lse_ref = refs[1 + 3 * parts :]
        head = pl.program_id(0)
        query = q_ref[...]
        aug_query = jnp.concatenate([query, jnp.ones((16, length), BF16)], axis=0)
        q_norm = jnp.max(jnp.sum(jnp.square(query.astype(F32)), axis=0, keepdims=True))
        k_norm = jnp.float32(0)
        for k_ref in k_refs:
            k_norm = jnp.maximum(
                k_norm, jnp.max(jnp.sum(jnp.square(k_ref[0].astype(F32)), axis=0, keepdims=True))
            )
        small = q_norm * k_norm < safe_score * safe_score

        def score(i):
            return dot(jnp.concatenate([k_refs[i][0], b_refs[i][...]], axis=0), aug_query, 0, 0)

        def finish(probs, top):
            mixed = None
            for i in range(parts):
                aug_value = jnp.concatenate([v_refs[i][0], jnp.ones((16, rows[i]), BF16)], axis=0)
                term = dot(aug_value, probs[i], 1, 0)
                mixed = term if mixed is None else mixed + term
            norm = mixed[HEAD_DIM : HEAD_DIM + 1]
            out = (mixed[:HEAD_DIM] / norm).astype(BF16)
            where = pl.ds(pl.multiple_of(head * HEAD_DIM, HEAD_DIM), HEAD_DIM)
            for g in range(groups):
                o_ref[g, where, :] = out[:, g * tokens : (g + 1) * tokens]
            lse_ref[pl.ds(head, 1), :] = top + jnp.log(norm)
            m_ref[0] = top

        @pl.when(small)
        def plain():
            probs = []
            for i in range(parts):
                prob = jnp.exp(score(i)).astype(BF16)
                p_ref[0, starts[i] : starts[i] + rows[i], :] = prob
                probs.append(prob)
            finish(probs, jnp.zeros((1, length), F32))

        @pl.when(jnp.logical_not(small))
        def shifted():
            raw = [score(i) for i in range(parts)]
            top = jnp.max(raw[0], axis=0, keepdims=True)
            for i in range(1, parts):
                top = jnp.maximum(top, jnp.max(raw[i], axis=0, keepdims=True))
            probs = []
            for i in range(parts):
                prob = jnp.exp(raw[i] - top).astype(BF16)
                p_ref[0, starts[i] : starts[i] + rows[i], :] = prob
                probs.append(prob)
            finish(probs, top)

        @pl.when(head == heads - 1)
        def stats():
            high, low = split_low(lse_ref[...])
            for g in range(groups):
                o_ref[g, width : width + stat_rows, :] = high[:, g * tokens : (g + 1) * tokens]
                o_ref[g, width + stat_rows :, :] = low[:, g * tokens : (g + 1) * tokens]

    payload = width + 2 * stat_rows
    key_specs = [pl.BlockSpec((1, HEAD_DIM, r), lambda h: (0, h, 0)) for r in rows]
    value_specs = [pl.BlockSpec((1, HEAD_DIM, r), lambda h: (1, h, 0)) for r in rows]
    return pl.pallas_call(
        kernel,
        grid=(heads,),
        in_specs=[pl.BlockSpec((HEAD_DIM, length), lambda h: (h, 0))]
        + key_specs
        + value_specs
        + [pl.BlockSpec((16, r), lambda h: (0, 0)) for r in rows],
        out_specs=[
            pl.BlockSpec((groups, payload, tokens), lambda h: (0, 0, 0)),
            pl.BlockSpec((1, total, length), lambda h: (h, 0, 0)),
            pl.BlockSpec((1, 1, length), lambda h: (h, 0, 0)),
        ],
        out_shape=[
            jax.ShapeDtypeStruct((groups, payload, tokens), BF16),
            jax.ShapeDtypeStruct((heads, total, length), BF16),
            jax.ShapeDtypeStruct((heads, 1, length), F32),
        ],
        scratch_shapes=[pltpu.VMEM((stat_rows, length), F32)],
        compiler_params=params(),
        cost_estimate=estimate(
            flops=16 * heads * total * length * HEAD_DIM,
            bytes_accessed=2 * heads * total * length,
            transcendentals=heads * total * length,
        ),
        name="cross_forward",
    )(query, *pairs, *pairs, *bias)


def cross_backward(query, pairs, prob, grads, weight, delta, width, groups):
    heads = width // HEAD_DIM
    length = query.shape[1]
    tokens = length // groups
    parts = len(pairs)
    rows = [p.shape[2] for p in pairs]
    starts = [sum(rows[:i]) for i in range(parts)]
    total = sum(rows)
    pair = 2

    def kernel(*refs):
        q_ref = refs[0]
        k_refs = refs[1 : 1 + parts]
        v_refs = refs[1 + parts : 1 + 2 * parts]
        p_ref, g_ref, w_ref, d_ref = refs[1 + 2 * parts : 5 + 2 * parts]
        dq_ref = refs[5 + 2 * parts]
        dk_refs = refs[6 + 2 * parts : 6 + 3 * parts]
        dv_refs = refs[6 + 3 * parts :]
        key_out = [[] for _ in range(parts)]
        value_out = [[] for _ in range(parts)]
        for j in range(pair):
            at = slice(j * HEAD_DIM, (j + 1) * HEAD_DIM)
            grad = jnp.concatenate([g_ref[g, at, :] for g in range(groups)], axis=1).astype(F32)
            scaled = grad * w_ref[j]
            high, low = split_low(-d_ref[j])
            scaled_low = scaled.astype(BF16)
            pad = jnp.zeros((14, length), BF16)
            aug = jnp.concatenate([scaled_low, high, low, pad], axis=0)
            scaled_rows = scaled.T.astype(BF16)
            query_rows = q_ref[at, :].astype(F32).T.astype(BF16)
            query_grad = None
            for i in range(parts):
                aug_value = jnp.concatenate(
                    [v_refs[i][0, at, :], jnp.ones((16, rows[i]), BF16)], axis=0
                )
                prob = p_ref[j, starts[i] : starts[i] + rows[i], :]
                score = (prob.astype(F32) * dot(aug_value, aug, 0, 0)).astype(BF16)
                value_out[i].append(dot(prob, scaled_rows, 1, 0).astype(BF16))
                key_out[i].append(dot(score, query_rows, 1, 0).astype(BF16))
                term = dot(k_refs[i][0, at, :], score, 1, 0)
                query_grad = term if query_grad is None else query_grad + term
            query_low = (query_grad * 0.125).astype(BF16)
            for g in range(groups):
                dq_ref[g, at, :] = query_low[:, g * tokens : (g + 1) * tokens]
        for i in range(parts):
            dk_refs[i][...] = jnp.concatenate(key_out[i], axis=1)
            dv_refs[i][...] = jnp.concatenate(value_out[i], axis=1)

    size = pair * HEAD_DIM
    key_specs = [pl.BlockSpec((1, size, r), lambda h: (0, h, 0)) for r in rows]
    value_specs = [pl.BlockSpec((1, size, r), lambda h: (1, h, 0)) for r in rows]
    kv_grads = [pl.BlockSpec((r, size), lambda h: (0, h)) for r in rows]
    outs = pl.pallas_call(
        kernel,
        grid=(heads // pair,),
        in_specs=[pl.BlockSpec((size, length), lambda h: (h, 0))]
        + key_specs
        + value_specs
        + [
            pl.BlockSpec((pair, total, length), lambda h: (h, 0, 0)),
            pl.BlockSpec((groups, size, tokens), lambda h: (0, h, 0)),
            pl.BlockSpec((pair, 1, length), lambda h: (h, 0, 0)),
            pl.BlockSpec((pair, 1, length), lambda h: (h, 0, 0)),
        ],
        out_specs=[pl.BlockSpec((groups, size, tokens), lambda h: (0, h, 0))] + kv_grads + kv_grads,
        out_shape=[jax.ShapeDtypeStruct((groups, width, tokens), BF16)]
        + [jax.ShapeDtypeStruct((r, width), BF16) for r in rows] * 2,
        compiler_params=params(),
        cost_estimate=estimate(
            flops=32 * heads * total * length * HEAD_DIM,
            bytes_accessed=2 * heads * total * length,
            transcendentals=0,
        ),
        name="cross_backward",
    )(query, *pairs, *pairs, prob, grads, weight, delta)
    return outs[0], list(outs[1 : 1 + parts]), list(outs[1 + parts :])


def self_forward(inputs, gain, weights, key_pos, query_pos, groups):
    length, width = inputs.shape
    own = weights.shape[1]
    heads = own // HEAD_DIM

    def kernel(x_ref, g_ref, w_ref, kp_ref, qp_ref, a_ref, pr_ref, o_ref, p_ref, n_ref):
        head = pl.program_id(0)

        @pl.when(head == 0)
        def project():
            low = normed(x_ref[...].astype(F32), g_ref[...]).astype(BF16)
            a_ref[...] = low
            for c in range(3):
                pr_ref[c] = dot(w_ref[c], low, 1, 1).astype(BF16)

        at = pl.ds(pl.multiple_of(head * HEAD_DIM, HEAD_DIM), HEAD_DIM)
        raw = dot(pr_ref[1, at, :], pr_ref[0, at, :], 0, 0) * 0.125
        raw = jnp.where(kp_ref[...] <= qp_ref[...], raw, negative_fill)
        top = jnp.max(raw, axis=0, keepdims=True)
        prob = jnp.exp(raw - top).astype(BF16)
        p_ref[0] = prob
        aug_value = jnp.concatenate([pr_ref[2, at, :], jnp.ones((16, length), BF16)], axis=0)
        mixed = dot(aug_value, prob, 1, 0)
        inverse = 1.0 / mixed[HEAD_DIM : HEAD_DIM + 1]
        out = (mixed[:HEAD_DIM] * inverse).astype(BF16)
        for g in range(groups):
            o_ref[g] = out
        n_ref[0] = inverse

    whole = lambda *shape: pl.BlockSpec(shape, lambda h: (0,) * len(shape))
    return pl.pallas_call(
        kernel,
        grid=(heads,),
        in_specs=[
            whole(length, width),
            whole(1, width),
            whole(3, own, width),
            whole(length, 1),
            whole(1, length),
        ],
        out_specs=[
            whole(length, width),
            whole(3, own, length),
            pl.BlockSpec((groups, HEAD_DIM, length), lambda h: (0, h, 0)),
            pl.BlockSpec((1, length, length), lambda h: (h, 0, 0)),
            pl.BlockSpec((1, 1, length), lambda h: (h, 0, 0)),
        ],
        out_shape=[
            jax.ShapeDtypeStruct((length, width), BF16),
            jax.ShapeDtypeStruct((3, own, length), BF16),
            jax.ShapeDtypeStruct((groups, own, length), BF16),
            jax.ShapeDtypeStruct((heads, length, length), BF16),
            jax.ShapeDtypeStruct((heads, 1, length), F32),
        ],
        compiler_params=params(),
        cost_estimate=estimate(
            flops=16 * heads * length * length * HEAD_DIM,
            bytes_accessed=2 * heads * length * length,
            transcendentals=heads * length * length,
        ),
        name="self_forward",
    )(inputs, gain, weights, key_pos, query_pos)


def project_rows(pieces, weights):
    counts = [p.shape[0] for p in pieces]
    total, width = sum(counts), pieces[0].shape[1]

    def kernel(*refs):
        w_ref, out_ref = refs[len(counts) :]
        start = 0
        for e_ref, count in zip(refs, counts):
            out_ref[0, :, start : start + count] = dot(w_ref[0], e_ref[...], 1, 1).astype(BF16)
            start += count

    return pl.pallas_call(
        kernel,
        grid=(2,),
        in_specs=[pl.BlockSpec((count, width), lambda c: (0, 0)) for count in counts]
        + [pl.BlockSpec((1, width, width), lambda c: (c, 0, 0))],
        out_specs=pl.BlockSpec((1, width, total), lambda c: (c, 0, 0)),
        out_shape=jax.ShapeDtypeStruct((2, width, total), BF16),
        compiler_params=params(),
        cost_estimate=estimate(
            flops=4 * total * width * width, bytes_accessed=8 * total * width, transcendentals=0
        ),
        name="project_rows",
    )(*pieces, weights)


def query_stage(inputs, mixed, out_weight, gain, query_weight, slot, groups):
    length, width = inputs.shape
    tokens = length // groups
    rows = mixed.shape[0]

    def kernel(s_ref, x_ref, o_ref, w_ref, g_ref, q_ref, qc_ref, h_ref, a_ref):
        after = x_ref[...].astype(F32) + dot(o_ref[...], w_ref[...], 0, 0)
        low = normed(after, g_ref[...]).astype(BF16)
        scaled = dot(q_ref[...], low, 1, 1).astype(BF16)
        qc_ref[...] = (scaled.astype(F32) * 0.125).astype(BF16)

        @pl.when(pl.program_id(0) == s_ref[0])
        def keep():
            h_ref[...] = after
            a_ref[...] = low

    whole = lambda *shape: pl.BlockSpec(shape, lambda i, s: (0,) * len(shape))
    return pl.pallas_call(
        kernel,
        grid_spec=pltpu.PrefetchScalarGridSpec(
            num_scalar_prefetch=1,
            grid=(groups,),
            in_specs=[
                pl.BlockSpec((tokens, width), lambda i, s: (i, 0)),
                pl.BlockSpec((rows, tokens), lambda i, s: (0, i)),
                whole(rows, width),
                whole(1, width),
                whole(width, width),
            ],
            out_specs=[
                pl.BlockSpec((width, tokens), lambda i, s: (0, i)),
                whole(tokens, width),
                whole(tokens, width),
            ],
        ),
        out_shape=[
            jax.ShapeDtypeStruct((width, length), BF16),
            jax.ShapeDtypeStruct((tokens, width), F32),
            jax.ShapeDtypeStruct((tokens, width), BF16),
        ],
        compiler_params=params(),
        cost_estimate=estimate(
            flops=8 * length * width * width, bytes_accessed=8 * width * width, transcendentals=0
        ),
        name="query_stage",
    )(slot, inputs, mixed, out_weight, gain, query_weight)


def gelu_parts(value):
    root = 0.7978845608028654
    cubic = 0.044715
    square = value * value
    bent = jnp.tanh(root * value * (1.0 + cubic * square))
    half = 0.5 * (1.0 + bent)
    slope = half + 0.5 * value * (1.0 - bent * bent) * root * (1.0 + 3.0 * cubic * square)
    return value * half, slope


def pulled_norm(values, gain, grad):
    inverse = lax.rsqrt(jnp.mean(values * values, axis=-1, keepdims=True) + epsilon)
    scaled = values * inverse
    gain_grad = jnp.sum(grad * scaled, axis=0, keepdims=True)
    weighted = grad * gain
    back = inverse * (weighted - scaled * jnp.mean(weighted * scaled, axis=-1, keepdims=True))
    return back, gain_grad


def token_stage(parts, after_self, cross_out, gain, ffn_in, ffn_out, cotangent, groups):
    tokens, width = after_self.shape
    heads = width // HEAD_DIM
    stat_rows = (parts.shape[1] - width) // 2
    hidden = ffn_in.shape[1]
    piece = 384
    steps = hidden // piece
    payload = width + 4 * stat_rows

    def kernel(
        r_ref, h_ref, co_ref, g_ref, w1_ref, w2_ref, c_ref,
        out_ref, dh_ref, g2_ref, a_ref, z_ref, du_ref, o_ref, pay_ref, gain_ref,
        after_ref, acc_ref, back_ref, lse_ref,
    ):
        step = pl.program_id(0)

        @pl.when(step == 0)
        def join():
            lse = [
                r_ref[g, width : width + stat_rows, :].astype(F32)
                + r_ref[g, width + stat_rows :, :].astype(F32)
                for g in range(groups)
            ]
            top = functools.reduce(jnp.maximum, lse)
            share = [jnp.exp(l - top) for l in lse]
            total = functools.reduce(jnp.add, share)
            lse_ref[...] = top + jnp.log(total)
            share = [s / total for s in share]
            for h in range(heads):
                at = slice(h * HEAD_DIM, (h + 1) * HEAD_DIM)
                mixed = None
                for g in range(groups):
                    term = r_ref[g, at, :].astype(F32) * share[g][h : h + 1]
                    mixed = term if mixed is None else mixed + term
                o_ref[at, :] = mixed.astype(BF16)
            after = h_ref[...] + dot(o_ref[...], co_ref[...], 0, 0)
            after_ref[...] = after
            a_ref[...] = normed(after, g_ref[...]).astype(BF16)
            acc_ref[...] = jnp.zeros_like(acc_ref)
            back_ref[...] = jnp.zeros_like(back_ref)

        pre = dot(a_ref[...], w1_ref[...], 1, 0)
        act, slope = gelu_parts(pre)
        act = act.astype(BF16)
        z_ref[...] = act
        acc_ref[...] += dot(act, w2_ref[...], 1, 0)
        pre_grad = (dot(c_ref[...], w2_ref[...], 1, 1) * slope).astype(BF16)
        du_ref[...] = pre_grad
        back_ref[...] += dot(pre_grad, w1_ref[...], 1, 1)

        @pl.when(step == steps - 1)
        def finish():
            after = after_ref[...]
            out_ref[...] = (after + acc_ref[...]).astype(BF16)
            back, gain_grad = pulled_norm(after, g_ref[...], back_ref[...])
            gain_ref[...] = gain_grad
            grad = c_ref[...].astype(F32) + back
            dh_ref[...] = grad
            low = grad.astype(BF16)
            g2_ref[...] = low
            mix_grad = dot(co_ref[...], low, 1, 1).astype(BF16)
            both = mix_grad.astype(F32) * o_ref[...].astype(F32)
            rows = [
                jnp.sum(both[h * HEAD_DIM : (h + 1) * HEAD_DIM], axis=0, keepdims=True)
                for h in range(heads)
            ]
            rows.append(jnp.zeros((stat_rows - heads, tokens), F32))
            stats = [*split_low(lse_ref[...]), *split_low(jnp.concatenate(rows, axis=0))]
            for g in range(groups):
                pay_ref[g, :width, :] = mix_grad
                for i in range(4):
                    start = width + i * stat_rows
                    pay_ref[g, start : start + stat_rows, :] = stats[i]

    whole = lambda *shape: pl.BlockSpec(shape, lambda i: (0,) * len(shape))
    flat = lambda rows, kind: jax.ShapeDtypeStruct((rows, width), kind)
    return pl.pallas_call(
        kernel,
        grid=(steps,),
        in_specs=[
            whole(*parts.shape),
            whole(tokens, width),
            whole(width, width),
            whole(1, width),
            pl.BlockSpec((width, piece), lambda i: (0, i)),
            pl.BlockSpec((piece, width), lambda i: (i, 0)),
            whole(tokens, width),
        ],
        out_specs=[
            whole(tokens, width),
            whole(tokens, width),
            whole(tokens, width),
            whole(tokens, width),
            pl.BlockSpec((tokens, piece), lambda i: (0, i)),
            pl.BlockSpec((tokens, piece), lambda i: (0, i)),
            whole(width, tokens),
            whole(groups, payload, tokens),
            whole(1, width),
        ],
        out_shape=[
            flat(tokens, BF16),
            flat(tokens, F32),
            flat(tokens, BF16),
            flat(tokens, BF16),
            jax.ShapeDtypeStruct((tokens, hidden), BF16),
            jax.ShapeDtypeStruct((tokens, hidden), BF16),
            jax.ShapeDtypeStruct((width, tokens), BF16),
            jax.ShapeDtypeStruct((groups, payload, tokens), BF16),
            flat(1, F32),
        ],
        scratch_shapes=[pltpu.VMEM((tokens, width), F32)] * 3
        + [pltpu.VMEM((stat_rows, tokens), F32)],
        compiler_params=params(),
        cost_estimate=estimate(
            flops=8 * tokens * width * hidden,
            bytes_accessed=4 * width * hidden,
            transcendentals=tokens * hidden,
        ),
        name="token_stage",
    )(parts, after_self, cross_out, gain, ffn_in, ffn_out, cotangent)


def hidden_weight_grads(low, pre_grad, act, cotangent, columns, blocks):
    tokens, width = low.shape
    hidden = act.shape[1]
    piece = hidden // blocks
    in_rows, out_rows = width // blocks, piece // columns
    per = width // piece

    def kernel(a_ref, du_ref, z_ref, c_ref, in_ref, out_ref):
        first = dot(a_ref[...], du_ref[...], 0, 0).astype(BF16)
        for b in range(blocks):
            in_ref[0, b] = first[b * in_rows : (b + 1) * in_rows]
        second = dot(z_ref[...], c_ref[...], 0, 0).astype(BF16)
        for d in range(columns):
            out_ref[d, 0] = second[d * out_rows : (d + 1) * out_rows]

    whole = lambda *shape: pl.BlockSpec(shape, lambda i: (0,) * len(shape))
    return pl.pallas_call(
        kernel,
        grid=(blocks,),
        in_specs=[
            whole(tokens, width),
            pl.BlockSpec((tokens, piece), lambda i: (0, i)),
            pl.BlockSpec((tokens, piece), lambda i: (0, i)),
            whole(tokens, width),
        ],
        out_specs=[
            pl.BlockSpec((1, blocks, in_rows, piece), lambda i: (i // per, 0, 0, i % per)),
            pl.BlockSpec((columns, 1, out_rows, width), lambda i: (0, i, 0, 0)),
        ],
        out_shape=[
            jax.ShapeDtypeStruct((columns, blocks, in_rows, width), BF16),
            jax.ShapeDtypeStruct((columns, blocks, out_rows, width), BF16),
        ],
        compiler_params=params(),
        cost_estimate=estimate(
            flops=4 * tokens * width * hidden,
            bytes_accessed=4 * width * hidden,
            transcendentals=0,
        ),
        name="hidden_weight_grads",
    )(low, pre_grad, act, cotangent)


def mixed_stage(parts, cross_q, after_self, gain, cross_grad, self_out, groups, own):
    tokens, width = after_self.shape
    rows = self_out.shape[0]

    def kernel(r_ref, q_ref, h_ref, g_ref, dh_ref, w_ref, dq_ref, out_ref, g1_ref, do_ref, gain_ref):
        total = r_ref[0].astype(F32)
        for g in range(1, groups):
            total = total + r_ref[g].astype(F32)
        query_grad = total.astype(BF16)
        dq_ref[...] = query_grad
        back, gain_grad = pulled_norm(h_ref[...], g_ref[...], dot(query_grad, q_ref[...], 0, 1))
        gain_ref[...] = gain_grad
        grad = dh_ref[...] + back
        out_ref[...] = grad
        low = grad.astype(BF16)
        g1_ref[...] = low
        mixed = dot(w_ref[...], low, 1, 1).astype(BF16)
        for g in range(groups):
            do_ref[g] = mixed[g * own : (g + 1) * own]

    return pl.pallas_call(
        kernel,
        out_shape=[
            jax.ShapeDtypeStruct((width, tokens), BF16),
            jax.ShapeDtypeStruct((tokens, width), F32),
            jax.ShapeDtypeStruct((tokens, width), BF16),
            jax.ShapeDtypeStruct((groups, own, tokens), BF16),
            jax.ShapeDtypeStruct((1, width), F32),
        ],
        compiler_params=params(),
        cost_estimate=estimate(
            flops=4 * tokens * width * width, bytes_accessed=8 * width * width, transcendentals=0
        ),
        name="mixed_stage",
    )(parts, cross_q, after_self, gain, cross_grad, self_out)


def input_stage(back, weights, inputs, gain, self_grad, groups):
    own, tokens = back.shape[2:]
    width = inputs.shape[1]
    padded = groups * own

    def kernel(b_ref, w_ref, x_ref, g_ref, h_ref, out_ref, acc_ref):
        step = pl.program_id(0)
        grads = jnp.concatenate([b_ref[g, 0] for g in range(groups)], axis=0)
        term = dot(grads, w_ref[0], 0, 1)

        @pl.when(step == 0)
        def first():
            acc_ref[...] = term

        @pl.when(step > 0)
        def more():
            acc_ref[...] += term

        @pl.when(step == 2)
        def last():
            back, unused = pulled_norm(x_ref[...].astype(F32), g_ref[...], acc_ref[...])
            out_ref[...] = (h_ref[...] + back).astype(BF16)

    whole = lambda *shape: pl.BlockSpec(shape, lambda i: (0,) * len(shape))
    return pl.pallas_call(
        kernel,
        grid=(3,),
        in_specs=[
            pl.BlockSpec((groups, 1, own, tokens), lambda i: (0, i, 0, 0)),
            pl.BlockSpec((1, width, padded), lambda i: (i, 0, 0)),
            whole(tokens, width),
            whole(1, width),
            whole(tokens, width),
        ],
        out_specs=whole(tokens, width),
        out_shape=jax.ShapeDtypeStruct((tokens, width), BF16),
        scratch_shapes=[pltpu.VMEM((tokens, width), F32)],
        compiler_params=params(),
        cost_estimate=estimate(
            flops=6 * tokens * width * width, bytes_accessed=6 * width * width, transcendentals=0
        ),
        name="input_stage",
    )(back, weights, inputs, gain, self_grad)


def both_queries(own, pieces, mine):
    rows, width = own.shape

    def kernel(s_ref, own_ref, *refs):
        out_ref = refs[-1]

        @pl.when(pl.program_id(0) == s_ref[0])
        def here():
            out_ref[0] = own_ref[...]

        @pl.when(pl.program_id(0) != s_ref[0])
        def there():
            start = 0
            for ref in refs[:-1]:
                out_ref[0, start : start + ref.shape[0], :] = ref[...]
                start += ref.shape[0]

    whole = lambda *shape: pl.BlockSpec(shape, lambda i, s: (0,) * len(shape))
    return pl.pallas_call(
        kernel,
        grid_spec=pltpu.PrefetchScalarGridSpec(
            num_scalar_prefetch=1,
            grid=(2,),
            in_specs=[whole(*own.shape)] + [whole(*p.shape) for p in pieces],
            out_specs=pl.BlockSpec((1, rows, width), lambda i, s: (i, 0, 0)),
        ),
        out_shape=jax.ShapeDtypeStruct((2, rows, width), own.dtype),
        compiler_params=params(),
        cost_estimate=estimate(flops=0, bytes_accessed=8 * rows * width, transcendentals=0),
        name="both_queries",
    )(mine, own, *pieces)


def own_weight_grads(low, inputs, grads, weights, blocks):
    length, width = inputs.shape
    groups, _, own, tokens = grads.shape
    rows = width // blocks

    def kernel(a_ref, x_ref, d_ref, w_ref, out_ref, gain_ref, acc_ref):
        step = pl.program_id(0)
        grads = jnp.concatenate([d_ref[g, 0] for g in range(groups)], axis=1)
        weight = dot(grads, a_ref[...], 1, 0).T.astype(BF16)
        for b in range(blocks):
            out_ref[b, 0] = weight[b * rows : (b + 1) * rows]
        term = dot(grads, w_ref[0], 0, 0)

        @pl.when(step == 0)
        def first():
            acc_ref[...] = term

        @pl.when(step > 0)
        def more():
            acc_ref[...] += term

        @pl.when(step == 2)
        def last():
            values = x_ref[...].astype(F32)
            inverse = lax.rsqrt(jnp.mean(values * values, axis=-1, keepdims=True) + epsilon)
            gain_ref[...] = jnp.sum(acc_ref[...] * values * inverse, axis=0, keepdims=True)

    whole = lambda *shape: pl.BlockSpec(shape, lambda i: (0,) * len(shape))
    return pl.pallas_call(
        kernel,
        grid=(3,),
        in_specs=[
            whole(length, width),
            whole(length, width),
            pl.BlockSpec((groups, 1, own, tokens), lambda i: (0, i, 0, 0)),
            pl.BlockSpec((1, own, width), lambda i: (i, 0, 0)),
        ],
        out_specs=[pl.BlockSpec((blocks, 1, rows, own), lambda i: (0, i, 0, 0)), whole(1, width)],
        out_shape=[
            jax.ShapeDtypeStruct((blocks, 3, rows, own), BF16),
            jax.ShapeDtypeStruct((1, width), F32),
        ],
        scratch_shapes=[pltpu.VMEM((length, width), F32)],
        compiler_params=params(),
        cost_estimate=estimate(
            flops=12 * length * width * own, bytes_accessed=4 * length * width, transcendentals=0
        ),
        name="own_weight_grads",
    )(low, inputs, grads, weights)


def self_backward(projected, mixed, grads, prob, weight, groups):
    own, length = projected.shape[1:]
    heads = own // HEAD_DIM
    tokens = length // groups

    def kernel(q_ref, k_ref, v_ref, o_ref, g_ref, p_ref, w_ref, out_ref):
        grad = jnp.concatenate([g_ref[g] for g in range(groups)], axis=1).astype(F32)
        scaled = grad * w_ref[0]
        high, low = split_low(-jnp.sum(scaled * o_ref[0].astype(F32), axis=0, keepdims=True))
        scaled_low = scaled.astype(BF16)
        aug = jnp.concatenate([scaled_low, high, low, jnp.zeros((14, length), BF16)], axis=0)
        aug_value = jnp.concatenate([v_ref[0], jnp.ones((16, length), BF16)], axis=0)
        prob = p_ref[0]
        score = (prob.astype(F32) * dot(aug_value, aug, 0, 0)).astype(BF16)
        results = (
            dot(k_ref[0], score, 1, 0) * 0.125,
            dot(q_ref[0], score, 1, 1) * 0.125,
            dot(scaled_low, prob, 1, 1),
        )
        for c in range(3):
            result = results[c].astype(BF16)
            for g in range(groups):
                out_ref[g, c] = result[:, g * tokens : (g + 1) * tokens]

    spec = lambda c: pl.BlockSpec((1, HEAD_DIM, length), lambda h: (c, h, 0))
    return pl.pallas_call(
        kernel,
        grid=(heads,),
        in_specs=[
            spec(0),
            spec(1),
            spec(2),
            pl.BlockSpec((1, HEAD_DIM, length), lambda h: (0, h, 0)),
            pl.BlockSpec((groups, HEAD_DIM, tokens), lambda h: (0, h, 0)),
            pl.BlockSpec((1, length, length), lambda h: (h, 0, 0)),
            pl.BlockSpec((1, 1, length), lambda h: (h, 0, 0)),
        ],
        out_specs=pl.BlockSpec((groups, 3, HEAD_DIM, tokens), lambda h: (0, 0, h, 0)),
        out_shape=jax.ShapeDtypeStruct((groups, 3, own, tokens), BF16),
        compiler_params=params(),
        cost_estimate=estimate(
            flops=32 * heads * length * length * HEAD_DIM,
            bytes_accessed=2 * heads * length * length,
            transcendentals=0,
        ),
        name="self_backward",
    )(projected, projected, projected, mixed, grads, prob, weight)


def body(
    dec_input,
    enc_output,
    lengths,
    gains,
    self_qkv,
    self_out,
    cross_q,
    cross_kv,
    cross_out,
    ffn_in,
    ffn_out,
    cotangent,
):
    seg, seqs, width = dec_input.shape
    heads = width // HEAD_DIM
    blocks = lax.axis_size("blk")
    place = lax.axis_index("blk")
    groups = blocks // seqs
    mine = place // groups
    slot_of = lax.rem(place, groups)
    members = [[s * groups + g for g in range(groups)] for s in range(seqs)]
    own_heads = -(-heads // groups)
    own = own_heads * HEAD_DIM
    padded = own * groups
    tokens = seqs * seg
    length = groups * tokens
    enc_rows = enc_output.shape[1]
    columns = lax.axis_size("dp")
    gain_rows = gains.astype(F32)[:, None, :]

    def shifted(step):
        return [(b, (b + step * groups) % blocks) for b in range(blocks)]

    def exchange(pieces):
        parts = [pieces(mine)]
        for step in range(1, seqs):
            parts.append(lax.ppermute(pieces(lax.rem(mine + step, seqs)), "blk", shifted(step)))
        return parts

    def in_order(parts):
        ordered = []
        for s in range(seqs):
            choice = parts[0]
            for step in range(1, seqs):
                from_there = lax.rem(mine - step + seqs, seqs) == s
                choice = jnp.where(from_there, parts[step], choice)
            ordered.append(choice)
        return ordered

    def spread(array):
        return lax.all_to_all(
            jnp.broadcast_to(array[None], (groups,) + array.shape),
            "blk",
            0,
            0,
            axis_index_groups=members,
        )

    def traded(array):
        return lax.all_to_all(array, "blk", 0, 0, axis_index_groups=members)

    def gathered(array):
        by_query = lax.optimization_barrier(array.swapaxes(0, 1))
        take = lambda s: lax.dynamic_index_in_dim(by_query, s, 0, False)
        return jnp.concatenate(in_order(exchange(take)), axis=0)

    def leaving(array):
        split = array.reshape(seqs, seg, width)
        return exchange(lambda s: lax.dynamic_index_in_dim(split, s, 0, False))

    def returned(parts):
        return jnp.stack(in_order(parts), axis=1)

    own_inputs = gathered(dec_input)
    all_inputs = spread(own_inputs).reshape(length, width)

    pick = lambda s: lax.dynamic_index_in_dim(enc_output, s, 0, False)
    cuts = [max(enc_rows * 3 // 7 // 128 * 128, 128)]
    cuts.append(cuts[0] + 128)
    spans = [(0, 0, enc_rows)]
    arrived = []
    for step in range(1, seqs):
        sent = pick(lax.rem(mine + step, seqs))
        arrived.append([lax.ppermute(sent[: cuts[0]], "blk", shifted(step))])
        spans += [(step, 0, cuts[0]), (step, cuts[0], enc_rows)]
        for start, stop in ((cuts[0], cuts[1]), (cuts[1], enc_rows)):
            piece, unused = lax.optimization_barrier((sent[start:stop], arrived[-1][-1]))
            arrived[-1].append(lax.ppermute(piece, "blk", shifted(step)))
    own_rows_low = pick(mine)
    turned_kv = cross_kv.swapaxes(1, 2)
    first_pair = project_rows([own_rows_low], turned_kv)
    all_inputs, first_pair, firsts = lax.optimization_barrier(
        (all_inputs, first_pair, [a[0] for a in arrived])
    )

    row_lengths = lax.dynamic_index_in_dim(lengths, mine, 0, False)
    bias = []
    for step, start, stop in spans:
        source = lax.rem(place - step * groups + blocks, blocks)
        slot = source * enc_rows + jnp.arange(start, stop)
        match = (slot // SLOTS)[:, None] == jnp.arange(lengths.shape[1])[None, :]
        filled = jnp.sum(jnp.where(match, row_lengths[None, :], 0), axis=-1)
        row = jnp.where((slot % SLOTS) < filled, 0.0, negative_fill).astype(BF16)
        bias.append(jnp.concatenate([row[None], jnp.zeros((15, stop - start), BF16)], axis=0))

    extra = [(0, 0), (0, 0), (0, padded - width)]
    padded_qkv = jnp.pad(self_qkv, extra)
    own_qkv = lax.dynamic_slice_in_dim(padded_qkv, slot_of * own, own, 2).swapaxes(1, 2)
    padded_out = jnp.pad(self_out, [(0, padded - width), (0, 0)])
    index = jnp.arange(length)
    block = index // seg
    position = ((block % seqs) * groups + block // seqs) * seg + index % seg
    position = position.astype(jnp.int32)
    first_low, projected, sent_mix, self_prob, self_weight = self_forward(
        all_inputs,
        gain_rows[0],
        own_qkv,
        position[:, None],
        position[None, :],
        groups,
    )
    sent_mix, seconds = lax.optimization_barrier((sent_mix, [a[1] for a in arrived]))
    self_mix = traded(sent_mix).reshape(padded, length)
    slot = jnp.full((1,), slot_of, jnp.int32)
    cross_query, after_self, second_low = query_stage(
        all_inputs, self_mix, padded_out, gain_rows[1], cross_q.T, slot, groups
    )

    cross_query, thirds = lax.optimization_barrier((cross_query, [a[2] for a in arrived]))
    encoded = [own_rows_low]
    pairs = [first_pair]
    for first, second, third in zip(firsts, seconds, thirds):
        pairs.append(project_rows([first], turned_kv))
        pairs.append(project_rows([second, third], turned_kv))
        encoded += [first, jnp.concatenate([second, third], axis=0)]

    def own_rows(array):
        return lax.dynamic_slice_in_dim(array, slot_of * tokens, tokens, 0)

    own_self_mix = lax.dynamic_slice_in_dim(self_mix, slot_of * tokens, tokens, 1)

    part_mix, cross_prob, local_top = cross_forward(cross_query, pairs, bias, width, groups)
    stat_rows = (part_mix.shape[1] - width) // 2

    own_cotangent = gathered(cotangent)
    (
        own_output,
        cross_grad,
        cross_grad_low,
        third_low,
        hidden_low,
        pre_low,
        cross_mix,
        payload,
        gain_three,
    ) = token_stage(
        traded(part_mix),
        after_self,
        cross_out,
        gain_rows[2],
        ffn_in,
        ffn_out,
        own_cotangent,
        groups,
    )
    packed = traded(payload)

    def by_rows(grad):
        return grad.astype(BF16).reshape(blocks, columns, -1, grad.shape[-1]).swapaxes(0, 1)

    def placed(rows, counts):
        count, full = rows.shape
        split = rows.reshape(count, columns, full // columns).swapaxes(0, 1)
        moved = lax.all_to_all(split, "dp", 0, 0).astype(F32)
        ends = [sum(counts[: i + 1]) for i in range(len(counts) - 1)]
        return [p.reshape(-1, full // columns) for p in jnp.split(moved, ends, axis=1)]

    cross_out_chunks = by_rows(dot(cross_mix, cross_grad_low, 1, 0))
    unit = width // blocks // columns
    staged = (
        padded == width
        and columns * own == width
        and columns * seqs == blocks
        and ffn_in.shape[1] == columns * width
        and width % (ffn_in.shape[1] // blocks) == 0
    )
    if staged:
        in_chunks, out_chunks = hidden_weight_grads(
            third_low, pre_low, hidden_low, own_cotangent, columns, blocks
        )
        chunks = jnp.concatenate([in_chunks, out_chunks], axis=2)
        packed, chunks, own_output = lax.optimization_barrier((packed, chunks, own_output))
        inner = chunks.shape[1:]
        hidden = lax.psum_scatter(
            chunks.reshape(-1, width), "dp", scatter_dimension=0, tiled=True
        )
    else:
        in_chunks = dot(third_low, pre_low, 0, 0).astype(BF16)
        in_chunks = in_chunks.reshape(blocks, width // blocks, columns, -1).transpose(2, 0, 1, 3)
        out_chunks = by_rows(dot(hidden_low, own_cotangent, 0, 0))
    output_parts = leaving(own_output)

    def whole_rows(start):
        rows = packed[:, start : start + 2 * stat_rows].astype(F32)
        rows = (rows[:, :stat_rows] + rows[:, stat_rows:])[:, :heads]
        return rows.transpose(1, 0, 2).reshape(heads, 1, length)

    scale = jnp.exp(local_top - whole_rows(width))
    query_parts, key_low, value_low = cross_backward(
        cross_query,
        pairs,
        cross_prob,
        packed,
        scale,
        whole_rows(width + 2 * stat_rows) * scale,
        width,
        groups,
    )
    query_parts, output_parts = lax.optimization_barrier((query_parts, output_parts))
    joined = traded(query_parts)
    enc_parts = [
        (dot(k, cross_kv[0], 1, 1) + dot(v, cross_kv[1], 1, 1)).astype(BF16)
        for k, v in zip(key_low, value_low)
    ]
    shares = [0, 4, 6, 8, 14]
    marks = [enc_rows * share // 14 // 16 * 16 for share in shares]
    enc_rest = [
        jnp.concatenate(enc_parts[2 * step - 1 : 2 * step + 1], axis=0) for step in range(1, seqs)
    ]
    enc_back = [[] for _ in enc_rest]

    def send_back(number):
        for step, rest in enumerate(enc_rest, 1):
            piece = rest[marks[number] : marks[number + 1]]
            if number:
                piece, unused = lax.optimization_barrier((piece, enc_back[step - 1][-1]))
            moved = lax.ppermute(piece, "blk", [(b, a) for a, b in shifted(step)])
            enc_back[step - 1].append(moved)

    def wait_back(value):
        value, last = lax.optimization_barrier((value, [back[-1] for back in enc_back]))
        for back, piece in zip(enc_back, last):
            back[-1] = piece
        return value

    send_back(0)
    key_chunks = by_rows(sum(dot(e, g, 0, 0) for e, g in zip(encoded, key_low)))
    value_chunks = by_rows(sum(dot(e, g, 0, 0) for e, g in zip(encoded, value_low)))
    if staged:
        firsts = Halving(jnp.concatenate([key_chunks, value_chunks], axis=2))
        joined, firsts.array, hidden = lax.optimization_barrier((joined, firsts.array, hidden))
    joined = wait_back(joined)
    send_back(1)
    if staged:
        hidden = lax.psum_scatter(hidden, "blk", scatter_dimension=0, tiled=True)
        firsts.send("dp", 0)

    query_grad, self_grad, self_grad_low, mixed_grad, gain_two = mixed_stage(
        joined, cross_q, after_self, gain_rows[1], cross_grad, padded_out, groups, own
    )
    own_mixed = traded(mixed_grad)
    cross_q_chunks = by_rows(dot(second_low, query_grad, 0, 1))
    self_out_chunks = by_rows(dot(own_self_mix[:width], self_grad_low, 1, 0))
    own_mixed, cross_q_chunks, self_out_chunks = wait_back(
        (own_mixed, cross_q_chunks, self_out_chunks)
    )
    send_back(2)
    if staged:
        seconds = Halving(
            jnp.concatenate([cross_out_chunks, cross_q_chunks, self_out_chunks], axis=2)
        )
        own_mixed = after(own_mixed, firsts)
        firsts.send("dp", 0)
        seconds.send("dp", 0)
    own_grads = self_backward(projected, sent_mix, own_mixed, self_prob, self_weight, groups)
    own_grads = wait_back(own_grads)
    if staged:
        own_grads = after(own_grads, firsts, seconds)
    send_back(3)
    back = traded(own_grads)
    if staged:
        firsts.array = jnp.squeeze(firsts.array, 0)
        firsts.send("blk", 0)
        seconds.send("dp", 0)
        part, gain_one = own_weight_grads(first_low, all_inputs, own_grads, own_qkv, blocks)
        back, part, gain_one = wait_back((back, part, gain_one))
        back = after(back, firsts, seconds)
        part = halved(part.reshape((columns, seqs) + part.shape[1:]), "dp", 0)
        seconds.array = jnp.squeeze(seconds.array, 0)
        seconds.send("blk", 0)
    own_grad = input_stage(
        back, padded_qkv, own_rows(all_inputs), gain_rows[0], self_grad, groups
    )
    if not staged:
        own_first = own_rows(first_low)
        full = back.transpose(1, 0, 2, 3).reshape(3, padded, tokens)[:, :width]
        first_back = sum(dot(full[c], self_qkv[c], 0, 1) for c in range(3))
        unused, gain_one = pulled_norm(
            own_rows(all_inputs).astype(F32), gain_rows[0], first_back
        )
        part = jnp.concatenate([by_rows(dot(own_first, full[c], 0, 1)) for c in range(3)], axis=2)
    gain_grads = total_of(jnp.concatenate([gain_one, gain_two, gain_three], axis=0))
    dec_grad = returned(leaving(own_grad))
    output = returned(output_parts)
    if seqs == 2:
        enc_grad = both_queries(enc_parts[0], enc_back[0], jnp.full((1,), mine, jnp.int32))
    else:
        enc_back = [enc_parts[0]] + [jnp.concatenate(pieces, axis=0) for pieces in enc_back]
        enc_grad = []
        for s in range(seqs):
            choice = enc_back[0]
            for step in range(1, seqs):
                choice = jnp.where(lax.rem(mine + step, seqs) == s, enc_back[step], choice)
            enc_grad.append(choice)
        enc_grad = jnp.stack(enc_grad, axis=0)

    if staged:
        seconds.take()
        rest = jnp.concatenate([firsts.array, seconds.array], axis=1)
        rest = halved(rest, "blk", 0)
        ffn_in_rows = hidden[: width // blocks]
        placed_rows = placed(
            jnp.concatenate([hidden[width // blocks :], rest], axis=0),
            [width // blocks] + [unit] * 5,
        )
        ffn_out_own, key_own, value_own, cross_out_own, cross_q_own, self_out_own = placed_rows
        qkv = 0.0
        for step in range(seqs):
            pairs = []
            for b in range(blocks):
                row = (b // groups + step) % seqs
                for d in range(columns):
                    pairs.append((b * columns + d, (d * seqs + row) * columns + b % groups))
            piece = lax.dynamic_index_in_dim(part, lax.rem(mine + step, seqs), 0, False)
            qkv = qkv + lax.ppermute(piece, ("blk", "dp"), pairs).astype(F32)
    else:
        reduced = lambda array: halved(halved(array, "dp", 0), "blk", 0)
        ffn_in_rows = reduced(in_chunks)
        chunks = [out_chunks, cross_out_chunks, key_chunks, value_chunks]
        chunks += [cross_q_chunks, self_out_chunks, part]
        counts = [out_chunks.shape[2]] + [unit] * 8
        rows = placed(reduced(jnp.concatenate(chunks, axis=2)), counts)
        ffn_out_own, cross_out_own, key_own, value_own, cross_q_own, self_out_own = rows[:6]
        qkv = jnp.stack(rows[6:])

    return (
        output,
        dec_grad,
        enc_grad,
        gain_grads,
        qkv,
        self_out_own,
        cross_q_own,
        jnp.stack([key_own, value_own]),
        cross_out_own,
        ffn_in_rows.astype(F32),
        ffn_out_own,
    )


def solution(mesh):
    placed = (
        P("blk", "dp", None),
        P("dp", "blk", None),
        P("dp", None),
        P(),
        P(),
        P(),
        P(),
        P(),
        P(),
        P(),
        P(),
        P("blk", "dp", None),
    )
    return jax.shard_map(
        body,
        mesh=mesh,
        in_specs=placed,
        out_specs=(
            P("blk", "dp", None),
            P("blk", "dp", None),
            P("dp", "blk", None),
            P(),
            P(None, "blk", "dp"),
            P("blk", "dp"),
            P("blk", "dp"),
            P(None, "blk", "dp"),
            P("blk", "dp"),
            P("blk", "dp"),
            P("blk", "dp"),
        ),
        check_vma=False,
    )
```

time: 1090 us -> 515 us (0.47)
  waiting for transfers between devices: 655 us -> 141 us
  matrix products: 98.5 us -> 19.3 us
  blocking collectives: 75.3 us -> 0 us
  Pallas kernels: 95 us -> 169 us
  starting transfers between devices: 35.9 us -> 71.8 us
    reduce_scatter x8 -> x2, waiting for transfers between devices: 493 us -> 0.01 us  [the longest x1 0.01 us: body(): lax.psum_scatter(chunks.reshape(-1, width), 'dp', scatter_dimension=0, ti...]
    dot_general x36 -> x15, matrix products: 98.5 us -> 19.3 us  [dot(): lax.dot_general(left, right, (((left_dim,), (right_dim,)), ((), ())), pre...]
    pallas_call x1 -> x11, Pallas kernels: 8.68 us -> 81.4 us  [the longest x1 17 us: token_stage(): pl.pallas_call(kernel, grid=(steps,), in_specs=[whole(*parts.shape), whol...]
    ppermute x1 -> x19, waiting for transfers between devices: 0.01 us -> 61.1 us  [the longest x4 38.4 us: send_back(): moved = lax.ppermute(piece, 'blk', [(b, a) for a, b in shifted(step)])]
    unnamed x20 -> x2, waiting for transfers between devices: 60.7 us -> 0.03 us
    psum x1 -> x0, blocking collectives: 39.4 us -> none  [body(): lax.psum(jnp.stack([gain_one, gain_two, gain_three]), ('blk', 'dp'))]
    all_to_all x2 -> x0, blocking collectives: 36 us -> none  [the longest x1 25.4 us: spread(): lax.all_to_all(jnp.broadcast_to(array[None], (groups,) + array.shape), 'b...]
    all_to_all x2 -> x1, waiting for transfers between devices: 30.2 us -> 0.01 us  [spread(): lax.all_to_all(jnp.broadcast_to(array[None], (groups,) + array.shape), 'b...]
  transfers between devices with their start and end apart: 25 -> 35, of which waited for: 18 -> 14; matrix products, arithmetic and copies ran while one was open for 13% -> 18% of each run, Pallas kernels for 2% -> 23%
where the time goes in v2:
time: 515 us; the launch traced here: 508 us
  Pallas kernels  169 us (33%)
  waiting for transfers between devices  141 us (27%)
  starting transfers between devices  71.8 us (14%)
  local copies, waits for them, and re-layouts  60.2 us (12%)
  other arithmetic  30.7 us (6%)
  matrix products  19.3 us (4%)
  between operations  15.3 us (3%)
    pallas_call x1, Pallas kernels, cross_backward(): pl.pallas_call(kernel, grid=(heads // pair,), in_specs=[pl.BlockSpec((siz...  49.7 us
    all_to_all x6, waiting for transfers between devices, traded(): return lax.all_to_all(array, 'blk', 0, 0, axis_index_groups=members)  39 us
    ppermute x4, waiting for transfers between devices, send_back(): moved = lax.ppermute(piece, 'blk', [(b, a) for a, b in shifted(step)])  38.4 us
    ppermute x4, waiting for transfers between devices, exchange(): lax.ppermute(pieces(lax.rem(mine + step, seqs)), 'blk', shifted(step))  28.4 us
    pallas_call x1, Pallas kernels, cross_forward(): pl.pallas_call(kernel, grid=(heads,), in_specs=[pl.BlockSpec((HEAD_DIM, l...  28.4 us
    unnamed x114, local copies, waits for them, and re-layouts  26.2 us
    all_to_all x6, starting transfers between devices, traded(): return lax.all_to_all(array, 'blk', 0, 0, axis_index_groups=members)  24.8 us
    dot_general x15, matrix products, dot(): lax.dot_general(left, right, (((left_dim,), (right_dim,)), ((), ())), pre...  19.3 us
  transfers between devices with their start and end apart: 35, of which 14 were waited for; matrix products, arithmetic and copies ran while one was open for 18% of the time, Pallas kernels for 23%

profile of v2, /device:TPU:0, one launch (start us, length us, event | category | flops | bytes accessed | tf_op | source)
XLA Modules:
  0.0 507.6 jit_solution(12307832256882306211)
XLA Ops:
  12.4 9.1 %collective-permute-done = bf16[128,768]{1,0:T(8,128)(2,1)S(1)} collective-permute-done((bf16[128,768]{1,0:T(8,128)(2,1)S(1)}, bf16[128,768]{1,0:T(8,128)(2,1)S(1)}, u32[]{:S(2)}, u32[]{:S(2)}) %collective-permute-start) | collective-permute-done | bytes 196640 | tf_op jit(solution)/shard_map/ppermute | solution.py:854
  38.1 5.6 %project_rows.3.refs_1_.refs_4_ = bf16[2,768,896]{2,1,0:T(8,128)(2,1)} custom-call(bf16[896,768]{1,0:T(8,128)(2,1)} %dynamic-slice_bitcast_fusion.1.refs_0_, bf16[2,768,768]{2,1,0:T(8,128)(2,1)} %bitcast.170), custom_call_target="tpu_custom_call" | custom-call | flops 2 | bytes 1 | tf_op jit(solution)/shard_map/project_rows/pallas_call | solution.py:355
  61.1 11.9 %self_forward.1 = (bf16[1024,768]{1,0:T(8,128)(2,1)}, bf16[3,192,1024]{2,1,0:T(8,128)(2,1)}, bf16[4,192,1024]{2,1,0:T(8,128)(2,1)}, bf16[3,1024,1024]{2,1,0:T(8,128)(2,1)}, f32[3,1,1024]{2,1,0:T(1,128)}) custom-call(bf16[1024,768]{1,0:T(8,128)(2,1)} %bitcast.174, f32[1,768]{1,0:T(1,128)} %get-tuple-element.273.g_ref, bf16[3,192,768]{2,1,0:T(8,128)(2,1)} %bitcast.182, ...), custom_call_target="tpu_custom_call" | custom-call | flops 3 | bytes 1 | tf_op jit(solution)/shard_map/self_forward/pallas_call | solution.py:310
  89.6 19.4 %all-to-all-done.1 = bf16[4,192,1024]{2,1,0:T(8,128)(2,1)S(1)} async-done(((bf16[4,192,1024]{2,1,0:T(8,128)(2,1)}), bf16[4,192,1024]{2,1,0:T(8,128)(2,1)S(1)}, u32[]{:S(2)}, u32[]{:S(2)}) %all-to-all-start.1) | async-done | bytes 1572896 | tf_op jit(solution)/shard_map/all_to_all | solution.py:877
  110.1 8.1 %query_stage.1 = (bf16[768,1024]{1,0:T(8,128)(2,1)}, f32[256,768]{1,0:T(8,128)}, bf16[256,768]{1,0:T(8,128)(2,1)}) custom-call(s32[1]{0:T(128)} %bitcast.s_ref, bf16[1024,768]{1,0:T(8,128)(2,1)} %bitcast.175, bf16[768,1024]{1,0:T(8,128)(2,1)} %bitcast.184, bf16[768,768]{1,0:T(8,128)(2,1)} %w_ref.4, f32[1,768]{1,0:T(1,128)} %get-tuple-element.272.g_ref, ...), custom_call_target="tpu_custom_call" | custom-call | flops 4 | bytes 1 | tf_op jit(solution)/shard_map/query_stage/pallas_call | solution.py:387
  123.6 28.4 %cross_forward.1 = (bf16[4,800,256]{2,1,0:T(8,128)(2,1)}, bf16[12,1792,1024]{2,1,0:T(8,128)(2,1)}, f32[12,1,1024]{2,1,0:T(1,128)}) custom-call(bf16[768,1024]{1,0:T(8,128)(2,1)} %get-tuple-element.94.refs_0_, bf16[2,768,896]{2,1,0:T(8,128)(2,1)} %project_rows.3.refs_1_.refs_4_, bf16[2,768,384]{2,1,0:T(8,128)(2,1)} %project_rows.4.refs_2_.refs_5_, ...), custom_call_target="tpu_custom_call" | custom-call | flops 22 | bytes 1 | tf_op jit(solution)/shard_map/cross_forward/pallas_call | solution.py:174
  157.6 19.3 %collective-permute-done.4 = bf16[128,768]{1,0:T(8,128)(2,1)S(1)} collective-permute-done((bf16[128,768]{1,0:T(8,128)(2,1)S(1)}, bf16[128,768]{1,0:T(8,128)(2,1)S(1)}, u32[]{:S(2)}, u32[]{:S(2)}) %collective-permute-start.4) | collective-permute-done | bytes 196640 | tf_op jit(solution)/shard_map/ppermute | solution.py:854
  180.3 17.0 %token_stage.1 = (bf16[256,768]{1,0:T(8,128)(2,1)}, f32[256,768]{1,0:T(8,128)}, bf16[256,768]{1,0:T(8,128)(2,1)}, bf16[256,768]{1,0:T(8,128)(2,1)}, bf16[256,307...) custom-call(bf16[4,800,256]{2,1,0:T(8,128)(2,1)} %copy-done.11, ...), custom_call_target="tpu_custom_call" | custom-call | flops 4 | bytes 1 | tf_op jit(solution)/shard_map/token_stage/pallas_call | solution.py:513
  201.2 9.4 %hidden_weight_grads.1 = (bf16[4,8,96,768]{3,2,1,0:T(8,128)(2,1)}, bf16[4,8,96,768]{3,2,1,0:T(8,128)(2,1)}) custom-call(bf16[256,768]{1,0:T(8,128)(2,1)} %get-tuple-element.103.a_ref, bf16[256,3072]{1,0:T(8,128)(2,1)} %get-tuple-element.104.du_ref, bf16[256,3072]{1,0:T(8,128)(2,1)} %get-tuple-element.105.z_ref, bf16[256,768]{1,0:T(8,128)(2,1)} %pad_maximum_fusion.5.c_ref), custom_call_target="tpu_custom_call" | custom-call | flops 2 | bytes 1 | tf_op jit(solution)/shard_map/hidden_weight_grads/pallas_call | solution.py:575
  210.6 7.6 %pad_maximum_fusion = bf16[4,8,192,768]{3,2,1,0:T(8,128)(2,1)} fusion(bf16[4,8,96,768]{3,2,1,0:T(8,128)(2,1)} %get-tuple-element.107, bf16[4,8,96,768]{3,2,1,0:T(8,128)(2,1)} %get-tuple-element.106), kind=kLoop, calls=%fused_computation | loop fusion | flops 18874368 | bytes 18874368 | tf_op jit(solution)/shard_map/concatenate | solution.py:1008
  228.2 49.7 %cross_backward.1 = (bf16[4,768,256]{2,1,0:T(8,128)(2,1)}, bf16[896,768]{1,0:T(8,128)(2,1)}, bf16[384,768]{1,0:T(8,128)(2,1)}, bf16[512,768]{1,0:T(8,128)(2,1)},...) custom-call(bf16[768,1024]{1,0:T(8,128)(2,1)} %get-tuple-element.94.refs_0_, ...), custom_call_target="tpu_custom_call" | custom-call | flops 45 | bytes 1 | tf_op jit(solution)/shard_map/cross_backward/pallas_call | solution.py:254
  279.7 4.8 all-to-all-start.4
  296.6 15.5 %all-to-all-done.4.r_ref = bf16[4,768,256]{2,1,0:T(8,128)(2,1)} async-done(((bf16[4,768,256]{2,1,0:T(8,128)(2,1)}), bf16[4,768,256]{2,1,0:T(8,128)(2,1)}, u32[]{:S(2)}, u32[]{:S(2)}) %all-to-all-start.4) | async-done | bytes 1572896 | tf_op jit(solution)/shard_map/all_to_all | solution.py:877
  312.1 4.9 mixed_stage.1
  326.6 9.5 %collective-permute-done.7.refs_1_ = bf16[128,768]{1,0:T(8,128)(2,1)} collective-permute-done((bf16[128,768]{1,0:T(8,128)(2,1)S(1)}, bf16[128,768]{1,0:T(8,128)(2,1)}, u32[]{:S(2)}, u32[]{:S(2)}) %collective-permute-start.7) | collective-permute-done | bytes 196640 | tf_op jit(solution)/shard_map/ppermute | solution.py:1054
  350.0 9.7 %self_backward.1.d_ref = bf16[4,3,192,256]{3,2,1,0:T(8,128)(2,1)} custom-call(bf16[3,192,1024]{2,1,0:T(8,128)(2,1)} %get-tuple-element.115.q_ref.k_ref.v_ref, bf16[3,192,1024]{2,1,0:T(8,128)(2,1)} %get-tuple-element.115.q_ref.k_ref.v_ref, bf16[3,192,1024]{2,1,0:T(8,128)(2,1)} %get-tuple-element.115.q_ref.k_ref.v_ref, ...), custom_call_target="tpu_custom_call" | custom-call | flops 6 | bytes 1 | tf_op jit(solution)/shard_map/self_backward/pallas_call | solution.py:793
  359.7 9.6 %collective-permute-done.9.refs_2_ = bf16[128,768]{1,0:T(8,128)(2,1)} collective-permute-done((bf16[128,768]{1,0:T(8,128)(2,1)}, bf16[128,768]{1,0:T(8,128)(2,1)}, u32[]{:S(2)}, u32[]{:S(2)}) %collective-permute-start.9) | collective-permute-done | bytes 196640 | tf_op jit(solution)/shard_map/ppermute | solution.py:1054
  390.3 7.1 %own_weight_grads.1 = (bf16[8,3,96,192]{3,2,1,0:T(8,128)(2,1)}, f32[1,768]{1,0:T(1,128)}) custom-call(bf16[1024,768]{1,0:T(8,128)(2,1)} %get-tuple-element.147.a_ref, bf16[1024,768]{1,0:T(8,128)(2,1)} %bitcast.177, bf16[4,3,192,256]{3,2,1,0:T(8,128)(2,1)} %self_backward.1.d_ref, bf16[3,192,768]{2,1,0:T(8,128)(2,1)} %bitcast.183), custom_call_target="tpu_custom_call" | custom-call | flops 1 | bytes 1 | tf_op jit(solution)/shard_map/own_weight_grads/pallas_call | solution.py:745
  397.4 19.2 %collective-permute-done.12.refs_3_ = bf16[384,768]{1,0:T(8,128)(2,1)} collective-permute-done((bf16[384,768]{1,0:T(8,128)(2,1)}, bf16[384,768]{1,0:T(8,128)(2,1)}, u32[]{:S(2)}, u32[]{:S(2)}) %collective-permute-start.12) | collective-permute-done | bytes 589856 | tf_op jit(solution)/shard_map/ppermute | solution.py:1054
  417.6 5.5 %input_stage.1 = bf16[256,768]{1,0:T(8,128)(2,1)} custom-call(bf16[4,3,192,256]{3,2,1,0:T(8,128)(2,1)} %all-to-all-done.6.b_ref, bf16[3,768,768]{2,1,0:T(8,128)(2,1)} %w_ref.5, bf16[256,768]{1,0:T(8,128)(2,1)} %constant_dynamic-slice_fusion.2.x_ref, f32[1,768]{1,0:T(1,128)} %get-tuple-element.273.g_ref, f32[256,768]{1,0:T(8,128)} %get-tuple-element.156.h_ref), custom_call_target="tpu_custom_call" | custom-call | flops 1 | bytes 1 | tf_op jit(solution)/shard_map/input_stage/pallas_call | solution.py:663
  433.4 5.2 %collective-permute-start.20 = (bf16[4,72,768]{2,1,0:T(8,128)(2,1)S(1)}, bf16[4,72,768]{2,1,0:T(8,128)(2,1)}, u32[]{:S(2)}, u32[]{:S(2)}) collective-permute-start(bf16[4,72,768]{2,1,0:T(8,128)(2,1)S(1)} %dynamic-slice_bitcast_fusion.6), channel_id=1, source_target_pairs={{0,4},{4,0},{8,12},{12,8},{16,20},{20,16},{24,28},{28,24},{1,5},{5... | collective-permute-start | bytes 1327112 | tf_op jit(solution)/shard_map/ppermute | solution.py:56
  447.8 7.0 %all-to-all-done.8 = f32[8,3,768]{2,1,0:T(4,128)S(1)} async-done(((f32[8,3,768]{2,1,0:T(4,128)}), f32[8,3,768]{2,1,0:T(4,128)S(1)}, u32[]{:S(2)}, u32[]{:S(2)}) %all-to-all-start.8) | async-done | bytes 73760 | tf_op jit(solution)/shard_map/all_to_all | solution.py:81
  468.8 14.6 %collective-permute-done.22 = bf16[1,120,768]{2,1,0:T(8,128)(2,1)S(1)} collective-permute-done((bf16[1,120,768]{2,1,0:T(8,128)(2,1)S(1)}, bf16[1,120,768]{2,1,0:T(8,128)(2,1)S(1)}, u32[]{:S(2)}, u32[]{:S(2)}) %collective-permute-start.22) | collective-permute-done | bytes 184352 | tf_op jit(solution)/shard_map/ppermute | solution.py:73
  490.0 5.5 %all-to-all-done.9 = bf16[4,216,192]{1,2,0:T(8,128)(2,1)S(1)} async-done(((bf16[4,216,192]{1,2,0:T(8,128)(2,1)}), bf16[4,216,192]{1,2,0:T(8,128)(2,1)S(1)}, u32[]{:S(2)}, u32[]{:S(2)}) %all-to-all-start.9) | async-done | bytes 331808 | tf_op jit(solution)/shard_map/all_to_all | solution.py:991
  (289 shorter events, 188.5 us)
Async XLA Ops:
  22.8 37.1 %all-to-all-start = ((bf16[4,256,768]{2,1,0:T(8,128)(2,1)}), bf16[4,256,768]{2,1,0:T(8,128)(2,1)S(1)}, u32[]{:S(2)}, u32[]{:S(2)}) async-start(bf16[4,256,768]{2,1,0:T(8,128)(2,1)} %broadcast_in_dim.105), calls=%async_computation | async-start | bytes 3145728 | tf_op jit(solution)/shard_map/all_to_all | solution.py:868
  28.6 27.3 %collective-permute-start.1 = (bf16[384,768]{1,0:T(8,128)(2,1)S(1)}, bf16[384,768]{1,0:T(8,128)(2,1)S(1)}, u32[]{:S(2)}, u32[]{:S(2)}) collective-permute-start(bf16[384,768]{1,0:T(8,128)(2,1)S(1)} %get-tuple-element.245), channel_id=1, source_target_pairs={{0,16},{4,20},{8,24},{12,28},{16,0},{20,4},{24,8},{28,12},{1,17},{... | collective-permute-start | bytes 1769480 | tf_op jit(solution)/shard_map/ppermute | solution.py:901
  73.6 35.3 %all-to-all-start.1 = ((bf16[4,192,1024]{2,1,0:T(8,128)(2,1)}), bf16[4,192,1024]{2,1,0:T(8,128)(2,1)S(1)}, u32[]{:S(2)}, u32[]{:S(2)}) async-start(bf16[4,192,1024]{2,1,0:T(8,128)(2,1)} %get-tuple-element.91.o_ref), calls=%async_computation.1 | async-start | bytes 3145728 | tf_op jit(solution)/shard_map/all_to_all | solution.py:877
  78.7 39.6 %collective-permute-start.3 = (bf16[384,768]{1,0:T(8,128)(2,1)}, bf16[384,768]{1,0:T(8,128)(2,1)S(1)}, u32[]{:S(2)}, u32[]{:S(2)}) collective-permute-start(bf16[384,768]{1,0:T(8,128)(2,1)} %get-tuple-element.93), channel_id=1, source_target_pairs={{0,16},{4,20},{8,24},{12,28},{16,0},{20,4},{24,8},{28,12},{1,17},{... | collective-permute-start | bytes 1769480 | tf_op jit(solution)/shard_map/ppermute | solution.py:905
  152.0 27.1 %all-to-all-start.2 = ((bf16[4,800,256]{2,1,0:T(8,128)(2,1)}), bf16[4,800,256]{2,1,0:T(8,128)(2,1)S(1)}, u32[]{:S(2)}, u32[]{:S(2)}) async-start(bf16[4,800,256]{2,1,0:T(8,128)(2,1)} %get-tuple-element.100), calls=%async_computation.2 | async-start | bytes 3276800 | tf_op jit(solution)/shard_map/all_to_all | solution.py:877
  155.8 21.1 %collective-permute-start.4 = (bf16[128,768]{1,0:T(8,128)(2,1)S(1)}, bf16[128,768]{1,0:T(8,128)(2,1)S(1)}, u32[]{:S(2)}, u32[]{:S(2)}) collective-permute-start(bf16[128,768]{1,0:T(8,128)(2,1)S(1)} %dynamic-slice_bitcast_fusion.13), channel_id=1, source_target_pairs={{0,16},{4,20},{8,24},{12,28},{16,0},{20,4},{24,8},{28,12},{1,17},{... | collective-permute-start | bytes 589832 | tf_op jit(solution)/shard_map/ppermute | solution.py:854
  197.3 23.7 %all-to-all-start.3 = ((bf16[4,832,256]{2,1,0:T(8,128)(2,1)}), bf16[4,832,256]{2,1,0:T(8,128)(2,1)S(1)}, u32[]{:S(2)}, u32[]{:S(2)}) async-start(bf16[4,832,256]{2,1,0:T(8,128)(2,1)} %get-tuple-element.102), calls=%async_computation.3 | async-start | bytes 3407872 | tf_op jit(solution)/shard_map/all_to_all | solution.py:877
  200.9 111.2 %reduce-scatter.3.cloned.1.call-start = ((), (), s32[]{:S(2)}) async-start(), calls=%async_computation.12 | async-start | bytes 11796480 | tf_op jit(solution)/shard_map/reduce_scatter | solution.py:1011
  226.4 53.3 %collective-permute-start.5 = (bf16[128,768]{1,0:T(8,128)(2,1)S(1)}, bf16[128,768]{1,0:T(8,128)(2,1)}, u32[]{:S(2)}, u32[]{:S(2)}) collective-permute-start(bf16[128,768]{1,0:T(8,128)(2,1)S(1)} %get-tuple-element.261), channel_id=1, source_target_pairs={{0,16},{4,20},{8,24},{12,28},{16,0},{20,4},{24,8},{28,12},{1,17},{... | collective-permute-start | bytes 589832 | tf_op jit(solution)/shard_map/ppermute | solution.py:854
  279.7 32.4 %all-to-all-start.4 = ((bf16[4,768,256]{2,1,0:T(8,128)(2,1)}), bf16[4,768,256]{2,1,0:T(8,128)(2,1)}, u32[]{:S(2)}, u32[]{:S(2)}) async-start(bf16[4,768,256]{2,1,0:T(8,128)(2,1)} %get-tuple-element.116), calls=%async_computation.4 | async-start | bytes 3145728 | tf_op jit(solution)/shard_map/all_to_all | solution.py:877
  291.3 20.8 %collective-permute-start.6 = (bf16[256,768]{1,0:T(8,128)(2,1)S(1)}, bf16[256,768]{1,0:T(8,128)(2,1)S(1)}, u32[]{:S(2)}, u32[]{:S(2)}) collective-permute-start(bf16[256,768]{1,0:T(8,128)(2,1)S(1)} %slice.120), channel_id=1, source_target_pairs={{16,0},{20,4},{24,8},{28,12},{0,16},{4,20},{8,24},{12,28},{17,1},{... | collective-permute-start | bytes 1179656 | tf_op jit(solution)/shard_map/ppermute | solution.py:1054
  320.6 140.3 %reduce-scatter.5.cloned.1.call-start = ((), (), s32[]{:S(2)}) async-start(), calls=%async_computation.13 | async-start | bytes 2654208 | tf_op jit(solution)/shard_map/reduce_scatter | solution.py:1072
  340.4 29.0 %collective-permute-start.11 = (bf16[2,8,72,768]{3,2,1,0:T(8,128)(2,1)}, bf16[2,8,72,768]{3,2,1,0:T(8,128)(2,1)}, u32[]{:S(2)}, u32[]{:S(2)}) collective-permute-start(bf16[2,8,72,768]{3,2,1,0:T(8,128)(2,1)} %dynamic-slice_bitcast_fusion), channel_id=1, source_target_pairs={{0,1},{1,0},{2,3},{3,2},{4,5},{5,4},{6,7},{7,6},{8,9},{9,8},{10,11... | collective-permute-start | bytes 5308424 | tf_op jit(solution)/shard_map/ppermute | solution.py:56
  343.4 25.9 %collective-permute-start.10 = (bf16[1,8,48,768]{3,2,1,0:T(8,128)(2,1)}, bf16[1,8,48,768]{3,2,1,0:T(8,128)(2,1)}, u32[]{:S(2)}, u32[]{:S(2)}) collective-permute-start(bf16[1,8,48,768]{3,2,1,0:T(8,128)(2,1)} %constant_dynamic-slice_fusion.4), channel_id=1, source_target_pairs={{0,2},{1,3},{2,0},{3,1},{4,6},{5,7},{6,4},{7,5},{8,10},{9,11},{10,... | collective-permute-start | bytes 1769480 | tf_op jit(solution)/shard_map/ppermute | solution.py:56
  348.2 21.2 %collective-permute-start.9 = (bf16[128,768]{1,0:T(8,128)(2,1)}, bf16[128,768]{1,0:T(8,128)(2,1)}, u32[]{:S(2)}, u32[]{:S(2)}) collective-permute-start(bf16[128,768]{1,0:T(8,128)(2,1)} %slice.122), channel_id=1, source_target_pairs={{16,0},{20,4},{24,8},{28,12},{0,16},{4,20},{8,24},{12,28},{17,1},{... | collective-permute-start | bytes 589832 | tf_op jit(solution)/shard_map/ppermute | solution.py:1054
  369.4 47.2 %all-to-all-start.6 = ((bf16[4,3,192,256]{3,2,1,0:T(8,128)(2,1)}), bf16[4,3,192,256]{3,2,1,0:T(8,128)(2,1)}, u32[]{:S(2)}, u32[]{:S(2)}) async-start(bf16[4,3,192,256]{3,2,1,0:T(8,128)(2,1)} %self_backward.1.d_ref), calls=%async_computation.7 | async-start | bytes 2359296 | tf_op jit(solution)/shard_map/all_to_all | solution.py:877
  378.9 37.8 %collective-permute-start.14 = (bf16[1,8,72,768]{3,2,1,0:T(8,128)(2,1)S(1)}, bf16[1,8,72,768]{3,2,1,0:T(8,128)(2,1)S(1)}, u32[]{:S(2)}, u32[]{:S(2)}) collective-permute-start(bf16[1,8,72,768]{3,2,1,0:T(8,128)(2,1)S(1)} %constant_dynamic-slice_fusion.3), channel_id=1, source_target_pairs={{0,2},{1,3},{2,0},{3,1},{4,6},{5,7},{6,4},{7,5},{8,10},{9,11},{10,... | collective-permute-start | bytes 2654216 | tf_op jit(solution)/shard_map/ppermute | solution.py:56
  384.1 32.5 %collective-permute-start.12 = (bf16[384,768]{1,0:T(8,128)(2,1)}, bf16[384,768]{1,0:T(8,128)(2,1)}, u32[]{:S(2)}, u32[]{:S(2)}) collective-permute-start(bf16[384,768]{1,0:T(8,128)(2,1)} %slice.123), channel_id=1, source_target_pairs={{16,0},{20,4},{24,8},{28,12},{0,16},{4,20},{8,24},{12,28},{17,1},{... | collective-permute-start | bytes 1769480 | tf_op jit(solution)/shard_map/ppermute | solution.py:1054
  386.0 30.6 %collective-permute-start.13 = (bf16[4,48,768]{2,1,0:T(8,128)(2,1)S(1)}, bf16[4,48,768]{2,1,0:T(8,128)(2,1)S(1)}, u32[]{:S(2)}, u32[]{:S(2)}) collective-permute-start(bf16[4,48,768]{2,1,0:T(8,128)(2,1)S(1)} %dynamic-slice_bitcast_fusion.8), channel_id=1, source_target_pairs={{0,4},{4,0},{8,12},{12,8},{16,20},{20,16},{24,28},{28,24},{1,5},{5... | collective-permute-start | bytes 884744 | tf_op jit(solution)/shard_map/ppermute | solution.py:56
  424.8 30.7 %collective-permute-start.15 = (bf16[128,768]{1,0:T(8,128)(2,1)}, bf16[128,768]{1,0:T(8,128)(2,1)}, u32[]{:S(2)}, u32[]{:S(2)}) collective-permute-start(bf16[128,768]{1,0:T(8,128)(2,1)} %dynamic-slice_bitcast_fusion.10), channel_id=1, source_target_pairs={{0,16},{4,20},{8,24},{12,28},{16,0},{20,4},{24,8},{28,12},{1,17},{... | collective-permute-start | bytes 589832 | tf_op jit(solution)/shard_map/ppermute | solution.py:854
  431.5 26.4 %collective-permute-start.16 = (bf16[2,2,3,96,192]{4,3,2,1,0:T(8,128)(2,1)}, bf16[2,2,3,96,192]{4,3,2,1,0:T(8,128)(2,1)}, u32[]{:S(2)}, u32[]{:S(2)}) collective-permute-start(bf16[2,2,3,96,192]{4,3,2,1,0:T(8,128)(2,1)} %dynamic-slice_bitcast_fusion.5), channel_id=1, source_target_pairs={{0,1},{1,0},{2,3},{3,2},{4,5},{5,4},{6,7},{7,6},{8,9},{9,8},{10,11... | collective-permute-start | bytes 1327112 | tf_op jit(solution)/shard_map/ppermute | solution.py:73
  433.4 23.1 %collective-permute-start.20 = (bf16[4,72,768]{2,1,0:T(8,128)(2,1)S(1)}, bf16[4,72,768]{2,1,0:T(8,128)(2,1)}, u32[]{:S(2)}, u32[]{:S(2)}) collective-permute-start(bf16[4,72,768]{2,1,0:T(8,128)(2,1)S(1)} %dynamic-slice_bitcast_fusion.6), channel_id=1, source_target_pairs={{0,4},{4,0},{8,12},{12,8},{16,20},{20,16},{24,28},{28,24},{1,5},{5... | collective-permute-start | bytes 1327112 | tf_op jit(solution)/shard_map/ppermute | solution.py:56
  467.7 21.6 %collective-permute-start.19 = (bf16[3,96,192]{2,1,0:T(8,128)(2,1)S(1)}, bf16[3,96,192]{2,1,0:T(8,128)(2,1)S(1)}, u32[]{:S(2)}, u32[]{:S(2)}) collective-permute-start(bf16[3,96,192]{2,1,0:T(8,128)(2,1)S(1)} %get-tuple-element.266), channel_id=1, source_target_pairs={{0,4},{1,12},{2,20},{3,28},{4,5},{5,13},{6,21},{7,29},{8,6},{9,14}... | collective-permute-start | bytes 331784 | tf_op jit(solution)/shard_map/ppermute | solution.py:1152
  468.2 21.1 %collective-permute-start.18 = (bf16[3,96,192]{2,1,0:T(8,128)(2,1)S(1)}, bf16[3,96,192]{2,1,0:T(8,128)(2,1)S(1)}, u32[]{:S(2)}, u32[]{:S(2)}) collective-permute-start(bf16[3,96,192]{2,1,0:T(8,128)(2,1)S(1)} %get-tuple-element.265), channel_id=1, source_target_pairs={{0,0},{1,8},{2,16},{3,24},{4,1},{5,9},{6,17},{7,25},{8,2},{9,10},{... | collective-permute-start | bytes 331784 | tf_op jit(solution)/shard_map/ppermute | solution.py:1152
  (64 other events, 495.1 us)
Sparse Core Ops, SparseCore 0:
  221.2 77.0 reduce-scatter.2
  340.5 85.7 reduce-scatter.4

commit v3 on v2

--- a/solution.py
+++ b/solution.py
@@ -47,24 +47,179 @@
     return (kept.astype(F32) + got.astype(F32)).astype(BF16)
 
 
-class Halving:
-    def __init__(self, array):
-        self.array = array
-
-    def send(self, axis, dim):
-        self.kept, sent, pairs = parted(self.array, axis, dim)
-        self.got = lax.ppermute(sent, axis, pairs)
-
-    def take(self):
-        self.array = added(self.kept, self.got)
-
-
-def after(value, *halvings):
-    value, got = lax.optimization_barrier((value, [h.got for h in halvings]))
-    for halving, piece in zip(halvings, got):
-        halving.got = piece
-        halving.take()
-    return value
+def fold(pairs, bit, low):
+    count, _, width = pairs[0][0].shape
+    rows = [k.shape[1] for k, _ in pairs]
+    high, total = count // 2 // low, sum(rows)
+
+    def kernel(s_ref, *refs):
+        start = 0
+        for i, size in enumerate(rows):
+            for side in range(2):
+                kept, got = refs[4 * i + 2 * side], refs[4 * i + 2 * side + 1]
+                both = kept[...].astype(F32) + got[...].astype(F32)
+                refs[4 * len(rows) + side][:, start : start + size, :] = both.reshape(
+                    high * low, size, width
+                ).astype(BF16)
+            start += size
+
+    def spec(size, side):
+        return pl.BlockSpec(
+            (high, 1, low, size, width), lambda j, s: (0, (s[0] + side) % 2, 0, 0, 0)
+        )
+
+    split = lambda array: array.reshape(high, 2, low, array.shape[1], width)
+    out = pl.BlockSpec((high * low, total, width), lambda j, s: (0, 0, 0))
+    return pl.pallas_call(
+        kernel,
+        grid_spec=pltpu.PrefetchScalarGridSpec(
+            num_scalar_prefetch=1,
+            grid=(1,),
+            in_specs=[spec(size, side) for size in rows for side in range(2) for _ in range(2)],
+            out_specs=[out] * 2,
+        ),
+        out_shape=[jax.ShapeDtypeStruct((high * low, total, width), BF16)] * 2,
+        compiler_params=params(),
+        cost_estimate=estimate(flops=0, bytes_accessed=0, transcendentals=0),
+        name="fold",
+    )(bit, *[split(array) for k, g in pairs for array in (k, g, k, g)])
+
+
+def evens(array, bit, sizes):
+    count, rows, width = array.shape
+    half = count // 2
+
+    def kernel(s_ref, here_ref, there_ref, *out_refs):
+        start = 0
+        for i, size in enumerate(sizes):
+            for side, ref in enumerate((here_ref, there_ref)):
+                out_refs[2 * i + side][...] = ref[:, 0, start : start + size]
+            start += size
+
+    spec = lambda side: pl.BlockSpec(
+        (half, 1, rows, width), lambda j, s: (0, (s[0] + side) % 2, 0, 0)
+    )
+    out = lambda size: pl.BlockSpec((half, size, width), lambda j, s: (0, 0, 0))
+    split = array.reshape(half, 2, rows, width)
+    outs = pl.pallas_call(
+        kernel,
+        grid_spec=pltpu.PrefetchScalarGridSpec(
+            num_scalar_prefetch=1,
+            grid=(1,),
+            in_specs=[spec(0), spec(1)],
+            out_specs=[out(size) for size in sizes for _ in range(2)],
+        ),
+        out_shape=[
+            jax.ShapeDtypeStruct((half, size, width), BF16) for size in sizes for _ in range(2)
+        ],
+        compiler_params=params(),
+        cost_estimate=estimate(flops=0, bytes_accessed=0, transcendentals=0),
+        name="evens",
+    )(bit, split, split)
+    return list(zip(outs[::2], outs[1::2]))
+
+
+def weight_chunks(kernel_dots, operands, specs, core, slot, columns, blocks, width):
+    number = len(kernel_dots)
+    size, piece = width // blocks, width // columns
+    rows = number // 2 * size + number % 2 * size // 2
+    shape = (columns // 2 * blocks, rows, 2 * piece)
+
+    def kernel(c_ref, n_ref, *refs):
+        kept_ref, sent_ref = refs[-2:]
+        grads = [one(refs[:-2]).astype(BF16) for one in kernel_dots]
+
+        def chunk(b, d):
+            cut = lambda g, start, stop: g[
+                b * size + start : b * size + stop, d * piece : (d + 1) * piece
+            ]
+            sides = [
+                jnp.concatenate([cut(g, 0, size), cut(h, 0, size)], axis=1)
+                for g, h in zip(grads[::2], grads[1::2])
+            ]
+            if number % 2:
+                g = grads[-1]
+                sides.append(
+                    jnp.concatenate([cut(g, 0, size // 2), cut(g, size // 2, size)], axis=1)
+                )
+            return sides[0] if len(sides) == 1 else jnp.concatenate(sides, axis=0)
+
+        for bit in range(2):
+
+            @pl.when(c_ref[0] == bit)
+            def put():
+                for b in range(blocks):
+                    for d in range(columns):
+                        ref = kept_ref if d % 2 == bit else sent_ref
+                        ref[d // 2 * blocks + b] = chunk(b, d)
+
+    whole = lambda *shape: pl.BlockSpec(shape, lambda i, c, n: (0,) * len(shape))
+    in_specs = [spec or whole(*array.shape) for array, spec in zip(operands, specs)]
+    return pl.pallas_call(
+        kernel,
+        grid_spec=pltpu.PrefetchScalarGridSpec(
+            num_scalar_prefetch=2,
+            grid=(1,),
+            in_specs=in_specs,
+            out_specs=[whole(*shape)] * 2,
+        ),
+        out_shape=[jax.ShapeDtypeStruct(shape, BF16)] * 2,
+        compiler_params=params(),
+        cost_estimate=estimate(flops=0, bytes_accessed=0, transcendentals=0),
+        name="weight_chunks",
+    )(core, slot, *operands)
+
+
+def row_grads(keys, values, weights, marks):
+    rows, width = keys.shape
+    sizes = [b - a for a, b in zip(marks, marks[1:])]
+
+    def kernel(k_ref, v_ref, w_ref, *out_refs):
+        total = dot(k_ref[...], w_ref[0], 1, 1) + dot(v_ref[...], w_ref[1], 1, 1)
+        for ref, start, size in zip(out_refs, marks, sizes):
+            ref[...] = total[start : start + size].astype(BF16)
+
+    return pl.pallas_call(
+        kernel,
+        out_shape=[jax.ShapeDtypeStruct((size, width), BF16) for size in sizes],
+        compiler_params=params(),
+        cost_estimate=estimate(flops=0, bytes_accessed=0, transcendentals=0),
+        name="row_grads",
+    )(keys, values, weights)
+
+
+def unpacked(hidden, late, size, piece):
+    half = size // 2
+
+    def kernel(hk_ref, hg_ref, lk_ref, lg_ref, in_ref, out_ref, kv_ref, co_ref, cq_ref, so_ref):
+        first = hk_ref[...].astype(F32) + hg_ref[...].astype(F32)
+        in_ref[...] = jnp.concatenate([first[:size], first[size : 2 * size]], axis=1)
+        turned = first[2 * size :].T
+        out_ref[...] = jnp.concatenate([turned[:piece], turned[piece:]], axis=1)
+        second = lk_ref[...].astype(F32) + lg_ref[...].astype(F32)
+        kv_ref[0] = second[:size, :piece]
+        kv_ref[1] = second[:size, piece:]
+        co_ref[:half, :] = second[size : size + half, :piece]
+        co_ref[half:, :] = second[size : size + half, piece:]
+        cq_ref[...] = second[size + half :, :piece]
+        so_ref[...] = second[size + half :, piece:]
+
+    flat = lambda *shape: jax.ShapeDtypeStruct(shape, F32)
+    outs = pl.pallas_call(
+        kernel,
+        out_shape=[
+            flat(size, 4 * piece),
+            flat(piece, 4 * size),
+            flat(2, size, piece),
+            flat(size, piece),
+            flat(size, piece),
+            flat(size, piece),
+        ],
+        compiler_params=params(),
+        cost_estimate=estimate(flops=0, bytes_accessed=0, transcendentals=0),
+        name="unpacked",
+    )(*hidden, *late)
+    return (outs[0], outs[1].T) + tuple(outs[2:])
 
 
 def halved(array, axis, dim):
@@ -74,12 +229,10 @@
     return jnp.squeeze(array, dim)
 
 
-def total_of(array):
-    for axis in ("dp", "blk"):
-        size = lax.axis_size(axis)
-        copies = jnp.broadcast_to(array[None], (size,) + array.shape)
-        array = jnp.sum(lax.all_to_all(copies, axis, 0, 0), axis=0)
-    return array
+def total_of(array, axis):
+    size = lax.axis_size(axis)
+    copies = jnp.broadcast_to(array[None], (size,) + array.shape)
+    return jnp.sum(lax.all_to_all(copies, axis, 0, 0), axis=0)
 
 
 def estimate(flops, bytes_accessed, transcendentals):
@@ -208,6 +361,8 @@
     starts = [sum(rows[:i]) for i in range(parts)]
     total = sum(rows)
     pair = 2
+    sources = [rows[0], total - rows[0]]
+    where = [(0, 0)] + [(1, start - rows[0]) for start in starts[1:]]
 
     def kernel(*refs):
         q_ref = refs[0]
@@ -215,8 +370,8 @@
         v_refs = refs[1 + parts : 1 + 2 * parts]
         p_ref, g_ref, w_ref, d_ref = refs[1 + 2 * parts : 5 + 2 * parts]
         dq_ref = refs[5 + 2 * parts]
-        dk_refs = refs[6 + 2 * parts : 6 + 3 * parts]
-        dv_refs = refs[6 + 3 * parts :]
+        dk_refs = refs[6 + 2 * parts : 8 + 2 * parts]
+        dv_refs = refs[8 + 2 * parts :]
         key_out = [[] for _ in range(parts)]
         value_out = [[] for _ in range(parts)]
         for j in range(pair):
@@ -244,13 +399,15 @@
             for g in range(groups):
                 dq_ref[g, at, :] = query_low[:, g * tokens : (g + 1) * tokens]
         for i in range(parts):
-            dk_refs[i][...] = jnp.concatenate(key_out[i], axis=1)
-            dv_refs[i][...] = jnp.concatenate(value_out[i], axis=1)
+            source, start = where[i]
+            at = slice(start, start + rows[i])
+            dk_refs[source][at, :] = jnp.concatenate(key_out[i], axis=1)
+            dv_refs[source][at, :] = jnp.concatenate(value_out[i], axis=1)
 
     size = pair * HEAD_DIM
     key_specs = [pl.BlockSpec((1, size, r), lambda h: (0, h, 0)) for r in rows]
     value_specs = [pl.BlockSpec((1, size, r), lambda h: (1, h, 0)) for r in rows]
-    kv_grads = [pl.BlockSpec((r, size), lambda h: (0, h)) for r in rows]
+    kv_grads = [pl.BlockSpec((r, size), lambda h: (0, h)) for r in sources]
     outs = pl.pallas_call(
         kernel,
         grid=(heads // pair,),
@@ -265,7 +422,7 @@
         ],
         out_specs=[pl.BlockSpec((groups, size, tokens), lambda h: (0, h, 0))] + kv_grads + kv_grads,
         out_shape=[jax.ShapeDtypeStruct((groups, width, tokens), BF16)]
-        + [jax.ShapeDtypeStruct((r, width), BF16) for r in rows] * 2,
+        + [jax.ShapeDtypeStruct((r, width), BF16) for r in sources] * 2,
         compiler_params=params(),
         cost_estimate=estimate(
             flops=32 * heads * total * length * HEAD_DIM,
@@ -274,7 +431,7 @@
         ),
         name="cross_backward",
     )(query, *pairs, *pairs, prob, grads, weight, delta)
-    return outs[0], list(outs[1 : 1 + parts]), list(outs[1 + parts :])
+    return outs[0], list(outs[1:3]), list(outs[3:5])
 
 
 def self_forward(inputs, gain, weights, key_pos, query_pos, groups):
@@ -559,36 +716,42 @@
 def hidden_weight_grads(low, pre_grad, act, cotangent, columns, blocks):
     tokens, width = low.shape
     hidden = act.shape[1]
-    piece = hidden // blocks
-    in_rows, out_rows = width // blocks, piece // columns
-    per = width // piece
-
-    def kernel(a_ref, du_ref, z_ref, c_ref, in_ref, out_ref):
+    step_size = hidden // blocks
+    size, piece = width // blocks, width // columns
+    half = step_size // 2
+
+    def kernel(a_ref, du_ref, z_ref, c_ref, out_ref):
+        step = pl.program_id(0)
         first = dot(a_ref[...], du_ref[...], 0, 0).astype(BF16)
-        for b in range(blocks):
-            in_ref[0, b] = first[b * in_rows : (b + 1) * in_rows]
+        for p in range(2):
+
+            @pl.when(lax.rem(step, 2) == p)
+            def put():
+                for b in range(blocks):
+                    out_ref[step // 2, b, p * size : (p + 1) * size, :] = first[
+                        b * size : (b + 1) * size
+                    ]
+
         second = dot(z_ref[...], c_ref[...], 0, 0).astype(BF16)
         for d in range(columns):
-            out_ref[d, 0] = second[d * out_rows : (d + 1) * out_rows]
-
+            at = slice(d * piece, (d + 1) * piece)
+            out_ref[d, step, 2 * size :, :] = jnp.concatenate(
+                [second[:half, at], second[half:, at]], axis=1
+            )
+
+    shape = (columns, blocks, 2 * size + half, 2 * piece)
     whole = lambda *shape: pl.BlockSpec(shape, lambda i: (0,) * len(shape))
     return pl.pallas_call(
         kernel,
         grid=(blocks,),
         in_specs=[
             whole(tokens, width),
-            pl.BlockSpec((tokens, piece), lambda i: (0, i)),
-            pl.BlockSpec((tokens, piece), lambda i: (0, i)),
+            pl.BlockSpec((tokens, step_size), lambda i: (0, i)),
+            pl.BlockSpec((tokens, step_size), lambda i: (0, i)),
             whole(tokens, width),
         ],
-        out_specs=[
-            pl.BlockSpec((1, blocks, in_rows, piece), lambda i: (i // per, 0, 0, i % per)),
-            pl.BlockSpec((columns, 1, out_rows, width), lambda i: (0, i, 0, 0)),
-        ],
-        out_shape=[
-            jax.ShapeDtypeStruct((columns, blocks, in_rows, width), BF16),
-            jax.ShapeDtypeStruct((columns, blocks, out_rows, width), BF16),
-        ],
+        out_specs=whole(*shape),
+        out_shape=jax.ShapeDtypeStruct(shape, BF16),
         compiler_params=params(),
         cost_estimate=estimate(
             flops=4 * tokens * width * hidden,
@@ -636,12 +799,12 @@
     )(parts, cross_q, after_self, gain, cross_grad, self_out)
 
 
-def input_stage(back, weights, inputs, gain, self_grad, groups):
+def input_stage(back, weights, inputs, gain, self_grad, slot, groups):
     own, tokens = back.shape[2:]
     width = inputs.shape[1]
     padded = groups * own
 
-    def kernel(b_ref, w_ref, x_ref, g_ref, h_ref, out_ref, acc_ref):
+    def kernel(s_ref, b_ref, w_ref, x_ref, g_ref, h_ref, out_ref, acc_ref):
         step = pl.program_id(0)
         grads = jnp.concatenate([b_ref[g, 0] for g in range(groups)], axis=0)
         term = dot(grads, w_ref[0], 0, 1)
@@ -659,26 +822,29 @@
             back, unused = pulled_norm(x_ref[...].astype(F32), g_ref[...], acc_ref[...])
             out_ref[...] = (h_ref[...] + back).astype(BF16)
 
-    whole = lambda *shape: pl.BlockSpec(shape, lambda i: (0,) * len(shape))
+    whole = lambda *shape: pl.BlockSpec(shape, lambda i, s: (0,) * len(shape))
     return pl.pallas_call(
         kernel,
-        grid=(3,),
-        in_specs=[
-            pl.BlockSpec((groups, 1, own, tokens), lambda i: (0, i, 0, 0)),
-            pl.BlockSpec((1, width, padded), lambda i: (i, 0, 0)),
-            whole(tokens, width),
-            whole(1, width),
-            whole(tokens, width),
-        ],
-        out_specs=whole(tokens, width),
+        grid_spec=pltpu.PrefetchScalarGridSpec(
+            num_scalar_prefetch=1,
+            grid=(3,),
+            in_specs=[
+                pl.BlockSpec((groups, 1, own, tokens), lambda i, s: (0, i, 0, 0)),
+                pl.BlockSpec((1, width, padded), lambda i, s: (i, 0, 0)),
+                pl.BlockSpec((tokens, width), lambda i, s: (s[0], 0)),
+                whole(1, width),
+                whole(tokens, width),
+            ],
+            out_specs=whole(tokens, width),
+            scratch_shapes=[pltpu.VMEM((tokens, width), F32)],
+        ),
         out_shape=jax.ShapeDtypeStruct((tokens, width), BF16),
-        scratch_shapes=[pltpu.VMEM((tokens, width), F32)],
         compiler_params=params(),
         cost_estimate=estimate(
             flops=6 * tokens * width * width, bytes_accessed=6 * width * width, transcendentals=0
         ),
         name="input_stage",
-    )(back, weights, inputs, gain, self_grad)
+    )(slot, back, weights, inputs, gain, self_grad)
 
 
 def both_queries(own, pieces, mine):
@@ -714,55 +880,59 @@
     )(mine, own, *pieces)
 
 
-def own_weight_grads(low, inputs, grads, weights, blocks):
-    length, width = inputs.shape
+def own_weight_grads(low, gain, grads, weights, core, columns, blocks):
+    length, width = low.shape
     groups, _, own, tokens = grads.shape
     rows = width // blocks
-
-    def kernel(a_ref, x_ref, d_ref, w_ref, out_ref, gain_ref, acc_ref):
+    per = blocks // columns
+
+    def kernel(c_ref, a_ref, g_ref, d_ref, w_ref, kept_ref, sent_ref, gain_ref):
         step = pl.program_id(0)
         grads = jnp.concatenate([d_ref[g, 0] for g in range(groups)], axis=1)
-        weight = dot(grads, a_ref[...], 1, 0).T.astype(BF16)
-        for b in range(blocks):
-            out_ref[b, 0] = weight[b * rows : (b + 1) * rows]
-        term = dot(grads, w_ref[0], 0, 0)
+        turned = dot(grads, a_ref[...], 1, 0)
+        weight = turned.T.astype(BF16)
+        for bit in range(2):
+
+            @pl.when(c_ref[0] == bit)
+            def put():
+                for b in range(blocks):
+                    column = b // per
+                    ref = kept_ref if column % 2 == bit else sent_ref
+                    ref[column // 2, b % per, 0] = weight[b * rows : (b + 1) * rows]
+
+        term = jnp.sum(turned * w_ref[0].astype(F32), axis=0, keepdims=True) / g_ref[...]
 
         @pl.when(step == 0)
         def first():
-            acc_ref[...] = term
+            gain_ref[...] = term
 
         @pl.when(step > 0)
         def more():
-            acc_ref[...] += term
-
-        @pl.when(step == 2)
-        def last():
-            values = x_ref[...].astype(F32)
-            inverse = lax.rsqrt(jnp.mean(values * values, axis=-1, keepdims=True) + epsilon)
-            gain_ref[...] = jnp.sum(acc_ref[...] * values * inverse, axis=0, keepdims=True)
-
-    whole = lambda *shape: pl.BlockSpec(shape, lambda i: (0,) * len(shape))
+            gain_ref[...] += term
+
+    shape = (columns // 2, per, 3, rows, own)
+    whole = lambda *shape: pl.BlockSpec(shape, lambda i, c: (0,) * len(shape))
+    part = pl.BlockSpec((columns // 2, per, 1, rows, own), lambda i, c: (0, 0, i, 0, 0))
     return pl.pallas_call(
         kernel,
-        grid=(3,),
-        in_specs=[
-            whole(length, width),
-            whole(length, width),
-            pl.BlockSpec((groups, 1, own, tokens), lambda i: (0, i, 0, 0)),
-            pl.BlockSpec((1, own, width), lambda i: (i, 0, 0)),
-        ],
-        out_specs=[pl.BlockSpec((blocks, 1, rows, own), lambda i: (0, i, 0, 0)), whole(1, width)],
-        out_shape=[
-            jax.ShapeDtypeStruct((blocks, 3, rows, own), BF16),
-            jax.ShapeDtypeStruct((1, width), F32),
-        ],
-        scratch_shapes=[pltpu.VMEM((length, width), F32)],
+        grid_spec=pltpu.PrefetchScalarGridSpec(
+            num_scalar_prefetch=1,
+            grid=(3,),
+            in_specs=[
+                whole(length, width),
+                whole(1, width),
+                pl.BlockSpec((groups, 1, own, tokens), lambda i, c: (0, i, 0, 0)),
+                pl.BlockSpec((1, own, width), lambda i, c: (i, 0, 0)),
+            ],
+            out_specs=[part, part, whole(1, width)],
+        ),
+        out_shape=[jax.ShapeDtypeStruct(shape, BF16)] * 2 + [jax.ShapeDtypeStruct((1, width), F32)],
         compiler_params=params(),
         cost_estimate=estimate(
             flops=12 * length * width * own, bytes_accessed=4 * length * width, transcendentals=0
         ),
         name="own_weight_grads",
-    )(low, inputs, grads, weights)
+    )(core, low, gain, grads, weights)
 
 
 def self_backward(projected, mixed, grads, prob, weight, groups):
@@ -944,17 +1114,12 @@
     )
 
     cross_query, thirds = lax.optimization_barrier((cross_query, [a[2] for a in arrived]))
-    encoded = [own_rows_low]
     pairs = [first_pair]
+    came = []
     for first, second, third in zip(firsts, seconds, thirds):
         pairs.append(project_rows([first], turned_kv))
         pairs.append(project_rows([second, third], turned_kv))
-        encoded += [first, jnp.concatenate([second, third], axis=0)]
-
-    def own_rows(array):
-        return lax.dynamic_slice_in_dim(array, slot_of * tokens, tokens, 0)
-
-    own_self_mix = lax.dynamic_slice_in_dim(self_mix, slot_of * tokens, tokens, 1)
+        came += [first, second, third]
 
     part_mix, cross_prob, local_top = cross_forward(cross_query, pairs, bias, width, groups)
     stat_rows = (part_mix.shape[1] - width) // 2
@@ -992,24 +1157,24 @@
         ends = [sum(counts[: i + 1]) for i in range(len(counts) - 1)]
         return [p.reshape(-1, full // columns) for p in jnp.split(moved, ends, axis=1)]
 
-    cross_out_chunks = by_rows(dot(cross_mix, cross_grad_low, 1, 0))
     unit = width // blocks // columns
     staged = (
         padded == width
         and columns * own == width
         and columns * seqs == blocks
+        and columns % 2 == 0
         and ffn_in.shape[1] == columns * width
-        and width % (ffn_in.shape[1] // blocks) == 0
+        and ffn_in.shape[1] // blocks * columns == 2 * width
+        and blocks == 8
     )
     if staged:
-        in_chunks, out_chunks = hidden_weight_grads(
+        chunks = hidden_weight_grads(
             third_low, pre_low, hidden_low, own_cotangent, columns, blocks
         )
-        chunks = jnp.concatenate([in_chunks, out_chunks], axis=2)
         packed, chunks, own_output = lax.optimization_barrier((packed, chunks, own_output))
-        inner = chunks.shape[1:]
+        inner = chunks.shape[2:]
         hidden = lax.psum_scatter(
-            chunks.reshape(-1, width), "dp", scatter_dimension=0, tiled=True
+            chunks.reshape(-1, inner[1]), "dp", scatter_dimension=0, tiled=True
         )
     else:
         in_chunks = dot(third_low, pre_low, 0, 0).astype(BF16)
@@ -1035,130 +1200,204 @@
     )
     query_parts, output_parts = lax.optimization_barrier((query_parts, output_parts))
     joined = traded(query_parts)
-    enc_parts = [
-        (dot(k, cross_kv[0], 1, 1) + dot(v, cross_kv[1], 1, 1)).astype(BF16)
-        for k, v in zip(key_low, value_low)
-    ]
-    shares = [0, 4, 6, 8, 14]
-    marks = [enc_rows * share // 14 // 16 * 16 for share in shares]
-    enc_rest = [
-        jnp.concatenate(enc_parts[2 * step - 1 : 2 * step + 1], axis=0) for step in range(1, seqs)
-    ]
-    enc_back = [[] for _ in enc_rest]
-
-    def send_back(number):
-        for step, rest in enumerate(enc_rest, 1):
-            piece = rest[marks[number] : marks[number + 1]]
-            if number:
-                piece, unused = lax.optimization_barrier((piece, enc_back[step - 1][-1]))
-            moved = lax.ppermute(piece, "blk", [(b, a) for a, b in shifted(step)])
-            enc_back[step - 1].append(moved)
-
-    def wait_back(value):
-        value, last = lax.optimization_barrier((value, [back[-1] for back in enc_back]))
-        for back, piece in zip(enc_back, last):
-            back[-1] = piece
-        return value
-
-    send_back(0)
-    key_chunks = by_rows(sum(dot(e, g, 0, 0) for e, g in zip(encoded, key_low)))
-    value_chunks = by_rows(sum(dot(e, g, 0, 0) for e, g in zip(encoded, value_low)))
+    shares = [0, 7, 11, 15, 22, 28]
+    marks = [enc_rows * share // 28 for share in shares]
+    pieces = row_grads(key_low[1], value_low[1], cross_kv, marks)
+    here = jnp.full((1,), mine, jnp.int32)
+    together = lambda *values: lax.optimization_barrier(values)
+
+    def sent_back(piece):
+        return lax.ppermute(piece, "blk", shifted(1))
+
+    def moved(array, axis, step):
+        size = lax.axis_size(axis)
+        return lax.ppermute(array, axis, [(i, i ^ step) for i in range(size)])
+
+    def bit_of(axis, step):
+        return jnp.full((1,), lax.rem(lax.axis_index(axis) // step, 2), jnp.int32)
+
+    def chunks_of(kernel_dots, operands, specs):
+        return weight_chunks(
+            kernel_dots, operands, specs, bit_of("dp", 1), slot, columns, blocks, width
+        )
+
+    back_1 = sent_back(pieces[0])
+    output = returned(output_parts)
     if staged:
-        firsts = Halving(jnp.concatenate([key_chunks, value_chunks], axis=2))
-        joined, firsts.array, hidden = lax.optimization_barrier((joined, firsts.array, hidden))
-    joined = wait_back(joined)
-    send_back(1)
-    if staged:
-        hidden = lax.psum_scatter(hidden, "blk", scatter_dimension=0, tiled=True)
-        firsts.send("dp", 0)
-
+        cuts = [0]
+        for piece in came:
+            cuts.append(cuts[-1] + piece.shape[0])
+
+        def rows_dot(grad):
+            def one(refs):
+                total = dot(refs[0][...], refs[grad][...], 0, 0)
+                for i, (start, stop) in enumerate(zip(cuts, cuts[1:])):
+                    total += dot(refs[1 + i][...], refs[grad + 1][start:stop, :], 0, 0)
+                return total
+
+            return one
+
+        count = 1 + len(came)
+        operands = [own_rows_low, *came, *key_low, *value_low, cross_mix, cross_grad_low]
+        kept_1, sent_1 = chunks_of(
+            [
+                rows_dot(count),
+                rows_dot(count + 2),
+                lambda refs: dot(refs[count + 4][...], refs[count + 5][...], 1, 0),
+            ],
+            operands,
+            [None] * len(operands),
+        )
+        joined, pieces, back_1, output, hidden, kept_1, sent_1 = together(
+            joined, pieces, back_1, output, hidden, kept_1, sent_1
+        )
+        got_1 = moved(sent_1, "dp", 1)
     query_grad, self_grad, self_grad_low, mixed_grad, gain_two = mixed_stage(
         joined, cross_q, after_self, gain_rows[1], cross_grad, padded_out, groups, own
     )
+    if staged:
+        (
+            query_grad, self_grad, self_grad_low, mixed_grad, gain_two, kept_1, got_1, pieces, hidden,
+        ) = together(
+            query_grad, self_grad, self_grad_low, mixed_grad, gain_two, kept_1, got_1, pieces, hidden,
+        )
     own_mixed = traded(mixed_grad)
-    cross_q_chunks = by_rows(dot(second_low, query_grad, 0, 1))
-    self_out_chunks = by_rows(dot(own_self_mix[:width], self_grad_low, 1, 0))
-    own_mixed, cross_q_chunks, self_out_chunks = wait_back(
-        (own_mixed, cross_q_chunks, self_out_chunks)
-    )
-    send_back(2)
     if staged:
-        seconds = Halving(
-            jnp.concatenate([cross_out_chunks, cross_q_chunks, self_out_chunks], axis=2)
-        )
-        own_mixed = after(own_mixed, firsts)
-        firsts.send("dp", 0)
-        seconds.send("dp", 0)
+        back_2 = sent_back(pieces[1])
+        shares = [inner[0] // 3, inner[0] * 5 // 12, inner[0] // 4]
+        (kept_i, sent_i), (kept_o, sent_o), (kept_u, sent_u) = evens(
+            hidden.reshape((blocks,) + inner), bit_of("blk", 1), shares
+        )
+        got_i = moved(sent_i, "blk", 1)
+        kept_1, sent_1 = fold([(kept_1, got_1)], bit_of("dp", 2), blocks)
+        operands = [second_low, query_grad, self_mix, self_grad_low]
+        specs = [None] * 2
+        specs += [pl.BlockSpec((width, tokens), lambda i, c, n: (0, n[0])), None]
+        kept_2, sent_2 = chunks_of(
+            [
+                lambda refs: dot(refs[0][...], refs[1][...], 0, 1),
+                lambda refs: dot(refs[2][...], refs[3][...], 1, 0),
+            ],
+            operands,
+            specs,
+        )
+        (
+            own_mixed, back_2, kept_i, got_i, kept_o, sent_o, kept_1, sent_1, kept_2, sent_2, pieces,
+            kept_u, sent_u,
+        ) = together(
+            own_mixed, back_2, kept_i, got_i, kept_o, sent_o, kept_1, sent_1, kept_2, sent_2, pieces,
+            kept_u, sent_u,
+        )
+        got_o = moved(sent_o, "blk", 1)
+        got_1 = moved(sent_1, "dp", 2)
+        got_2 = moved(sent_2, "dp", 1)
+        back_3 = sent_back(pieces[2])
     own_grads = self_backward(projected, sent_mix, own_mixed, self_prob, self_weight, groups)
-    own_grads = wait_back(own_grads)
     if staged:
-        own_grads = after(own_grads, firsts, seconds)
-    send_back(3)
+        own_grads, kept_o, got_o, kept_2, got_2, pieces, back_3, sent_u = together(
+            own_grads, kept_o, got_o, kept_2, got_2, pieces, back_3, sent_u
+        )
     back = traded(own_grads)
     if staged:
-        firsts.array = jnp.squeeze(firsts.array, 0)
-        firsts.send("blk", 0)
-        seconds.send("dp", 0)
-        part, gain_one = own_weight_grads(first_low, all_inputs, own_grads, own_qkv, blocks)
-        back, part, gain_one = wait_back((back, part, gain_one))
-        back = after(back, firsts, seconds)
-        part = halved(part.reshape((columns, seqs) + part.shape[1:]), "dp", 0)
-        seconds.array = jnp.squeeze(seconds.array, 0)
-        seconds.send("blk", 0)
-    own_grad = input_stage(
-        back, padded_qkv, own_rows(all_inputs), gain_rows[0], self_grad, groups
-    )
-    if not staged:
-        own_first = own_rows(first_low)
-        full = back.transpose(1, 0, 2, 3).reshape(3, padded, tokens)[:, :width]
-        first_back = sum(dot(full[c], self_qkv[c], 0, 1) for c in range(3))
-        unused, gain_one = pulled_norm(
-            own_rows(all_inputs).astype(F32), gain_rows[0], first_back
-        )
-        part = jnp.concatenate([by_rows(dot(own_first, full[c], 0, 1)) for c in range(3)], axis=2)
-    gain_grads = total_of(jnp.concatenate([gain_one, gain_two, gain_three], axis=0))
-    dec_grad = returned(leaving(own_grad))
-    output = returned(output_parts)
-    if seqs == 2:
-        enc_grad = both_queries(enc_parts[0], enc_back[0], jnp.full((1,), mine, jnp.int32))
-    else:
-        enc_back = [enc_parts[0]] + [jnp.concatenate(pieces, axis=0) for pieces in enc_back]
-        enc_grad = []
-        for s in range(seqs):
-            choice = enc_back[0]
-            for step in range(1, seqs):
-                choice = jnp.where(lax.rem(mine + step, seqs) == s, enc_back[step], choice)
-            enc_grad.append(choice)
-        enc_grad = jnp.stack(enc_grad, axis=0)
-
+        back_4 = sent_back(pieces[3])
+        kept_2, sent_2 = fold([(kept_2, got_2)], bit_of("dp", 2), blocks)
+        got_2 = moved(sent_2, "dp", 2)
+        got_u = moved(sent_u, "blk", 1)
+        kept_w, sent_w, gain_one = own_weight_grads(
+            first_low, gain_rows[0], own_grads, own_qkv, bit_of("dp", 1), columns, blocks
+        )
+        gains = jnp.concatenate([gain_one, gain_two, gain_three], axis=0)
+        (
+            back, back_4, kept_1, got_1, kept_2, got_2, kept_u, got_u, kept_w, sent_w, gains, pieces,
+        ) = together(
+            back, back_4, kept_1, got_1, kept_2, got_2, kept_u, got_u, kept_w, sent_w, gains, pieces,
+        )
+    own_grad = input_stage(back, padded_qkv, all_inputs, gain_rows[0], self_grad, slot, groups)
     if staged:
-        seconds.take()
-        rest = jnp.concatenate([firsts.array, seconds.array], axis=1)
-        rest = halved(rest, "blk", 0)
-        ffn_in_rows = hidden[: width // blocks]
-        placed_rows = placed(
-            jnp.concatenate([hidden[width // blocks :], rest], axis=0),
-            [width // blocks] + [unit] * 5,
-        )
-        ffn_out_own, key_own, value_own, cross_out_own, cross_q_own, self_out_own = placed_rows
-        qkv = 0.0
-        for step in range(seqs):
+        back_5 = sent_back(pieces[4])
+        got_w = moved(sent_w, "dp", 1)
+        kept_j, sent_j = fold([(kept_1, got_1), (kept_2, got_2)], bit_of("blk", 1), 1)
+        got_j = moved(sent_j, "blk", 1)
+        kept_h, sent_h = fold(
+            [(kept_i, got_i), (kept_o, got_o), (kept_u, got_u)], bit_of("blk", 2), 1
+        )
+        got_h = moved(sent_h, "blk", 2)
+        gains = gains + moved(gains, "dp", 1)
+        own_grad, back_5, kept_w, got_w, kept_j, got_j, kept_h, got_h, gains, pieces, key_low = (
+            together(
+                own_grad, back_5, kept_w, got_w, kept_j, got_j, kept_h, got_h, gains, pieces, key_low
+            )
+        )
+    dec_parts = leaving(own_grad)
+    if staged:
+        kept_h, sent_h = fold([(kept_h, got_h)], bit_of("blk", 4), 1)
+        got_h = moved(sent_h, "blk", 4)
+        flat = (columns // 2, -1, own)
+        kept_w, sent_w = fold([(kept_w.reshape(flat), got_w.reshape(flat))], bit_of("dp", 2), 1)
+        got_w = moved(sent_w, "dp", 2)
+        kept_j, sent_j = fold([(kept_j, got_j)], bit_of("blk", 2), 1)
+        got_j = moved(sent_j, "blk", 2)
+        gains = gains + moved(gains, "dp", 2)
+        dec_parts, kept_w, got_w, kept_j, got_j, gains, key_low, kept_h, got_h = together(
+            dec_parts, kept_w, got_w, kept_j, got_j, gains, key_low, kept_h, got_h
+        )
+        (enc_own,) = row_grads(key_low[0], value_low[0], cross_kv, [0, enc_rows])
+        flat = (seqs, -1, own)
+        halves = fold([(kept_w.reshape(flat), got_w.reshape(flat))], here, 1)
+        got_w = []
+        for step, piece in enumerate(halves):
             pairs = []
             for b in range(blocks):
                 row = (b // groups + step) % seqs
                 for d in range(columns):
                     pairs.append((b * columns + d, (d * seqs + row) * columns + b % groups))
-            piece = lax.dynamic_index_in_dim(part, lax.rem(mine + step, seqs), 0, False)
-            qkv = qkv + lax.ppermute(piece, ("blk", "dp"), pairs).astype(F32)
+            piece = piece.reshape(3, width // blocks, own)
+            got_w.append(lax.ppermute(piece, ("blk", "dp"), pairs))
+        kept_j, sent_j = fold([(kept_j, got_j)], bit_of("blk", 4), 1)
+        got_j = moved(sent_j, "blk", 4)
+        dec_grad = returned(dec_parts)
+        gains = gains + moved(gains, "blk", 1)
+        kept_j, got_j, dec_grad, gains, enc_own = together(
+            kept_j, got_j, dec_grad, gains, enc_own
+        )
+        enc_grad = both_queries(enc_own, [back_1, back_2, back_3, back_4, back_5], here)
+        qkv = sum(piece.astype(F32) for piece in got_w)
+        gains = gains + moved(gains, "blk", 2)
+        gain_grads = gains + moved(gains, "blk", 4)
+        ffn_in_own, ffn_out_own, kv_own, cross_out_own, cross_q_own, self_out_own = unpacked(
+            (kept_h[0], got_h[0]), (kept_j[0], got_j[0]), width // blocks, width // columns
+        )
     else:
+        rest = sent_back(jnp.concatenate(pieces[1:], axis=0))
+        (enc_own,) = row_grads(key_low[0], value_low[0], cross_kv, [0, enc_rows])
+        enc_grad = both_queries(enc_own, [back_1, rest], here)
+        own_rows = lambda array: lax.dynamic_slice_in_dim(array, slot_of * tokens, tokens, 0)
+        full = back.transpose(1, 0, 2, 3).reshape(3, padded, tokens)[:, :width]
+        first_back = sum(dot(full[c], self_qkv[c], 0, 1) for c in range(3))
+        unused, gain_one = pulled_norm(
+            own_rows(all_inputs).astype(F32), gain_rows[0], first_back
+        )
+        gains = jnp.concatenate([gain_one, gain_two, gain_three], axis=0)
+        gain_grads = total_of(total_of(gains, "dp"), "blk")
+        dec_grad = returned(dec_parts)
         reduced = lambda array: halved(halved(array, "dp", 0), "blk", 0)
-        ffn_in_rows = reduced(in_chunks)
-        chunks = [out_chunks, cross_out_chunks, key_chunks, value_chunks]
-        chunks += [cross_q_chunks, self_out_chunks, part]
+        own_first = own_rows(first_low)
+        own_self_mix = lax.dynamic_slice_in_dim(self_mix, slot_of * tokens, tokens, 1)
+        encoded = [own_rows_low, jnp.concatenate(came, axis=0)]
+        late = [
+            sum(dot(e, g, 0, 0) for e, g in zip(encoded, key_low)),
+            sum(dot(e, g, 0, 0) for e, g in zip(encoded, value_low)),
+            dot(cross_mix, cross_grad_low, 1, 0),
+            dot(second_low, query_grad, 0, 1),
+            dot(own_self_mix[:width], self_grad_low, 1, 0),
+        ] + [dot(own_first, full[c], 0, 1) for c in range(3)]
+        chunks = [out_chunks] + [by_rows(grad) for grad in late]
         counts = [out_chunks.shape[2]] + [unit] * 8
         rows = placed(reduced(jnp.concatenate(chunks, axis=2)), counts)
-        ffn_out_own, cross_out_own, key_own, value_own, cross_q_own, self_out_own = rows[:6]
+        ffn_out_own, key_own, value_own, cross_out_own, cross_q_own, self_out_own = rows[:6]
+        kv_own = jnp.stack([key_own, value_own])
         qkv = jnp.stack(rows[6:])
+        ffn_in_own = reduced(in_chunks).astype(F32)
 
     return (
         output,
@@ -1168,9 +1407,9 @@
         qkv,
         self_out_own,
         cross_q_own,
-        jnp.stack([key_own, value_own]),
+        kv_own,
         cross_out_own,
-        ffn_in_rows.astype(F32),
+        ffn_in_own,
         ffn_out_own,
     )
 

time: 515 us -> 488 us (0.948)
  Pallas kernels: 169 us -> 226 us
  local copies, waits for them, and re-layouts: 60.2 us -> 33.9 us
  other arithmetic: 30.7 us -> 6.54 us
  matrix products: 19.3 us -> 0 us
  starting transfers between devices: 71.8 us -> 64.4 us
  waiting for transfers between devices: 141 us -> 135 us
    pallas_call x2 -> x17, Pallas kernels: 12.7 us -> 67.4 us  [the longest x9 23.1 us: fold(): pl.pallas_call(kernel, grid_spec=pltpu.PrefetchScalarGridSpec(num_scalar_...]
    dot_general x15 -> x0, matrix products: 19.3 us -> none  [dot(): lax.dot_general(left, right, (((left_dim,), (right_dim,)), ((), ())), pre...]
    ppermute x4, waiting for transfers between devices: 28.4 us -> 43.3 us  [exchange(): lax.ppermute(pieces(lax.rem(mine + step, seqs)), 'blk', shifted(step))]
    all_to_all x3 -> x0, waiting for transfers between devices: 12.5 us -> none  [the longest x2 7.04 us: total_of(): array = jnp.sum(lax.all_to_all(copies, axis, 0, 0), axis=0)]
    all_to_all x3 -> x0, starting transfers between devices: 11.7 us -> none  [the longest x2 8.28 us: total_of(): array = jnp.sum(lax.all_to_all(copies, axis, 0, 0), axis=0)]
    convert_element_type x11 -> x0, other arithmetic: 11.3 us -> none  [the longest x10 9.53 us: added(): return (kept.astype(F32) + got.astype(F32)).astype(BF16)]
    concatenate x5 -> x1, other arithmetic: 9.95 us -> 0.7 us  [body(): gains = jnp.concatenate([gain_one, gain_two, gain_three], axis=0)]
    all_to_all x6, waiting for transfers between devices: 39 us -> 31.2 us  [traded(): return lax.all_to_all(array, 'blk', 0, 0, axis_index_groups=members)]
  transfers between devices with their start and end apart: 35 -> 41, of which waited for: 14 -> 19; matrix products, arithmetic and copies ran while one was open for 18% -> 5% of each run, Pallas kernels for 23% -> 36%
where the time goes in v3:
time: 488 us; the launch traced here: 481 us
  Pallas kernels  226 us (46%)
  waiting for transfers between devices  135 us (28%)
  starting transfers between devices  64.4 us (13%)
  local copies, waits for them, and re-layouts  33.9 us (7%)
  between operations  14.8 us (3%)
  other arithmetic  6.54 us (1%)
    pallas_call x1, Pallas kernels, cross_backward(): pl.pallas_call(kernel, grid=(heads // pair,), in_specs=[pl.BlockSpec((siz...  48.8 us
    ppermute x4, waiting for transfers between devices, exchange(): lax.ppermute(pieces(lax.rem(mine + step, seqs)), 'blk', shifted(step))  43.3 us
    ppermute x19, waiting for transfers between devices, moved(): return lax.ppermute(array, axis, [(i, i ^ step) for i in range(size)])  35.6 us
    all_to_all x6, waiting for transfers between devices, traded(): return lax.all_to_all(array, 'blk', 0, 0, axis_index_groups=members)  31.2 us
    pallas_call x1, Pallas kernels, cross_forward(): pl.pallas_call(kernel, grid=(heads,), in_specs=[pl.BlockSpec((HEAD_DIM, l...  28.4 us
    all_to_all x6, starting transfers between devices, traded(): return lax.all_to_all(array, 'blk', 0, 0, axis_index_groups=members)  23.2 us
    pallas_call x9, Pallas kernels, fold(): pl.pallas_call(kernel, grid_spec=pltpu.PrefetchScalarGridSpec(num_scalar_...  23.1 us
    unnamed x95, local copies, waits for them, and re-layouts  21.9 us
  transfers between devices with their start and end apart: 41, of which 19 were waited for; matrix products, arithmetic and copies ran while one was open for 5% of the time, Pallas kernels for 36%

profile of v3, /device:TPU:0, one launch (start us, length us, event | category | flops | bytes accessed | tf_op | source)
XLA Modules:
  0.0 481.3 jit_solution(5296862998309223082)
XLA Ops:
  12.4 9.1 %collective-permute-done = bf16[128,768]{1,0:T(8,128)(2,1)S(1)} collective-permute-done((bf16[128,768]{1,0:T(8,128)(2,1)S(1)}, bf16[128,768]{1,0:T(8,128)(2,1)S(1)}, u32[]{:S(2)}, u32[]{:S(2)}) %collective-permute-start) | collective-permute-done | bytes 196640 | tf_op jit(solution)/shard_map/ppermute | solution.py:1024
  38.5 5.6 %project_rows.3.refs_1_.refs_4_ = bf16[2,768,896]{2,1,0:T(8,128)(2,1)} custom-call(bf16[896,768]{1,0:T(8,128)(2,1)} %dynamic-slice_bitcast_fusion.refs_0_, bf16[2,768,768]{2,1,0:T(8,128)(2,1)} %bitcast.94), custom_call_target="tpu_custom_call" | custom-call | flops 2 | bytes 1 | tf_op jit(solution)/shard_map/project_rows/pallas_call | solution.py:512
  50.0 6.0 %collective-permute-done.1.refs_0_.refs_1_ = bf16[384,768]{1,0:T(8,128)(2,1)S(1)} collective-permute-done((bf16[384,768]{1,0:T(8,128)(2,1)}, bf16[384,768]{1,0:T(8,128)(2,1)S(1)}, u32[]{:S(2)}, u32[]{:S(2)}) %collective-permute-start.1) | collective-permute-done | bytes 589856 | tf_op jit(solution)/shard_map/ppermute | solution.py:1071
  61.1 11.8 %self_forward.1 = (bf16[1024,768]{1,0:T(8,128)(2,1)}, bf16[3,192,1024]{2,1,0:T(8,128)(2,1)}, bf16[4,192,1024]{2,1,0:T(8,128)(2,1)}, bf16[3,1024,1024]{2,1,0:T(8,128)(2,1)}, f32[3,1,1024]{2,1,0:T(1,128)}) custom-call(bf16[1024,768]{1,0:T(8,128)(2,1)} %bitcast.98, f32[1,768]{1,0:T(1,128)} %get-tuple-element.408.g_ref, bf16[3,192,768]{2,1,0:T(8,128)(2,1)} %bitcast.105, ...), custom_call_target="tpu_custom_call" | custom-call | flops 3 | bytes 1 | tf_op jit(solution)/shard_map/self_forward/pallas_call | solution.py:467
  73.6 5.2 %all-to-all-start.1 = ((bf16[4,192,1024]{2,1,0:T(8,128)(2,1)}), bf16[4,192,1024]{2,1,0:T(8,128)(2,1)S(1)}, u32[]{:S(2)}, u32[]{:S(2)}) async-start(bf16[4,192,1024]{2,1,0:T(8,128)(2,1)} %get-tuple-element.184.o_ref), calls=%async_computation.1 | async-start | bytes 3145728 | tf_op jit(solution)/shard_map/all_to_all | solution.py:1047
  88.7 20.3 %all-to-all-done.1 = bf16[4,192,1024]{2,1,0:T(8,128)(2,1)S(1)} async-done(((bf16[4,192,1024]{2,1,0:T(8,128)(2,1)}), bf16[4,192,1024]{2,1,0:T(8,128)(2,1)S(1)}, u32[]{:S(2)}, u32[]{:S(2)}) %all-to-all-start.1) | async-done | bytes 1572896 | tf_op jit(solution)/shard_map/all_to_all | solution.py:1047
  110.2 8.2 %query_stage.1 = (bf16[768,1024]{1,0:T(8,128)(2,1)}, f32[256,768]{1,0:T(8,128)}, bf16[256,768]{1,0:T(8,128)(2,1)}) custom-call(s32[1]{0:T(128)} %bitcast.s_ref.n_ref, bf16[1024,768]{1,0:T(8,128)(2,1)} %bitcast.99, bf16[768,1024]{1,0:T(8,128)(2,1)} %bitcast.101, bf16[768,768]{1,0:T(8,128)(2,1)} %w_ref.7, f32[1,768]{1,0:T(1,128)} %get-tuple-element.407.g_ref, ...), custom_call_target="tpu_custom_call" | custom-call | flops 4 | bytes 1 | tf_op jit(solution)/shard_map/query_stage/pallas_call | solution.py:544
  123.8 28.4 %cross_forward.1 = (bf16[4,800,256]{2,1,0:T(8,128)(2,1)}, bf16[12,1792,1024]{2,1,0:T(8,128)(2,1)}, f32[12,1,1024]{2,1,0:T(1,128)}) custom-call(bf16[768,1024]{1,0:T(8,128)(2,1)} %get-tuple-element.187.refs_0_, bf16[2,768,896]{2,1,0:T(8,128)(2,1)} %project_rows.3.refs_1_.refs_4_, bf16[2,768,384]{2,1,0:T(8,128)(2,1)} %project_rows.4.refs_2_.refs_5_, ...), custom_call_target="tpu_custom_call" | custom-call | flops 22 | bytes 1 | tf_op jit(solution)/shard_map/cross_forward/pallas_call | solution.py:327
  157.7 19.3 %collective-permute-done.4 = bf16[128,768]{1,0:T(8,128)(2,1)S(1)} collective-permute-done((bf16[128,768]{1,0:T(8,128)(2,1)S(1)}, bf16[128,768]{1,0:T(8,128)(2,1)S(1)}, u32[]{:S(2)}, u32[]{:S(2)}) %collective-permute-start.4) | collective-permute-done | bytes 196640 | tf_op jit(solution)/shard_map/ppermute | solution.py:1024
  180.4 16.9 %token_stage.1 = (bf16[256,768]{1,0:T(8,128)(2,1)}, f32[256,768]{1,0:T(8,128)}, bf16[256,768]{1,0:T(8,128)(2,1)}, bf16[256,768]{1,0:T(8,128)(2,1)}, bf16[256,307...) custom-call(bf16[4,800,256]{2,1,0:T(8,128)(2,1)} %copy-done.6, ...), custom_call_target="tpu_custom_call" | custom-call | flops 4 | bytes 1 | tf_op jit(solution)/shard_map/token_stage/pallas_call | solution.py:670
  201.5 12.9 %hidden_weight_grads.1 = bf16[4,8,384,384]{3,2,1,0:T(8,128)(2,1)} custom-call(bf16[256,768]{1,0:T(8,128)(2,1)} %get-tuple-element.196.a_ref, bf16[256,3072]{1,0:T(8,128)(2,1)} %get-tuple-element.197.du_ref, bf16[256,3072]{1,0:T(8,128)(2,1)} %get-tuple-element.198.z_ref, bf16[256,768]{1,0:T(8,128)(2,1)} %pad_maximum_fusion.1.c_ref), custom_call_target="tpu_custom_call" | custom-call | flops 2 | bytes 1 | tf_op jit(solution)/shard_map/hidden_weight_grads/pallas_call | solution.py:744
  214.4 6.6 %all-to-all-done.3.refs_8_ = bf16[4,832,256]{2,1,0:T(8,128)(2,1)S(1)} async-done(((bf16[4,832,256]{2,1,0:T(8,128)(2,1)}), bf16[4,832,256]{2,1,0:T(8,128)(2,1)S(1)}, u32[]{:S(2)}, u32[]{:S(2)}) %all-to-all-start.3) | async-done | bytes 1703968 | tf_op jit(solution)/shard_map/all_to_all | solution.py:1047
  224.6 48.8 %cross_backward.1 = (bf16[4,768,256]{2,1,0:T(8,128)(2,1)}, bf16[896,768]{1,0:T(8,128)(2,1)}, bf16[896,768]{1,0:T(8,128)(2,1)}, bf16[896,768]{1,0:T(8,128)(2,1)}, bf16[896,768]{1,0:T(8,128)(2,1)}) custom-call(bf16[768,1024]{1,0:T(8,128)(2,1)} %get-tuple-element.187.refs_0_, bf16[2,768,896]{2,1,0:T(8,128)(2,1)} %project_rows.3.refs_1_.refs_4_, ...), custom_call_target="tpu_custom_call" | custom-call | flops 45 | bytes 1 | tf_op jit(solution)/shard_map/cross_backward/pallas_call | solution.py:411
  277.2 5.7 %row_grads.2 = (bf16[224,768]{1,0:T(8,128)(2,1)}, bf16[128,768]{1,0:T(8,128)(2,1)}, bf16[128,768]{1,0:T(8,128)(2,1)}, bf16[224,768]{1,0:T(8,128)(2,1)}, bf16[192,768]{1,0:T(8,128)(2,1)}) custom-call(bf16[896,768]{1,0:T(8,128)(2,1)} %get-tuple-element.205.k_ref.refs_5_, bf16[896,768]{1,0:T(8,128)(2,1)} %get-tuple-element.206.v_ref.refs_7_, ...), custom_call_target="tpu_custom_call" | custom-call | flops 1 | bytes 1 | tf_op jit(solution)/shard_map/row_grads/pallas_call | solution.py:182
  284.4 12.2 %weight_chunks.2 = (bf16[16,144,384]{2,1,0:T(8,128)(2,1)}, bf16[16,144,384]{2,1,0:T(8,128)(2,1)}) custom-call(s32[1]{0:T(128)} %bitcast.26.c_ref, s32[1]{0:T(128)} %bitcast.s_ref.n_ref, bf16[896,768]{1,0:T(8,128)(2,1)} %dynamic-slice_bitcast_fusion.refs_0_, bf16[384,768]{1,0:T(8,128)(2,1)} %copy-done.15, bf16[128,768]{1,0:T(8,128)(2,1)} %copy-done.25, ...), custom_call_target="tpu_custom_call" | custom-call | flops 1 | bytes 1 | tf_op jit(solution)/shard_map/weight_chunks/pallas_call | solution.py:158
  329.6 9.7 %self_backward.1.d_ref = bf16[4,3,192,256]{3,2,1,0:T(8,128)(2,1)} custom-call(bf16[3,192,1024]{2,1,0:T(8,128)(2,1)} %get-tuple-element.222.q_ref.k_ref.v_ref, bf16[3,192,1024]{2,1,0:T(8,128)(2,1)} %get-tuple-element.222.q_ref.k_ref.v_ref, bf16[3,192,1024]{2,1,0:T(8,128)(2,1)} %get-tuple-element.222.q_ref.k_ref.v_ref, ...), custom_call_target="tpu_custom_call" | custom-call | flops 6 | bytes 1 | tf_op jit(solution)/shard_map/self_backward/pallas_call | solution.py:963
  353.6 5.1 %own_weight_grads.1 = (bf16[2,2,3,96,192]{4,3,2,1,0:T(8,128)(2,1)}, bf16[2,2,3,96,192]{4,3,2,1,0:T(8,128)(2,1)}, f32[1,768]{1,0:T(1,128)}) custom-call(s32[1]{0:T(128)} %bitcast.26.c_ref, bf16[1024,768]{1,0:T(8,128)(2,1)} %get-tuple-element.279.a_ref, f32[1,768]{1,0:T(1,128)} %get-tuple-element.408.g_ref, bf16[4,3,192,256]{3,2,1,0:T(8,128)(2,1)} %self_backward.1.d_ref, ...), custom_call_target="tpu_custom_call" | custom-call | flops 1 | bytes 1 | tf_op jit(solution)/shard_map/own_weight_grads/pallas_call | solution.py:916
  359.4 9.9 %collective-permute-done.14 = bf16[8,144,384]{2,1,0:T(8,128)(2,1)S(1)} collective-permute-done((bf16[8,144,384]{2,1,0:T(8,128)(2,1)}, bf16[8,144,384]{2,1,0:T(8,128)(2,1)S(1)}, u32[]{:S(2)}, u32[]{:S(2)}) %collective-permute-start.14) | collective-permute-done | bytes 884768 | tf_op jit(solution)/shard_map/ppermute | solution.py:1214
  370.1 10.5 %collective-permute-done.15 = bf16[8,96,384]{2,1,0:T(8,128)(2,1)S(1)} collective-permute-done((bf16[8,96,384]{2,1,0:T(8,128)(2,1)}, bf16[8,96,384]{2,1,0:T(8,128)(2,1)S(1)}, u32[]{:S(2)}, u32[]{:S(2)}) %collective-permute-start.15) | collective-permute-done | bytes 589856 | tf_op jit(solution)/shard_map/ppermute | solution.py:1214
  391.4 5.4 %input_stage.1 = bf16[256,768]{1,0:T(8,128)(2,1)} custom-call(s32[1]{0:T(128)} %bitcast.s_ref.n_ref, bf16[4,3,192,256]{3,2,1,0:T(8,128)(2,1)} %copy-done.10, bf16[3,768,768]{2,1,0:T(8,128)(2,1)} %w_ref.8, bf16[1024,768]{1,0:T(8,128)(2,1)} %bitcast.100, f32[1,768]{1,0:T(1,128)} %get-tuple-element.408.g_ref, f32[256,768]{1,0:T(8,128)} %get-tuple-element.287.h_ref), custom_call_target="tpu_custom_call" | custom-call | flops 1 | bytes 1 | tf_op jit(solution)/shard_map/input_stage/pallas_call | solution.py:826
  396.8 11.4 %collective-permute-done.17.refs_4_ = bf16[192,768]{1,0:T(8,128)(2,1)S(1)} collective-permute-done((bf16[192,768]{1,0:T(8,128)(2,1)S(1)}, bf16[192,768]{1,0:T(8,128)(2,1)S(1)}, u32[]{:S(2)}, u32[]{:S(2)}) %collective-permute-start.17) | collective-permute-done | bytes 294944 | tf_op jit(solution)/shard_map/ppermute | solution.py:1210
  425.6 14.8 %collective-permute-done.22 = bf16[128,768]{1,0:T(8,128)(2,1)S(1)} collective-permute-done((bf16[128,768]{1,0:T(8,128)(2,1)S(1)}, bf16[128,768]{1,0:T(8,128)(2,1)S(1)}, u32[]{:S(2)}, u32[]{:S(2)}) %collective-permute-start.22) | collective-permute-done | bytes 196640 | tf_op jit(solution)/shard_map/ppermute | solution.py:1024
  448.1 6.0 %row_grads.3.own_ref = bf16[896,768]{1,0:T(8,128)(2,1)} custom-call(bf16[896,768]{1,0:T(8,128)(2,1)} %get-tuple-element.328.refs_4_.k_ref, bf16[896,768]{1,0:T(8,128)(2,1)} %get-tuple-element.216.refs_6_.v_ref, bf16[2,768,768]{2,1,0:T(8,128)(2,1)} %w_ref.9), custom_call_target="tpu_custom_call" | custom-call | flops 1 | bytes 1 | tf_op jit(solution)/shard_map/row_grads/pallas_call | solution.py:182
  454.1 7.0 %collective-permute-done.27 = bf16[1,240,384]{2,1,0:T(8,128)(2,1)S(1)} collective-permute-done((bf16[1,240,384]{2,1,0:T(8,128)(2,1)}, bf16[1,240,384]{2,1,0:T(8,128)(2,1)S(1)}, u32[]{:S(2)}, u32[]{:S(2)}) %collective-permute-start.27) | collective-permute-done | bytes 184352 | tf_op jit(solution)/shard_map/ppermute | solution.py:1214
  (232 shorter events, 169.5 us)
Async XLA Ops:
  22.9 37.1 %all-to-all-start = ((bf16[4,256,768]{2,1,0:T(8,128)(2,1)}), bf16[4,256,768]{2,1,0:T(8,128)(2,1)S(1)}, u32[]{:S(2)}, u32[]{:S(2)}) async-start(bf16[4,256,768]{2,1,0:T(8,128)(2,1)} %broadcast_in_dim.115), calls=%async_computation | async-start | bytes 3145728 | tf_op jit(solution)/shard_map/all_to_all | solution.py:1038
  28.8 27.2 %collective-permute-start.1 = (bf16[384,768]{1,0:T(8,128)(2,1)}, bf16[384,768]{1,0:T(8,128)(2,1)S(1)}, u32[]{:S(2)}, u32[]{:S(2)}) collective-permute-start(bf16[384,768]{1,0:T(8,128)(2,1)} %get-tuple-element.387), channel_id=1, source_target_pairs={{0,16},{4,20},{8,24},{12,28},{16,0},{20,4},{24,8},{28,12},{1,17},{... | collective-permute-start | bytes 1769480 | tf_op jit(solution)/shard_map/ppermute | solution.py:1071
  73.6 35.4 %all-to-all-start.1 = ((bf16[4,192,1024]{2,1,0:T(8,128)(2,1)}), bf16[4,192,1024]{2,1,0:T(8,128)(2,1)S(1)}, u32[]{:S(2)}, u32[]{:S(2)}) async-start(bf16[4,192,1024]{2,1,0:T(8,128)(2,1)} %get-tuple-element.184.o_ref), calls=%async_computation.1 | async-start | bytes 3145728 | tf_op jit(solution)/shard_map/all_to_all | solution.py:1047
  79.1 39.3 %collective-permute-start.3 = (bf16[384,768]{1,0:T(8,128)(2,1)}, bf16[384,768]{1,0:T(8,128)(2,1)S(1)}, u32[]{:S(2)}, u32[]{:S(2)}) collective-permute-start(bf16[384,768]{1,0:T(8,128)(2,1)} %get-tuple-element.186), channel_id=1, source_target_pairs={{0,16},{4,20},{8,24},{12,28},{16,0},{20,4},{24,8},{28,12},{1,17},{... | collective-permute-start | bytes 1769480 | tf_op jit(solution)/shard_map/ppermute | solution.py:1075
  152.2 27.1 %all-to-all-start.2 = ((bf16[4,800,256]{2,1,0:T(8,128)(2,1)}), bf16[4,800,256]{2,1,0:T(8,128)(2,1)S(1)}, u32[]{:S(2)}, u32[]{:S(2)}) async-start(bf16[4,800,256]{2,1,0:T(8,128)(2,1)} %get-tuple-element.193), calls=%async_computation.2 | async-start | bytes 3276800 | tf_op jit(solution)/shard_map/all_to_all | solution.py:1047
  156.0 21.1 %collective-permute-start.4 = (bf16[128,768]{1,0:T(8,128)(2,1)S(1)}, bf16[128,768]{1,0:T(8,128)(2,1)S(1)}, u32[]{:S(2)}, u32[]{:S(2)}) collective-permute-start(bf16[128,768]{1,0:T(8,128)(2,1)S(1)} %dynamic-slice_bitcast_fusion.8), channel_id=1, source_target_pairs={{0,16},{4,20},{8,24},{12,28},{16,0},{20,4},{24,8},{28,12},{1,17},{... | collective-permute-start | bytes 589832 | tf_op jit(solution)/shard_map/ppermute | solution.py:1024
  197.3 23.7 %all-to-all-start.3 = ((bf16[4,832,256]{2,1,0:T(8,128)(2,1)}), bf16[4,832,256]{2,1,0:T(8,128)(2,1)S(1)}, u32[]{:S(2)}, u32[]{:S(2)}) async-start(bf16[4,832,256]{2,1,0:T(8,128)(2,1)} %get-tuple-element.195), calls=%async_computation.3 | async-start | bytes 3407872 | tf_op jit(solution)/shard_map/all_to_all | solution.py:1047
  200.9 102.2 %reduce-scatter.2.cloned.1.call-start = ((), (), s32[]{:S(2)}) async-start(), calls=%async_computation.8 | async-start | bytes 11796480 | tf_op jit(solution)/shard_map/reduce_scatter | solution.py:1176
  222.3 51.1 %collective-permute-start.5 = (bf16[128,768]{1,0:T(8,128)(2,1)S(1)}, bf16[128,768]{1,0:T(8,128)(2,1)S(1)}, u32[]{:S(2)}, u32[]{:S(2)}) collective-permute-start(bf16[128,768]{1,0:T(8,128)(2,1)S(1)} %get-tuple-element.400), channel_id=1, source_target_pairs={{0,16},{4,20},{8,24},{12,28},{16,0},{20,4},{24,8},{28,12},{1,17},{... | collective-permute-start | bytes 589832 | tf_op jit(solution)/shard_map/ppermute | solution.py:1024
  273.4 29.7 %all-to-all-start.4 = ((bf16[4,768,256]{2,1,0:T(8,128)(2,1)}), bf16[4,768,256]{2,1,0:T(8,128)(2,1)S(1)}, u32[]{:S(2)}, u32[]{:S(2)}) async-start(bf16[4,768,256]{2,1,0:T(8,128)(2,1)} %get-tuple-element.204), calls=%async_computation.4 | async-start | bytes 3145728 | tf_op jit(solution)/shard_map/all_to_all | solution.py:1047
  309.0 19.4 %all-to-all-start.5 = ((bf16[4,192,256]{2,1,0:T(8,128)(2,1)}), bf16[4,192,256]{2,1,0:T(8,128)(2,1)S(1)}, u32[]{:S(2)}, u32[]{:S(2)}) async-start(bf16[4,192,256]{2,1,0:T(8,128)(2,1)} %get-tuple-element.237), calls=%async_computation.6 | async-start | bytes 786432 | tf_op jit(solution)/shard_map/all_to_all | solution.py:1047
  342.9 37.7 %all-to-all-start.6 = ((bf16[4,3,192,256]{3,2,1,0:T(8,128)(2,1)}), bf16[4,3,192,256]{3,2,1,0:T(8,128)(2,1)S(1)}, u32[]{:S(2)}, u32[]{:S(2)}) async-start(bf16[4,3,192,256]{3,2,1,0:T(8,128)(2,1)} %self_backward.1.d_ref), calls=%async_computation.7 | async-start | bytes 2359296 | tf_op jit(solution)/shard_map/all_to_all | solution.py:1047
  346.5 22.8 %collective-permute-start.14 = (bf16[8,144,384]{2,1,0:T(8,128)(2,1)}, bf16[8,144,384]{2,1,0:T(8,128)(2,1)S(1)}, u32[]{:S(2)}, u32[]{:S(2)}) collective-permute-start(bf16[8,144,384]{2,1,0:T(8,128)(2,1)} %get-tuple-element.272), channel_id=1, source_target_pairs={{0,2},{1,3},{2,0},{3,1},{4,6},{5,7},{6,4},{7,5},{8,10},{9,11},{10,... | collective-permute-start | bytes 2654216 | tf_op jit(solution)/shard_map/ppermute | solution.py:1214
  350.9 29.7 %collective-permute-start.15 = (bf16[8,96,384]{2,1,0:T(8,128)(2,1)}, bf16[8,96,384]{2,1,0:T(8,128)(2,1)S(1)}, u32[]{:S(2)}, u32[]{:S(2)}) collective-permute-start(bf16[8,96,384]{2,1,0:T(8,128)(2,1)} %get-tuple-element.276), channel_id=1, source_target_pairs={{0,2},{1,3},{2,0},{3,1},{4,6},{5,7},{6,4},{7,5},{8,10},{9,11},{10,... | collective-permute-start | bytes 1769480 | tf_op jit(solution)/shard_map/ppermute | solution.py:1214
  351.4 17.9 %collective-permute-start.13 = (bf16[224,768]{1,0:T(8,128)(2,1)}, bf16[224,768]{1,0:T(8,128)(2,1)S(1)}, u32[]{:S(2)}, u32[]{:S(2)}) collective-permute-start(bf16[224,768]{1,0:T(8,128)(2,1)} %get-tuple-element.270), channel_id=1, source_target_pairs={{0,16},{4,20},{8,24},{12,28},{16,0},{20,4},{24,8},{28,12},{1,17},{... | collective-permute-start | bytes 1032200 | tf_op jit(solution)/shard_map/ppermute | solution.py:1210
  351.6 17.7 %collective-permute-start.16 = (bf16[4,96,384]{2,1,0:T(8,128)(2,1)S(1)}, bf16[4,96,384]{2,1,0:T(8,128)(2,1)S(1)}, u32[]{:S(2)}, u32[]{:S(2)}) collective-permute-start(bf16[4,96,384]{2,1,0:T(8,128)(2,1)S(1)} %copy-done.42), channel_id=1, source_target_pairs={{0,4},{4,0},{8,12},{12,8},{16,20},{20,16},{24,28},{28,24},{1,5},{5... | collective-permute-start | bytes 884744 | tf_op jit(solution)/shard_map/ppermute | solution.py:1214
  384.6 24.7 %collective-permute-start.19 = (bf16[4,240,384]{2,1,0:T(8,128)(2,1)}, bf16[4,240,384]{2,1,0:T(8,128)(2,1)S(1)}, u32[]{:S(2)}, u32[]{:S(2)}) collective-permute-start(bf16[4,240,384]{2,1,0:T(8,128)(2,1)} %get-tuple-element.296), channel_id=1, source_target_pairs={{0,4},{4,0},{8,12},{12,8},{16,20},{20,16},{24,28},{28,24},{1,5},{5... | collective-permute-start | bytes 2211848 | tf_op jit(solution)/shard_map/ppermute | solution.py:1214
  389.3 19.9 %collective-permute-start.20 = (bf16[2,384,384]{2,1,0:T(8,128)(2,1)}, bf16[2,384,384]{2,1,0:T(8,128)(2,1)S(1)}, u32[]{:S(2)}, u32[]{:S(2)}) collective-permute-start(bf16[2,384,384]{2,1,0:T(8,128)(2,1)} %get-tuple-element.304), channel_id=1, source_target_pairs={{0,8},{4,12},{8,0},{12,4},{16,24},{20,28},{24,16},{28,20},{1,9},{5... | collective-permute-start | bytes 1769480 | tf_op jit(solution)/shard_map/ppermute | solution.py:1214
  412.5 27.9 %collective-permute-start.24 = (bf16[2,240,384]{2,1,0:T(8,128)(2,1)}, bf16[2,240,384]{2,1,0:T(8,128)(2,1)S(1)}, u32[]{:S(2)}, u32[]{:S(2)}) collective-permute-start(bf16[2,240,384]{2,1,0:T(8,128)(2,1)} %get-tuple-element.314), channel_id=1, source_target_pairs={{0,8},{4,12},{8,0},{12,4},{16,24},{20,28},{24,16},{28,20},{1,9},{5... | collective-permute-start | bytes 1105928 | tf_op jit(solution)/shard_map/ppermute | solution.py:1214
  415.2 25.2 %collective-permute-start.23 = (bf16[1,576,192]{2,1,0:T(8,128)(2,1)}, bf16[1,576,192]{2,1,0:T(8,128)(2,1)S(1)}, u32[]{:S(2)}, u32[]{:S(2)}) collective-permute-start(bf16[1,576,192]{2,1,0:T(8,128)(2,1)} %get-tuple-element.310), channel_id=1, source_target_pairs={{0,2},{1,3},{2,0},{3,1},{4,6},{5,7},{6,4},{7,5},{8,10},{9,11},{10,... | collective-permute-start | bytes 663560 | tf_op jit(solution)/shard_map/ppermute | solution.py:1214
  418.8 21.6 %collective-permute-start.26 = (bf16[1,384,384]{2,1,0:T(8,128)(2,1)}, bf16[1,384,384]{2,1,0:T(8,128)(2,1)S(1)}, u32[]{:S(2)}, u32[]{:S(2)}) collective-permute-start(bf16[1,384,384]{2,1,0:T(8,128)(2,1)} %get-tuple-element.320), channel_id=1, source_target_pairs={{0,16},{4,20},{8,24},{12,28},{16,0},{20,4},{24,8},{28,12},{1,17},{... | collective-permute-start | bytes 884744 | tf_op jit(solution)/shard_map/ppermute | solution.py:1214
  420.7 19.7 %collective-permute-start.22 = (bf16[128,768]{1,0:T(8,128)(2,1)S(1)}, bf16[128,768]{1,0:T(8,128)(2,1)S(1)}, u32[]{:S(2)}, u32[]{:S(2)}) collective-permute-start(bf16[128,768]{1,0:T(8,128)(2,1)S(1)} %get-tuple-element.396), channel_id=1, source_target_pairs={{0,16},{4,20},{8,24},{12,28},{16,0},{20,4},{24,8},{28,12},{1,17},{... | collective-permute-start | bytes 589832 | tf_op jit(solution)/shard_map/ppermute | solution.py:1024
  445.3 20.6 %collective-permute-start.32 = (bf16[3,96,192]{2,1,0:T(8,128)(2,1)}, bf16[3,96,192]{2,1,0:T(8,128)(2,1)S(1)}, u32[]{:S(2)}, u32[]{:S(2)}) collective-permute-start(bf16[3,96,192]{2,1,0:T(8,128)(2,1)} %bitcast.167), channel_id=1, source_target_pairs={{0,4},{1,12},{2,20},{3,28},{4,5},{5,13},{6,21},{7,29},{8,6},{9,14}... | collective-permute-start | bytes 331784 | tf_op jit(solution)/shard_map/ppermute | solution.py:1355
  446.4 19.5 %collective-permute-start.31 = (bf16[3,96,192]{2,1,0:T(8,128)(2,1)}, bf16[3,96,192]{2,1,0:T(8,128)(2,1)S(1)}, u32[]{:S(2)}, u32[]{:S(2)}) collective-permute-start(bf16[3,96,192]{2,1,0:T(8,128)(2,1)} %bitcast.166), channel_id=1, source_target_pairs={{0,0},{1,8},{2,16},{3,24},{4,1},{5,9},{6,17},{7,25},{8,2},{9,10},{... | collective-permute-start | bytes 331784 | tf_op jit(solution)/shard_map/ppermute | solution.py:1355
  (61 other events, 535.1 us)
Sparse Core Ops, SparseCore 0:
  221.2 77.1 reduce-scatter.1

commit v4 on v3

--- a/solution.py
+++ b/solution.py
@@ -83,40 +83,6 @@
         cost_estimate=estimate(flops=0, bytes_accessed=0, transcendentals=0),
         name="fold",
     )(bit, *[split(array) for k, g in pairs for array in (k, g, k, g)])
-
-
-def evens(array, bit, sizes):
-    count, rows, width = array.shape
-    half = count // 2
-
-    def kernel(s_ref, here_ref, there_ref, *out_refs):
-        start = 0
-        for i, size in enumerate(sizes):
-            for side, ref in enumerate((here_ref, there_ref)):
-                out_refs[2 * i + side][...] = ref[:, 0, start : start + size]
-            start += size
-
-    spec = lambda side: pl.BlockSpec(
-        (half, 1, rows, width), lambda j, s: (0, (s[0] + side) % 2, 0, 0)
-    )
-    out = lambda size: pl.BlockSpec((half, size, width), lambda j, s: (0, 0, 0))
-    split = array.reshape(half, 2, rows, width)
-    outs = pl.pallas_call(
-        kernel,
-        grid_spec=pltpu.PrefetchScalarGridSpec(
-            num_scalar_prefetch=1,
-            grid=(1,),
-            in_specs=[spec(0), spec(1)],
-            out_specs=[out(size) for size in sizes for _ in range(2)],
-        ),
-        out_shape=[
-            jax.ShapeDtypeStruct((half, size, width), BF16) for size in sizes for _ in range(2)
-        ],
-        compiler_params=params(),
-        cost_estimate=estimate(flops=0, bytes_accessed=0, transcendentals=0),
-        name="evens",
-    )(bit, split, split)
-    return list(zip(outs[::2], outs[1::2]))
 
 
 def weight_chunks(kernel_dots, operands, specs, core, slot, columns, blocks, width):
@@ -188,21 +154,21 @@
     )(keys, values, weights)
 
 
-def unpacked(hidden, late, size, piece):
+def unpacked(early, late, size, piece):
     half = size // 2
 
-    def kernel(hk_ref, hg_ref, lk_ref, lg_ref, in_ref, out_ref, kv_ref, co_ref, cq_ref, so_ref):
-        first = hk_ref[...].astype(F32) + hg_ref[...].astype(F32)
+    def kernel(e_ref, lk_ref, lg_ref, in_ref, out_ref, kv_ref, co_ref, cq_ref, so_ref):
+        first = e_ref[...].astype(F32)
         in_ref[...] = jnp.concatenate([first[:size], first[size : 2 * size]], axis=1)
-        turned = first[2 * size :].T
+        turned = first[2 * size : 4 * size].T
         out_ref[...] = jnp.concatenate([turned[:piece], turned[piece:]], axis=1)
+        co_ref[:half, :] = first[4 * size :, :piece]
+        co_ref[half:, :] = first[4 * size :, piece:]
         second = lk_ref[...].astype(F32) + lg_ref[...].astype(F32)
         kv_ref[0] = second[:size, :piece]
         kv_ref[1] = second[:size, piece:]
-        co_ref[:half, :] = second[size : size + half, :piece]
-        co_ref[half:, :] = second[size : size + half, piece:]
-        cq_ref[...] = second[size + half :, :piece]
-        so_ref[...] = second[size + half :, piece:]
+        cq_ref[...] = second[size:, :piece]
+        so_ref[...] = second[size:, piece:]
 
     flat = lambda *shape: jax.ShapeDtypeStruct(shape, F32)
     outs = pl.pallas_call(
@@ -218,7 +184,7 @@
         compiler_params=params(),
         cost_estimate=estimate(flops=0, bytes_accessed=0, transcendentals=0),
         name="unpacked",
-    )(*hidden, *late)
+    )(early, *late)
     return (outs[0], outs[1].T) + tuple(outs[2:])
 
 
@@ -352,7 +318,7 @@
     )(query, *pairs, *pairs, *bias)
 
 
-def cross_backward(query, pairs, prob, grads, weight, delta, width, groups):
+def cross_backward(query, pairs, prob, place, grads, tops, earlier, width, groups):
     heads = width // HEAD_DIM
     length = query.shape[1]
     tokens = length // groups
@@ -361,24 +327,31 @@
     starts = [sum(rows[:i]) for i in range(parts)]
     total = sum(rows)
     pair = 2
-    sources = [rows[0], total - rows[0]]
-    where = [(0, 0)] + [(1, start - rows[0]) for start in starts[1:]]
+    stat_rows = grads.shape[1] - width
+    each = stat_rows // 4
 
     def kernel(*refs):
         q_ref = refs[0]
         k_refs = refs[1 : 1 + parts]
         v_refs = refs[1 + parts : 1 + 2 * parts]
-        p_ref, g_ref, w_ref, d_ref = refs[1 + 2 * parts : 5 + 2 * parts]
-        dq_ref = refs[5 + 2 * parts]
-        dk_refs = refs[6 + 2 * parts : 8 + 2 * parts]
-        dv_refs = refs[8 + 2 * parts :]
+        p_ref, g_ref, s_ref, t_ref = refs[1 + 2 * parts : 5 + 2 * parts]
+        dq_ref, dk_ref, dv_ref = refs[-3:]
+        step = pl.program_id(0)
+        stats = jnp.concatenate([s_ref[g] for g in range(groups)], axis=1).astype(F32)
+        lse = stats[:each] + stats[each : 2 * each]
+        delta = stats[2 * each : 3 * each] + stats[3 * each :]
+        row = lax.broadcasted_iota(jnp.int32, (each, length), 0)
         key_out = [[] for _ in range(parts)]
         value_out = [[] for _ in range(parts)]
         for j in range(pair):
             at = slice(j * HEAD_DIM, (j + 1) * HEAD_DIM)
             grad = jnp.concatenate([g_ref[g, at, :] for g in range(groups)], axis=1).astype(F32)
-            scaled = grad * w_ref[j]
-            high, low = split_low(-d_ref[j])
+            pick = lambda x: jnp.sum(
+                jnp.where(row == step * pair + j, x, 0.0), axis=0, keepdims=True
+            )
+            scale = jnp.exp(t_ref[j] - pick(lse))
+            scaled = grad * scale
+            high, low = split_low(-pick(delta) * scale)
             scaled_low = scaled.astype(BF16)
             pad = jnp.zeros((14, length), BF16)
             aug = jnp.concatenate([scaled_low, high, low, pad], axis=0)
@@ -395,34 +368,42 @@
                 key_out[i].append(dot(score, query_rows, 1, 0).astype(BF16))
                 term = dot(k_refs[i][0, at, :], score, 1, 0)
                 query_grad = term if query_grad is None else query_grad + term
-            query_low = (query_grad * 0.125).astype(BF16)
+            query_grad = query_grad * 0.125
+            if earlier is not None:
+                before = refs[5 + 2 * parts]
+                query_grad += jnp.concatenate(
+                    [before[g, at, :] for g in range(groups)], axis=1
+                ).astype(F32)
+            query_low = query_grad.astype(BF16)
             for g in range(groups):
                 dq_ref[g, at, :] = query_low[:, g * tokens : (g + 1) * tokens]
         for i in range(parts):
-            source, start = where[i]
-            at = slice(start, start + rows[i])
-            dk_refs[source][at, :] = jnp.concatenate(key_out[i], axis=1)
-            dv_refs[source][at, :] = jnp.concatenate(value_out[i], axis=1)
+            at = slice(starts[i], starts[i] + rows[i])
+            dk_ref[at, :] = jnp.concatenate(key_out[i], axis=1)
+            dv_ref[at, :] = jnp.concatenate(value_out[i], axis=1)
 
     size = pair * HEAD_DIM
     key_specs = [pl.BlockSpec((1, size, r), lambda h: (0, h, 0)) for r in rows]
     value_specs = [pl.BlockSpec((1, size, r), lambda h: (1, h, 0)) for r in rows]
-    kv_grads = [pl.BlockSpec((r, size), lambda h: (0, h)) for r in sources]
-    outs = pl.pallas_call(
+    token_spec = pl.BlockSpec((groups, size, tokens), lambda h: (0, h, 0))
+    row_spec = pl.BlockSpec((total, size), lambda h: (0, h))
+    more = [] if earlier is None else [earlier]
+    return pl.pallas_call(
         kernel,
         grid=(heads // pair,),
         in_specs=[pl.BlockSpec((size, length), lambda h: (h, 0))]
         + key_specs
         + value_specs
         + [
-            pl.BlockSpec((pair, total, length), lambda h: (h, 0, 0)),
-            pl.BlockSpec((groups, size, tokens), lambda h: (0, h, 0)),
+            pl.BlockSpec((pair, total, length), lambda h: (h, place, 0)),
+            token_spec,
+            pl.BlockSpec((groups, stat_rows, tokens), lambda h: (0, width // stat_rows, 0)),
             pl.BlockSpec((pair, 1, length), lambda h: (h, 0, 0)),
-            pl.BlockSpec((pair, 1, length), lambda h: (h, 0, 0)),
-        ],
-        out_specs=[pl.BlockSpec((groups, size, tokens), lambda h: (0, h, 0))] + kv_grads + kv_grads,
+        ]
+        + [token_spec for _ in more],
+        out_specs=[token_spec, row_spec, row_spec],
         out_shape=[jax.ShapeDtypeStruct((groups, width, tokens), BF16)]
-        + [jax.ShapeDtypeStruct((r, width), BF16) for r in sources] * 2,
+        + [jax.ShapeDtypeStruct((total, width), BF16)] * 2,
         compiler_params=params(),
         cost_estimate=estimate(
             flops=32 * heads * total * length * HEAD_DIM,
@@ -430,8 +411,7 @@
             transcendentals=0,
         ),
         name="cross_backward",
-    )(query, *pairs, *pairs, prob, grads, weight, delta)
-    return outs[0], list(outs[1:3]), list(outs[3:5])
+    )(query, *pairs, *pairs, prob, grads, grads, tops, *more)
 
 
 def self_forward(inputs, gain, weights, key_pos, query_pos, groups):
@@ -713,14 +693,14 @@
     )(parts, after_self, cross_out, gain, ffn_in, ffn_out, cotangent)
 
 
-def hidden_weight_grads(low, pre_grad, act, cotangent, columns, blocks):
+def early_weight_grads(low, pre_grad, act, cotangent, mixed, mixed_grad, columns, blocks):
     tokens, width = low.shape
     hidden = act.shape[1]
     step_size = hidden // blocks
     size, piece = width // blocks, width // columns
     half = step_size // 2
 
-    def kernel(a_ref, du_ref, z_ref, c_ref, out_ref):
+    def kernel(a_ref, du_ref, z_ref, c_ref, m_ref, g_ref, out_ref):
         step = pl.program_id(0)
         first = dot(a_ref[...], du_ref[...], 0, 0).astype(BF16)
         for p in range(2):
@@ -735,11 +715,17 @@
         second = dot(z_ref[...], c_ref[...], 0, 0).astype(BF16)
         for d in range(columns):
             at = slice(d * piece, (d + 1) * piece)
-            out_ref[d, step, 2 * size :, :] = jnp.concatenate(
+            out_ref[d, step, 2 * size : 2 * size + half, :] = jnp.concatenate(
                 [second[:half, at], second[half:, at]], axis=1
             )
-
-    shape = (columns, blocks, 2 * size + half, 2 * piece)
+        third = dot(m_ref[...], g_ref[...], 1, 0).astype(BF16)
+        for d in range(columns):
+            at = slice(d * piece, (d + 1) * piece)
+            out_ref[d, step, 2 * size + half :, :] = jnp.concatenate(
+                [third[: size // 2, at], third[size // 2 :, at]], axis=1
+            )
+
+    shape = (columns, blocks, 2 * size + half + size // 2, 2 * piece)
     whole = lambda *shape: pl.BlockSpec(shape, lambda i: (0,) * len(shape))
     return pl.pallas_call(
         kernel,
@@ -749,6 +735,8 @@
             pl.BlockSpec((tokens, step_size), lambda i: (0, i)),
             pl.BlockSpec((tokens, step_size), lambda i: (0, i)),
             whole(tokens, width),
+            pl.BlockSpec((size, tokens), lambda i: (i, 0)),
+            whole(tokens, width),
         ],
         out_specs=whole(*shape),
         out_shape=jax.ShapeDtypeStruct(shape, BF16),
@@ -758,8 +746,8 @@
             bytes_accessed=4 * width * hidden,
             transcendentals=0,
         ),
-        name="hidden_weight_grads",
-    )(low, pre_grad, act, cotangent)
+        name="early_weight_grads",
+    )(low, pre_grad, act, cotangent, mixed, mixed_grad)
 
 
 def mixed_stage(parts, cross_q, after_self, gain, cross_grad, self_out, groups, own):
@@ -880,25 +868,24 @@
     )(mine, own, *pieces)
 
 
-def own_weight_grads(low, gain, grads, weights, core, columns, blocks):
+def own_weight_grads(low, gain, grads, weights, column, columns, blocks):
     length, width = low.shape
     groups, _, own, tokens = grads.shape
     rows = width // blocks
     per = blocks // columns
 
-    def kernel(c_ref, a_ref, g_ref, d_ref, w_ref, kept_ref, sent_ref, gain_ref):
+    def kernel(c_ref, a_ref, g_ref, d_ref, w_ref, *refs):
+        gain_ref = refs[-1]
         step = pl.program_id(0)
         grads = jnp.concatenate([d_ref[g, 0] for g in range(groups)], axis=1)
         turned = dot(grads, a_ref[...], 1, 0)
         weight = turned.T.astype(BF16)
-        for bit in range(2):
-
-            @pl.when(c_ref[0] == bit)
+        for d in range(columns):
+
+            @pl.when(c_ref[0] == d)
             def put():
                 for b in range(blocks):
-                    column = b // per
-                    ref = kept_ref if column % 2 == bit else sent_ref
-                    ref[column // 2, b % per, 0] = weight[b * rows : (b + 1) * rows]
+                    refs[b // per ^ d][b % per, 0] = weight[b * rows : (b + 1) * rows]
 
         term = jnp.sum(turned * w_ref[0].astype(F32), axis=0, keepdims=True) / g_ref[...]
 
@@ -910,9 +897,9 @@
         def more():
             gain_ref[...] += term
 
-    shape = (columns // 2, per, 3, rows, own)
+    shape = (per, 3, rows, own)
     whole = lambda *shape: pl.BlockSpec(shape, lambda i, c: (0,) * len(shape))
-    part = pl.BlockSpec((columns // 2, per, 1, rows, own), lambda i, c: (0, 0, i, 0, 0))
+    part = pl.BlockSpec((per, 1, rows, own), lambda i, c: (0, i, 0, 0))
     return pl.pallas_call(
         kernel,
         grid_spec=pltpu.PrefetchScalarGridSpec(
@@ -924,15 +911,65 @@
                 pl.BlockSpec((groups, 1, own, tokens), lambda i, c: (0, i, 0, 0)),
                 pl.BlockSpec((1, own, width), lambda i, c: (i, 0, 0)),
             ],
-            out_specs=[part, part, whole(1, width)],
-        ),
-        out_shape=[jax.ShapeDtypeStruct(shape, BF16)] * 2 + [jax.ShapeDtypeStruct((1, width), F32)],
+            out_specs=[part] * columns + [whole(1, width)],
+        ),
+        out_shape=[jax.ShapeDtypeStruct(shape, BF16)] * columns
+        + [jax.ShapeDtypeStruct((1, width), F32)],
         compiler_params=params(),
         cost_estimate=estimate(
             flops=12 * length * width * own, bytes_accessed=4 * length * width, transcendentals=0
         ),
         name="own_weight_grads",
-    )(core, low, gain, grads, weights)
+    )(column, low, gain, grads, weights)
+
+
+def sums_for(pairs, groups):
+    blocks, _, width = pairs[0][0].shape
+    rows = [k.shape[1] for k, _ in pairs]
+    high = blocks // groups
+
+    def kernel(*refs):
+        out_ref = refs[-1]
+        start = 0
+        for i, size in enumerate(rows):
+            both = refs[2 * i][...].astype(F32) + refs[2 * i + 1][...].astype(F32)
+            both = both.astype(BF16)
+            for b in range(blocks):
+                out_ref[b % groups, b // groups, start : start + size, :] = both[b]
+            start += size
+
+    return pl.pallas_call(
+        kernel,
+        out_shape=jax.ShapeDtypeStruct((groups, high, sum(rows), width), BF16),
+        compiler_params=params(),
+        cost_estimate=estimate(flops=0, bytes_accessed=0, transcendentals=0),
+        name="sums_for",
+    )(*[array for pair in pairs for array in pair])
+
+
+def sums_of(arrays, bit):
+    _, rows, width = arrays[0].shape
+
+    def kernel(s_ref, *refs):
+        for side in range(2):
+            terms = [refs[2 * i + side][0].astype(F32) for i in range(len(arrays))]
+            refs[2 * len(arrays) + side][...] = functools.reduce(jnp.add, terms).astype(BF16)
+
+    spec = lambda side: pl.BlockSpec((1, rows, width), lambda j, s: ((s[0] + side) % 2, 0, 0))
+    out = pl.BlockSpec((rows, width), lambda j, s: (0, 0))
+    return pl.pallas_call(
+        kernel,
+        grid_spec=pltpu.PrefetchScalarGridSpec(
+            num_scalar_prefetch=1,
+            grid=(1,),
+            in_specs=[spec(side) for _ in arrays for side in range(2)],
+            out_specs=[out] * 2,
+        ),
+        out_shape=[jax.ShapeDtypeStruct((rows, width), BF16)] * 2,
+        compiler_params=params(),
+        cost_estimate=estimate(flops=0, bytes_accessed=0, transcendentals=0),
+        name="sums_of",
+    )(bit, *[array for array in arrays for _ in range(2)])
 
 
 def self_backward(projected, mixed, grads, prob, weight, groups):
@@ -1122,7 +1159,6 @@
         came += [first, second, third]
 
     part_mix, cross_prob, local_top = cross_forward(cross_query, pairs, bias, width, groups)
-    stat_rows = (part_mix.shape[1] - width) // 2
 
     own_cotangent = gathered(cotangent)
     (
@@ -1168,8 +1204,15 @@
         and blocks == 8
     )
     if staged:
-        chunks = hidden_weight_grads(
-            third_low, pre_low, hidden_low, own_cotangent, columns, blocks
+        chunks = early_weight_grads(
+            third_low,
+            pre_low,
+            hidden_low,
+            own_cotangent,
+            cross_mix,
+            cross_grad_low,
+            columns,
+            blocks,
         )
         packed, chunks, own_output = lax.optimization_barrier((packed, chunks, own_output))
         inner = chunks.shape[2:]
@@ -1180,34 +1223,32 @@
         in_chunks = dot(third_low, pre_low, 0, 0).astype(BF16)
         in_chunks = in_chunks.reshape(blocks, width // blocks, columns, -1).transpose(2, 0, 1, 3)
         out_chunks = by_rows(dot(hidden_low, own_cotangent, 0, 0))
+    together = lambda *values: lax.optimization_barrier(values)
+
     output_parts = leaving(own_output)
 
-    def whole_rows(start):
-        rows = packed[:, start : start + 2 * stat_rows].astype(F32)
-        rows = (rows[:, :stat_rows] + rows[:, stat_rows:])[:, :heads]
-        return rows.transpose(1, 0, 2).reshape(heads, 1, length)
-
-    scale = jnp.exp(local_top - whole_rows(width))
-    query_parts, key_low, value_low = cross_backward(
-        cross_query,
-        pairs,
-        cross_prob,
-        packed,
-        scale,
-        whole_rows(width + 2 * stat_rows) * scale,
-        width,
-        groups,
-    )
-    query_parts, output_parts = lax.optimization_barrier((query_parts, output_parts))
-    joined = traded(query_parts)
-    shares = [0, 7, 11, 15, 22, 28]
+    def rows_backward(place, subset, earlier):
+        return cross_backward(
+            cross_query, subset, cross_prob, place, packed, local_top, earlier, width, groups
+        )
+
+    shares = [0, 11, 19, 23, 28]
     marks = [enc_rows * share // 28 for share in shares]
-    pieces = row_grads(key_low[1], value_low[1], cross_kv, marks)
-    here = jnp.full((1,), mine, jnp.int32)
-    together = lambda *values: lax.optimization_barrier(values)
+    part_grads, came_key, came_value = rows_backward(1, pairs[1:], None)
+    pieces = row_grads(came_key, came_value, cross_kv, marks)
 
     def sent_back(piece):
         return lax.ppermute(piece, "blk", shifted(1))
+
+    part_grads, pieces, output_parts = together(part_grads, pieces, output_parts)
+    back_1 = sent_back(pieces[0])
+    query_parts, own_key, own_value = rows_backward(0, pairs[:1], part_grads)
+    key_low, value_low = [own_key, came_key], [own_value, came_value]
+    query_parts, key_low, value_low, back_1, pieces = together(
+        query_parts, key_low, value_low, back_1, pieces
+    )
+    joined = traded(query_parts)
+    here = jnp.full((1,), mine, jnp.int32)
 
     def moved(array, axis, step):
         size = lax.axis_size(axis)
@@ -1221,7 +1262,7 @@
             kernel_dots, operands, specs, bit_of("dp", 1), slot, columns, blocks, width
         )
 
-    back_1 = sent_back(pieces[0])
+    back_2 = sent_back(pieces[1])
     output = returned(output_parts)
     if staged:
         cuts = [0]
@@ -1238,37 +1279,32 @@
             return one
 
         count = 1 + len(came)
-        operands = [own_rows_low, *came, *key_low, *value_low, cross_mix, cross_grad_low]
+        operands = [own_rows_low, *came, *key_low, *value_low]
         kept_1, sent_1 = chunks_of(
             [
                 rows_dot(count),
                 rows_dot(count + 2),
-                lambda refs: dot(refs[count + 4][...], refs[count + 5][...], 1, 0),
             ],
             operands,
             [None] * len(operands),
         )
-        joined, pieces, back_1, output, hidden, kept_1, sent_1 = together(
-            joined, pieces, back_1, output, hidden, kept_1, sent_1
-        )
+        joined, pieces, back_2, output, hidden, kept_1, sent_1 = together(
+            joined, pieces, back_2, output, hidden, kept_1, sent_1
+        )
+        hidden = lax.psum_scatter(hidden, "blk", scatter_dimension=0, tiled=True)
         got_1 = moved(sent_1, "dp", 1)
     query_grad, self_grad, self_grad_low, mixed_grad, gain_two = mixed_stage(
         joined, cross_q, after_self, gain_rows[1], cross_grad, padded_out, groups, own
     )
     if staged:
-        (
-            query_grad, self_grad, self_grad_low, mixed_grad, gain_two, kept_1, got_1, pieces, hidden,
-        ) = together(
-            query_grad, self_grad, self_grad_low, mixed_grad, gain_two, kept_1, got_1, pieces, hidden,
+        query_grad, self_grad, self_grad_low, mixed_grad, gain_two, kept_1, got_1, pieces = (
+            together(
+                query_grad, self_grad, self_grad_low, mixed_grad, gain_two, kept_1, got_1, pieces
+            )
         )
     own_mixed = traded(mixed_grad)
     if staged:
-        back_2 = sent_back(pieces[1])
-        shares = [inner[0] // 3, inner[0] * 5 // 12, inner[0] // 4]
-        (kept_i, sent_i), (kept_o, sent_o), (kept_u, sent_u) = evens(
-            hidden.reshape((blocks,) + inner), bit_of("blk", 1), shares
-        )
-        got_i = moved(sent_i, "blk", 1)
+        back_3 = sent_back(pieces[2])
         kept_1, sent_1 = fold([(kept_1, got_1)], bit_of("dp", 2), blocks)
         operands = [second_low, query_grad, self_mix, self_grad_low]
         specs = [None] * 2
@@ -1281,69 +1317,50 @@
             operands,
             specs,
         )
-        (
-            own_mixed, back_2, kept_i, got_i, kept_o, sent_o, kept_1, sent_1, kept_2, sent_2, pieces,
-            kept_u, sent_u,
-        ) = together(
-            own_mixed, back_2, kept_i, got_i, kept_o, sent_o, kept_1, sent_1, kept_2, sent_2, pieces,
-            kept_u, sent_u,
-        )
-        got_o = moved(sent_o, "blk", 1)
+        own_mixed, back_3, kept_1, sent_1, kept_2, sent_2, pieces = together(
+            own_mixed, back_3, kept_1, sent_1, kept_2, sent_2, pieces
+        )
         got_1 = moved(sent_1, "dp", 2)
         got_2 = moved(sent_2, "dp", 1)
-        back_3 = sent_back(pieces[2])
     own_grads = self_backward(projected, sent_mix, own_mixed, self_prob, self_weight, groups)
     if staged:
-        own_grads, kept_o, got_o, kept_2, got_2, pieces, back_3, sent_u = together(
-            own_grads, kept_o, got_o, kept_2, got_2, pieces, back_3, sent_u
+        own_grads, kept_1, got_1, kept_2, got_2, pieces = together(
+            own_grads, kept_1, got_1, kept_2, got_2, pieces
         )
     back = traded(own_grads)
     if staged:
         back_4 = sent_back(pieces[3])
         kept_2, sent_2 = fold([(kept_2, got_2)], bit_of("dp", 2), blocks)
         got_2 = moved(sent_2, "dp", 2)
-        got_u = moved(sent_u, "blk", 1)
-        kept_w, sent_w, gain_one = own_weight_grads(
-            first_low, gain_rows[0], own_grads, own_qkv, bit_of("dp", 1), columns, blocks
+        *parts_w, gain_one = own_weight_grads(
+            first_low,
+            gain_rows[0],
+            own_grads,
+            own_qkv,
+            jnp.full((1,), lax.axis_index("dp"), jnp.int32),
+            columns,
+            blocks,
         )
         gains = jnp.concatenate([gain_one, gain_two, gain_three], axis=0)
-        (
-            back, back_4, kept_1, got_1, kept_2, got_2, kept_u, got_u, kept_w, sent_w, gains, pieces,
-        ) = together(
-            back, back_4, kept_1, got_1, kept_2, got_2, kept_u, got_u, kept_w, sent_w, gains, pieces,
+        back, back_4, kept_1, got_1, kept_2, got_2, parts_w, gains, key_low = together(
+            back, back_4, kept_1, got_1, kept_2, got_2, parts_w, gains, key_low
         )
     own_grad = input_stage(back, padded_qkv, all_inputs, gain_rows[0], self_grad, slot, groups)
     if staged:
-        back_5 = sent_back(pieces[4])
-        got_w = moved(sent_w, "dp", 1)
-        kept_j, sent_j = fold([(kept_1, got_1), (kept_2, got_2)], bit_of("blk", 1), 1)
-        got_j = moved(sent_j, "blk", 1)
-        kept_h, sent_h = fold(
-            [(kept_i, got_i), (kept_o, got_o), (kept_u, got_u)], bit_of("blk", 2), 1
-        )
-        got_h = moved(sent_h, "blk", 2)
+        late = traded(sums_for([(kept_1, got_1), (kept_2, got_2)], groups))
+        parts_w = [parts_w[0]] + [moved(p, "dp", r) for r, p in enumerate(parts_w) if r]
         gains = gains + moved(gains, "dp", 1)
-        own_grad, back_5, kept_w, got_w, kept_j, got_j, kept_h, got_h, gains, pieces, key_low = (
-            together(
-                own_grad, back_5, kept_w, got_w, kept_j, got_j, kept_h, got_h, gains, pieces, key_low
-            )
+        gains = gains + moved(gains, "dp", 2)
+        (enc_own,) = row_grads(key_low[0], value_low[0], cross_kv, [0, enc_rows])
+        enc_grad = both_queries(enc_own, [back_1, back_2, back_3, back_4], here)
+        own_grad, late, parts_w, gains, enc_grad = together(
+            own_grad, late, parts_w, gains, enc_grad
         )
     dec_parts = leaving(own_grad)
     if staged:
-        kept_h, sent_h = fold([(kept_h, got_h)], bit_of("blk", 4), 1)
-        got_h = moved(sent_h, "blk", 4)
-        flat = (columns // 2, -1, own)
-        kept_w, sent_w = fold([(kept_w.reshape(flat), got_w.reshape(flat))], bit_of("dp", 2), 1)
-        got_w = moved(sent_w, "dp", 2)
-        kept_j, sent_j = fold([(kept_j, got_j)], bit_of("blk", 2), 1)
-        got_j = moved(sent_j, "blk", 2)
-        gains = gains + moved(gains, "dp", 2)
-        dec_parts, kept_w, got_w, kept_j, got_j, gains, key_low, kept_h, got_h = together(
-            dec_parts, kept_w, got_w, kept_j, got_j, gains, key_low, kept_h, got_h
-        )
-        (enc_own,) = row_grads(key_low[0], value_low[0], cross_kv, [0, enc_rows])
-        flat = (seqs, -1, own)
-        halves = fold([(kept_w.reshape(flat), got_w.reshape(flat))], here, 1)
+        kept_j, sent_j = sums_of([late[g] for g in range(groups)], here)
+        got_j = moved(sent_j, "blk", groups)
+        halves = sums_of([p.reshape(seqs, -1, own) for p in parts_w], here)
         got_w = []
         for step, piece in enumerate(halves):
             pairs = []
@@ -1353,24 +1370,21 @@
                     pairs.append((b * columns + d, (d * seqs + row) * columns + b % groups))
             piece = piece.reshape(3, width // blocks, own)
             got_w.append(lax.ppermute(piece, ("blk", "dp"), pairs))
-        kept_j, sent_j = fold([(kept_j, got_j)], bit_of("blk", 4), 1)
-        got_j = moved(sent_j, "blk", 4)
+        gains = gains + moved(gains, "blk", 1)
+        gains = gains + moved(gains, "blk", 2)
+        dec_parts, kept_j, got_j, got_w, gains = together(
+            dec_parts, kept_j, got_j, got_w, gains
+        )
+        gain_grads = gains + moved(gains, "blk", 4)
         dec_grad = returned(dec_parts)
-        gains = gains + moved(gains, "blk", 1)
-        kept_j, got_j, dec_grad, gains, enc_own = together(
-            kept_j, got_j, dec_grad, gains, enc_own
-        )
-        enc_grad = both_queries(enc_own, [back_1, back_2, back_3, back_4, back_5], here)
         qkv = sum(piece.astype(F32) for piece in got_w)
-        gains = gains + moved(gains, "blk", 2)
-        gain_grads = gains + moved(gains, "blk", 4)
         ffn_in_own, ffn_out_own, kv_own, cross_out_own, cross_q_own, self_out_own = unpacked(
-            (kept_h[0], got_h[0]), (kept_j[0], got_j[0]), width // blocks, width // columns
+            hidden, (kept_j, got_j), width // blocks, width // columns
         )
     else:
-        rest = sent_back(jnp.concatenate(pieces[1:], axis=0))
+        rest = sent_back(jnp.concatenate(pieces[2:], axis=0))
         (enc_own,) = row_grads(key_low[0], value_low[0], cross_kv, [0, enc_rows])
-        enc_grad = both_queries(enc_own, [back_1, rest], here)
+        enc_grad = both_queries(enc_own, [back_1, back_2, rest], here)
         own_rows = lambda array: lax.dynamic_slice_in_dim(array, slot_of * tokens, tokens, 0)
         full = back.transpose(1, 0, 2, 3).reshape(3, padded, tokens)[:, :width]
         first_back = sum(dot(full[c], self_qkv[c], 0, 1) for c in range(3))

time: 488 us -> 465 us (0.953)
  waiting for transfers between devices: 135 us -> 120 us
  Pallas kernels: 226 us -> 216 us
  starting transfers between devices: 64.4 us -> 70.4 us
    ppermute x19 -> x13, waiting for transfers between devices: 35.6 us -> 13.2 us  [moved(): return lax.ppermute(array, axis, [(i, i ^ step) for i in range(size)])]
    pallas_call x9 -> x2, Pallas kernels: 23.1 us -> 5.71 us  [fold(): pl.pallas_call(kernel, grid_spec=pltpu.PrefetchScalarGridSpec(num_scalar_...]
    ppermute x4, waiting for transfers between devices: 43.3 us -> 28.4 us  [exchange(): lax.ppermute(pieces(lax.rem(mine + step, seqs)), 'blk', shifted(step))]
    ppermute x5 -> x4, waiting for transfers between devices: 19.1 us -> 32.3 us  [sent_back(): return lax.ppermute(piece, 'blk', shifted(1))]
    all_to_all x6 -> x7, waiting for transfers between devices: 31.2 us -> 37.4 us  [traded(): return lax.all_to_all(array, 'blk', 0, 0, axis_index_groups=members)]
    pallas_call x2 -> x4, Pallas kernels: 16.1 us -> 21 us  [the longest x1 13.3 us: early_weight_grads(): pl.pallas_call(kernel, grid=(blocks,), in_specs=[whole(tokens, width), pl...]
    all_to_all x6 -> x7, starting transfers between devices: 23.2 us -> 27.8 us  [traded(): return lax.all_to_all(array, 'blk', 0, 0, axis_index_groups=members)]
    pallas_call x1 -> x2, Pallas kernels: 48.8 us -> 52.1 us  [cross_backward(): pl.pallas_call(kernel, grid=(heads // pair,), in_specs=[pl.BlockSpec((siz...]
  transfers between devices with their start and end apart: 41 -> 36, of which waited for: 19 -> 17; matrix products, arithmetic and copies ran while one was open for 5% -> 6% of each run, Pallas kernels for 36% -> 36%
where the time goes in v4:
time: 465 us; the launch traced here: 458 us
  Pallas kernels  216 us (46%)
  waiting for transfers between devices  120 us (26%)
  starting transfers between devices  70.4 us (15%)
  local copies, waits for them, and re-layouts  32.2 us (7%)
  between operations  14.7 us (3%)
  other arithmetic  5 us (1%)
    pallas_call x2, Pallas kernels, cross_backward(): pl.pallas_call(kernel, grid=(heads // pair,), in_specs=[pl.BlockSpec((siz...  52.1 us
    all_to_all x7, waiting for transfers between devices, traded(): return lax.all_to_all(array, 'blk', 0, 0, axis_index_groups=members)  37.4 us
    ppermute x4, waiting for transfers between devices, sent_back(): return lax.ppermute(piece, 'blk', shifted(1))  32.3 us
    ppermute x4, waiting for transfers between devices, exchange(): lax.ppermute(pieces(lax.rem(mine + step, seqs)), 'blk', shifted(step))  28.4 us
    pallas_call x1, Pallas kernels, cross_forward(): pl.pallas_call(kernel, grid=(heads,), in_specs=[pl.BlockSpec((HEAD_DIM, l...  28.4 us
    all_to_all x7, starting transfers between devices, traded(): return lax.all_to_all(array, 'blk', 0, 0, axis_index_groups=members)  27.8 us
    unnamed x75, local copies, waits for them, and re-layouts  19.5 us
    pallas_call x1, Pallas kernels, token_stage(): pl.pallas_call(kernel, grid=(steps,), in_specs=[whole(*parts.shape), whol...  16.9 us
  transfers between devices with their start and end apart: 36, of which 17 were waited for; matrix products, arithmetic and copies ran while one was open for 6% of the time, Pallas kernels for 36%

profile of v4, /device:TPU:0, one launch (start us, length us, event | category | flops | bytes accessed | tf_op | source)
XLA Modules:
  0.0 457.8 jit_solution(10229705777453882412)
XLA Ops:
  12.4 9.1 %collective-permute-done = bf16[128,768]{1,0:T(8,128)(2,1)S(1)} collective-permute-done((bf16[128,768]{1,0:T(8,128)(2,1)S(1)}, bf16[128,768]{1,0:T(8,128)(2,1)S(1)}, u32[]{:S(2)}, u32[]{:S(2)}) %collective-permute-start) | collective-permute-done | bytes 196640 | tf_op jit(solution)/shard_map/ppermute | solution.py:1061
  38.4 5.6 %project_rows.3.refs_1_.refs_4_.refs_2_ = bf16[2,768,896]{2,1,0:T(8,128)(2,1)} custom-call(bf16[896,768]{1,0:T(8,128)(2,1)} %dynamic-slice_bitcast_fusion.refs_0_, bf16[2,768,768]{2,1,0:T(8,128)(2,1)} %bitcast.76), custom_call_target="tpu_custom_call" | custom-call | flops 2 | bytes 1 | tf_op jit(solution)/shard_map/project_rows/pallas_call | solution.py:492
  49.9 6.1 %collective-permute-done.1.refs_0_.refs_1_ = bf16[384,768]{1,0:T(8,128)(2,1)S(1)} collective-permute-done((bf16[384,768]{1,0:T(8,128)(2,1)}, bf16[384,768]{1,0:T(8,128)(2,1)S(1)}, u32[]{:S(2)}, u32[]{:S(2)}) %collective-permute-start.1) | collective-permute-done | bytes 589856 | tf_op jit(solution)/shard_map/ppermute | solution.py:1108
  61.1 11.8 %self_forward.1 = (bf16[1024,768]{1,0:T(8,128)(2,1)}, bf16[3,192,1024]{2,1,0:T(8,128)(2,1)}, bf16[4,192,1024]{2,1,0:T(8,128)(2,1)}, bf16[3,1024,1024]{2,1,0:T(8,128)(2,1)}, f32[3,1,1024]{2,1,0:T(1,128)}) custom-call(bf16[1024,768]{1,0:T(8,128)(2,1)} %bitcast.79, f32[1,768]{1,0:T(1,128)} %get-tuple-element.350.g_ref, bf16[3,192,768]{2,1,0:T(8,128)(2,1)} %bitcast.84, ...), custom_call_target="tpu_custom_call" | custom-call | flops 3 | bytes 1 | tf_op jit(solution)/shard_map/self_forward/pallas_call | solution.py:447
  73.5 5.0 %all-to-all-start.1 = ((bf16[4,192,1024]{2,1,0:T(8,128)(2,1)}), bf16[4,192,1024]{2,1,0:T(8,128)(2,1)S(1)}, u32[]{:S(2)}, u32[]{:S(2)}) async-start(bf16[4,192,1024]{2,1,0:T(8,128)(2,1)} %get-tuple-element.157.o_ref), calls=%async_computation.1 | async-start | bytes 3145728 | tf_op jit(solution)/shard_map/all_to_all | solution.py:1084
  88.6 20.2 %all-to-all-done.1 = bf16[4,192,1024]{2,1,0:T(8,128)(2,1)S(1)} async-done(((bf16[4,192,1024]{2,1,0:T(8,128)(2,1)}), bf16[4,192,1024]{2,1,0:T(8,128)(2,1)S(1)}, u32[]{:S(2)}, u32[]{:S(2)}) %all-to-all-start.1) | async-done | bytes 1572896 | tf_op jit(solution)/shard_map/all_to_all | solution.py:1084
  110.0 8.1 %query_stage.1 = (bf16[768,1024]{1,0:T(8,128)(2,1)}, f32[256,768]{1,0:T(8,128)}, bf16[256,768]{1,0:T(8,128)(2,1)}) custom-call(s32[1]{0:T(128)} %bitcast.s_ref.n_ref, bf16[1024,768]{1,0:T(8,128)(2,1)} %bitcast.80, bf16[768,1024]{1,0:T(8,128)(2,1)} %bitcast.82, bf16[768,768]{1,0:T(8,128)(2,1)} %w_ref.7, f32[1,768]{1,0:T(1,128)} %get-tuple-element.349.g_ref, ...), custom_call_target="tpu_custom_call" | custom-call | flops 4 | bytes 1 | tf_op jit(solution)/shard_map/query_stage/pallas_call | solution.py:524
  123.5 28.4 %cross_forward.1 = (bf16[4,800,256]{2,1,0:T(8,128)(2,1)}, bf16[12,1792,1024]{2,1,0:T(8,128)(2,1)}, f32[12,1,1024]{2,1,0:T(1,128)}) custom-call(bf16[768,1024]{1,0:T(8,128)(2,1)} %get-tuple-element.160.refs_0_, bf16[2,768,896]{2,1,0:T(8,128)(2,1)} %project_rows.3.refs_1_.refs_4_.refs_2_, bf16[2,768,384]{2,1,0:T(8,128)(2,1)} %project_rows.4.refs_2_.refs_5_.refs_1_.refs_3_, ...), custom_call_target="tpu_custom_call" | custom-call | flops 22 | bytes 1 | tf_op jit(solution)/shard_map/cross_forward/pallas_call | solution.py:293
  157.5 19.3 %collective-permute-done.4 = bf16[128,768]{1,0:T(8,128)(2,1)S(1)} collective-permute-done((bf16[128,768]{1,0:T(8,128)(2,1)S(1)}, bf16[128,768]{1,0:T(8,128)(2,1)S(1)}, u32[]{:S(2)}, u32[]{:S(2)}) %collective-permute-start.4) | collective-permute-done | bytes 196640 | tf_op jit(solution)/shard_map/ppermute | solution.py:1061
  180.2 16.9 %token_stage.1 = (bf16[256,768]{1,0:T(8,128)(2,1)}, f32[256,768]{1,0:T(8,128)}, bf16[256,768]{1,0:T(8,128)(2,1)}, bf16[256,768]{1,0:T(8,128)(2,1)}, bf16[256,307...) custom-call(bf16[4,800,256]{2,1,0:T(8,128)(2,1)} %copy-done.5, ...), custom_call_target="tpu_custom_call" | custom-call | flops 4 | bytes 1 | tf_op jit(solution)/shard_map/token_stage/pallas_call | solution.py:650
  200.9 13.3 %early_weight_grads.1 = bf16[4,8,432,384]{3,2,1,0:T(8,128)(2,1)} custom-call(bf16[256,768]{1,0:T(8,128)(2,1)} %get-tuple-element.169.a_ref, bf16[256,3072]{1,0:T(8,128)(2,1)} %get-tuple-element.170.du_ref, bf16[256,3072]{1,0:T(8,128)(2,1)} %get-tuple-element.171.z_ref, bf16[256,768]{1,0:T(8,128)(2,1)} %pad_maximum_fusion.1.c_ref, ...), custom_call_target="tpu_custom_call" | custom-call | flops 2 | bytes 1 | tf_op jit(solution)/shard_map/early_weight_grads/pallas_call | solution.py:730
  214.2 6.6 %all-to-all-done.3.refs_6_.refs_7_.refs_4_.refs_5_ = bf16[4,832,256]{2,1,0:T(8,128)(2,1)S(1)} async-done(((bf16[4,832,256]{2,1,0:T(8,128)(2,1)}), bf16[4,832,256]{2,1,0:T(8,128)(2,1)S(1)}, u32[]{:S(2)}, u32[]{:S(2)}) %all-to-all-start.3) | async-done | bytes 1703968 | tf_op jit(solution)/shard_map/all_to_all | solution.py:1084
  223.2 26.4 %cross_backward.2 = (bf16[4,768,256]{2,1,0:T(8,128)(2,1)}, bf16[896,768]{1,0:T(8,128)(2,1)}, bf16[896,768]{1,0:T(8,128)(2,1)}) custom-call(bf16[768,1024]{1,0:T(8,128)(2,1)} %get-tuple-element.160.refs_0_, bf16[2,768,384]{2,1,0:T(8,128)(2,1)} %project_rows.4.refs_2_.refs_5_.refs_1_.refs_3_, bf16[2,768,512]{2,1,0:T(8,128)(2,1)} %project_rows.5.refs_3_.refs_6_.refs_2_.refs_4_, ...), custom_call_target="tpu_custom_call" | custom-call | flops 22 | bytes 1 | tf_op jit(solution)/shard_map/cross_backward/pallas_call | solution.py:391
  249.6 5.8 %row_grads.2 = (bf16[352,768]{1,0:T(8,128)(2,1)}, bf16[256,768]{1,0:T(8,128)(2,1)}, bf16[128,768]{1,0:T(8,128)(2,1)}, bf16[160,768]{1,0:T(8,128)(2,1)}) custom-call(bf16[896,768]{1,0:T(8,128)(2,1)} %get-tuple-element.201.k_ref.refs_5_, bf16[896,768]{1,0:T(8,128)(2,1)} %get-tuple-element.203.v_ref.refs_7_, bf16[2,768,768]{2,1,0:T(8,128)(2,1)} %w_ref.9), custom_call_target="tpu_custom_call" | custom-call | flops 1 | bytes 1 | tf_op jit(solution)/shard_map/row_grads/pallas_call | solution.py:148
  256.4 25.7 %cross_backward.3 = (bf16[4,768,256]{2,1,0:T(8,128)(2,1)}, bf16[896,768]{1,0:T(8,128)(2,1)}, bf16[896,768]{1,0:T(8,128)(2,1)}) custom-call(bf16[768,1024]{1,0:T(8,128)(2,1)} %get-tuple-element.160.refs_0_, bf16[2,768,896]{2,1,0:T(8,128)(2,1)} %project_rows.3.refs_1_.refs_4_.refs_2_, bf16[2,768,896]{2,1,0:T(8,128)(2,1)} %project_rows.3.refs_1_.refs_4_.refs_2_, ...), custom_call_target="tpu_custom_call" | custom-call | flops 22 | bytes 1 | tf_op jit(solution)/shard_map/cross_backward/pallas_call | solution.py:391
  288.4 11.1 %weight_chunks.2 = (bf16[16,96,384]{2,1,0:T(8,128)(2,1)}, bf16[16,96,384]{2,1,0:T(8,128)(2,1)}) custom-call(s32[1]{0:T(128)} %bitcast.24.c_ref, s32[1]{0:T(128)} %bitcast.s_ref.n_ref, bf16[896,768]{1,0:T(8,128)(2,1)} %dynamic-slice_bitcast_fusion.refs_0_, bf16[384,768]{1,0:T(8,128)(2,1)} %copy-done.12, bf16[128,768]{1,0:T(8,128)(2,1)} %copy-done.18, ...), custom_call_target="tpu_custom_call" | custom-call | flops 1 | bytes 1 | tf_op jit(solution)/shard_map/weight_chunks/pallas_call | solution.py:124
  299.5 11.4 %collective-permute-done.7.refs_1_ = bf16[256,768]{1,0:T(8,128)(2,1)S(1)} collective-permute-done((bf16[256,768]{1,0:T(8,128)(2,1)S(1)}, bf16[256,768]{1,0:T(8,128)(2,1)S(1)}, u32[]{:S(2)}, u32[]{:S(2)}) %collective-permute-start.7) | collective-permute-done | bytes 393248 | tf_op jit(solution)/shard_map/ppermute | solution.py:1241
  314.7 4.7 %mixed_stage.1 = (bf16[768,256]{1,0:T(8,128)(2,1)}, f32[256,768]{1,0:T(8,128)}, bf16[256,768]{1,0:T(8,128)(2,1)}, bf16[4,192,256]{2,1,0:T(8,128)(2,1)}, f32[1,768]{1,0:T(1,128)}) custom-call(bf16[4,768,256]{2,1,0:T(8,128)(2,1)} %copy-done.6, bf16[768,768]{1,0:T(8,128)(2,1)} %q_ref.1, f32[256,768]{1,0:T(8,128)} %get-tuple-element.167.h_ref, ...), custom_call_target="tpu_custom_call" | custom-call | flops 1 | bytes 1 | tf_op jit(solution)/shard_map/mixed_stage/pallas_call | solution.py:773
  337.2 9.7 %self_backward.1.d_ref = bf16[4,3,192,256]{3,2,1,0:T(8,128)(2,1)} custom-call(bf16[3,192,1024]{2,1,0:T(8,128)(2,1)} %get-tuple-element.207.q_ref.k_ref.v_ref, bf16[3,192,1024]{2,1,0:T(8,128)(2,1)} %get-tuple-element.207.q_ref.k_ref.v_ref, bf16[3,192,1024]{2,1,0:T(8,128)(2,1)} %get-tuple-element.207.q_ref.k_ref.v_ref, ...), custom_call_target="tpu_custom_call" | custom-call | flops 6 | bytes 1 | tf_op jit(solution)/shard_map/self_backward/pallas_call | solution.py:1000
  360.6 5.1 %own_weight_grads.1 = (bf16[2,3,96,192]{3,2,1,0:T(8,128)(2,1)}, bf16[2,3,96,192]{3,2,1,0:T(8,128)(2,1)}, bf16[2,3,96,192]{3,2,1,0:T(8,128)(2,1)}, bf16[2,3,96,192]{3,2,1,0:T(8,128)(2,1)}, f32[1,768]{1,0:T(1,128)}) custom-call(s32[1]{0:T(128)} %bitcast.30.c_ref, bf16[1024,768]{1,0:T(8,128)(2,1)} %get-tuple-element.247.a_ref, ...), custom_call_target="tpu_custom_call" | custom-call | flops 1 | bytes 1 | tf_op jit(solution)/shard_map/own_weight_grads/pallas_call | solution.py:903
  366.5 16.7 %collective-permute-done.12.refs_3_ = bf16[160,768]{1,0:T(8,128)(2,1)S(1)} collective-permute-done((bf16[160,768]{1,0:T(8,128)(2,1)S(1)}, bf16[160,768]{1,0:T(8,128)(2,1)S(1)}, u32[]{:S(2)}, u32[]{:S(2)}) %collective-permute-start.12) | collective-permute-done | bytes 245792 | tf_op jit(solution)/shard_map/ppermute | solution.py:1241
  396.6 6.1 %row_grads.3.own_ref = bf16[896,768]{1,0:T(8,128)(2,1)} custom-call(bf16[896,768]{1,0:T(8,128)(2,1)} %get-tuple-element.266.refs_4_.k_ref, bf16[896,768]{1,0:T(8,128)(2,1)} %get-tuple-element.202.refs_6_.v_ref, bf16[2,768,768]{2,1,0:T(8,128)(2,1)} %w_ref.9), custom_call_target="tpu_custom_call" | custom-call | flops 1 | bytes 1 | tf_op jit(solution)/shard_map/row_grads/pallas_call | solution.py:148
  402.8 5.4 %input_stage.1 = bf16[256,768]{1,0:T(8,128)(2,1)} custom-call(s32[1]{0:T(128)} %bitcast.s_ref.n_ref, bf16[4,3,192,256]{3,2,1,0:T(8,128)(2,1)} %copy-done.10, bf16[3,768,768]{2,1,0:T(8,128)(2,1)} %w_ref.8, bf16[1024,768]{1,0:T(8,128)(2,1)} %bitcast.81, f32[1,768]{1,0:T(1,128)} %get-tuple-element.350.g_ref, f32[256,768]{1,0:T(8,128)} %get-tuple-element.256.h_ref), custom_call_target="tpu_custom_call" | custom-call | flops 1 | bytes 1 | tf_op jit(solution)/shard_map/input_stage/pallas_call | solution.py:814
  411.6 4.8 %all-to-all-done.7 = bf16[4,2,192,384]{3,2,1,0:T(8,128)(2,1)S(1)} async-done(((bf16[4,2,192,384]{3,2,1,0:T(8,128)(2,1)}), bf16[4,2,192,384]{3,2,1,0:T(8,128)(2,1)S(1)}, u32[]{:S(2)}, u32[]{:S(2)}) %all-to-all-start.7) | async-done | bytes 1179680 | tf_op jit(solution)/shard_map/all_to_all | solution.py:1084
  (191 shorter events, 159.8 us)
Async XLA Ops:
  22.8 37.1 %all-to-all-start = ((bf16[4,256,768]{2,1,0:T(8,128)(2,1)}), bf16[4,256,768]{2,1,0:T(8,128)(2,1)S(1)}, u32[]{:S(2)}, u32[]{:S(2)}) async-start(bf16[4,256,768]{2,1,0:T(8,128)(2,1)} %broadcast_in_dim.104), calls=%async_computation | async-start | bytes 3145728 | tf_op jit(solution)/shard_map/all_to_all | solution.py:1075
  28.7 27.2 %collective-permute-start.1 = (bf16[384,768]{1,0:T(8,128)(2,1)}, bf16[384,768]{1,0:T(8,128)(2,1)S(1)}, u32[]{:S(2)}, u32[]{:S(2)}) collective-permute-start(bf16[384,768]{1,0:T(8,128)(2,1)} %get-tuple-element.331), channel_id=1, source_target_pairs={{0,16},{4,20},{8,24},{12,28},{16,0},{20,4},{24,8},{28,12},{1,17},{... | collective-permute-start | bytes 1769480 | tf_op jit(solution)/shard_map/ppermute | solution.py:1108
  73.5 35.3 %all-to-all-start.1 = ((bf16[4,192,1024]{2,1,0:T(8,128)(2,1)}), bf16[4,192,1024]{2,1,0:T(8,128)(2,1)S(1)}, u32[]{:S(2)}, u32[]{:S(2)}) async-start(bf16[4,192,1024]{2,1,0:T(8,128)(2,1)} %get-tuple-element.157.o_ref), calls=%async_computation.1 | async-start | bytes 3145728 | tf_op jit(solution)/shard_map/all_to_all | solution.py:1084
  78.8 39.3 %collective-permute-start.3 = (bf16[384,768]{1,0:T(8,128)(2,1)}, bf16[384,768]{1,0:T(8,128)(2,1)S(1)}, u32[]{:S(2)}, u32[]{:S(2)}) collective-permute-start(bf16[384,768]{1,0:T(8,128)(2,1)} %get-tuple-element.159), channel_id=1, source_target_pairs={{0,16},{4,20},{8,24},{12,28},{16,0},{20,4},{24,8},{28,12},{1,17},{... | collective-permute-start | bytes 1769480 | tf_op jit(solution)/shard_map/ppermute | solution.py:1112
  151.9 27.1 %all-to-all-start.2 = ((bf16[4,800,256]{2,1,0:T(8,128)(2,1)}), bf16[4,800,256]{2,1,0:T(8,128)(2,1)S(1)}, u32[]{:S(2)}, u32[]{:S(2)}) async-start(bf16[4,800,256]{2,1,0:T(8,128)(2,1)} %get-tuple-element.166), calls=%async_computation.2 | async-start | bytes 3276800 | tf_op jit(solution)/shard_map/all_to_all | solution.py:1084
  155.7 21.1 %collective-permute-start.4 = (bf16[128,768]{1,0:T(8,128)(2,1)S(1)}, bf16[128,768]{1,0:T(8,128)(2,1)S(1)}, u32[]{:S(2)}, u32[]{:S(2)}) collective-permute-start(bf16[128,768]{1,0:T(8,128)(2,1)S(1)} %dynamic-slice_bitcast_fusion.8), channel_id=1, source_target_pairs={{0,16},{4,20},{8,24},{12,28},{16,0},{20,4},{24,8},{28,12},{1,17},{... | collective-permute-start | bytes 589832 | tf_op jit(solution)/shard_map/ppermute | solution.py:1061
  197.1 23.7 %all-to-all-start.3 = ((bf16[4,832,256]{2,1,0:T(8,128)(2,1)}), bf16[4,832,256]{2,1,0:T(8,128)(2,1)S(1)}, u32[]{:S(2)}, u32[]{:S(2)}) async-start(bf16[4,832,256]{2,1,0:T(8,128)(2,1)} %get-tuple-element.168), calls=%async_computation.3 | async-start | bytes 3407872 | tf_op jit(solution)/shard_map/all_to_all | solution.py:1084
  200.7 112.9 %reduce-scatter.3.cloned.1.call-start = ((), (), s32[]{:S(2)}) async-start(), calls=%async_computation.10 | async-start | bytes 13271040 | tf_op jit(solution)/shard_map/reduce_scatter | solution.py:1219
  222.1 33.3 %collective-permute-start.5 = (bf16[128,768]{1,0:T(8,128)(2,1)S(1)}, bf16[128,768]{1,0:T(8,128)(2,1)S(1)}, u32[]{:S(2)}, u32[]{:S(2)}) collective-permute-start(bf16[128,768]{1,0:T(8,128)(2,1)S(1)} %get-tuple-element.346), channel_id=1, source_target_pairs={{0,16},{4,20},{8,24},{12,28},{16,0},{20,4},{24,8},{28,12},{1,17},{... | collective-permute-start | bytes 589832 | tf_op jit(solution)/shard_map/ppermute | solution.py:1061
  255.4 26.7 %collective-permute-start.6 = (bf16[352,768]{1,0:T(8,128)(2,1)}, bf16[352,768]{1,0:T(8,128)(2,1)}, u32[]{:S(2)}, u32[]{:S(2)}) collective-permute-start(bf16[352,768]{1,0:T(8,128)(2,1)} %get-tuple-element.189), channel_id=1, source_target_pairs={{0,16},{4,20},{8,24},{12,28},{16,0},{20,4},{24,8},{28,12},{1,17},{... | collective-permute-start | bytes 1622024 | tf_op jit(solution)/shard_map/ppermute | solution.py:1241
  282.1 31.4 %all-to-all-start.4 = ((bf16[4,768,256]{2,1,0:T(8,128)(2,1)}), bf16[4,768,256]{2,1,0:T(8,128)(2,1)S(1)}, u32[]{:S(2)}, u32[]{:S(2)}) async-start(bf16[4,768,256]{2,1,0:T(8,128)(2,1)} %get-tuple-element.193), calls=%async_computation.4 | async-start | bytes 3145728 | tf_op jit(solution)/shard_map/all_to_all | solution.py:1084
  286.2 24.6 %collective-permute-start.7 = (bf16[256,768]{1,0:T(8,128)(2,1)S(1)}, bf16[256,768]{1,0:T(8,128)(2,1)S(1)}, u32[]{:S(2)}, u32[]{:S(2)}) collective-permute-start(bf16[256,768]{1,0:T(8,128)(2,1)S(1)} %copy-done.31), channel_id=1, source_target_pairs={{0,16},{4,20},{8,24},{12,28},{16,0},{20,4},{24,8},{28,12},{1,17},{... | collective-permute-start | bytes 1179656 | tf_op jit(solution)/shard_map/ppermute | solution.py:1241
  322.9 123.9 %reduce-scatter.5.cloned.1.call-start = ((), (), s32[]{:S(2)}) async-start(), calls=%async_computation.11 | async-start | bytes 2985984 | tf_op jit(solution)/shard_map/reduce_scatter | solution.py:1294
  352.2 32.7 %all-to-all-start.6 = ((bf16[4,3,192,256]{3,2,1,0:T(8,128)(2,1)}), bf16[4,3,192,256]{3,2,1,0:T(8,128)(2,1)S(1)}, u32[]{:S(2)}, u32[]{:S(2)}) async-start(bf16[4,3,192,256]{3,2,1,0:T(8,128)(2,1)} %self_backward.1.d_ref), calls=%async_computation.7 | async-start | bytes 2359296 | tf_op jit(solution)/shard_map/all_to_all | solution.py:1084
  358.8 24.3 %collective-permute-start.13 = (bf16[8,96,384]{2,1,0:T(8,128)(2,1)}, bf16[8,96,384]{2,1,0:T(8,128)(2,1)S(1)}, u32[]{:S(2)}, u32[]{:S(2)}) collective-permute-start(bf16[8,96,384]{2,1,0:T(8,128)(2,1)} %get-tuple-element.246), channel_id=1, source_target_pairs={{0,2},{1,3},{2,0},{3,1},{4,6},{5,7},{6,4},{7,5},{8,10},{9,11},{10,... | collective-permute-start | bytes 1769480 | tf_op jit(solution)/shard_map/ppermute | solution.py:1255
  360.5 22.7 %collective-permute-start.12 = (bf16[160,768]{1,0:T(8,128)(2,1)S(1)}, bf16[160,768]{1,0:T(8,128)(2,1)S(1)}, u32[]{:S(2)}, u32[]{:S(2)}) collective-permute-start(bf16[160,768]{1,0:T(8,128)(2,1)S(1)} %copy-done.33), channel_id=1, source_target_pairs={{0,16},{4,20},{8,24},{12,28},{16,0},{20,4},{24,8},{28,12},{1,17},{... | collective-permute-start | bytes 737288 | tf_op jit(solution)/shard_map/ppermute | solution.py:1241
  388.3 28.2 %all-to-all-start.7 = ((bf16[4,2,192,384]{3,2,1,0:T(8,128)(2,1)}), bf16[4,2,192,384]{3,2,1,0:T(8,128)(2,1)S(1)}, u32[]{:S(2)}, u32[]{:S(2)}) async-start(bf16[4,2,192,384]{3,2,1,0:T(8,128)(2,1)} %sums_for.1), calls=%async_computation.8 | async-start | bytes 2359296 | tf_op jit(solution)/shard_map/all_to_all | solution.py:1084
  392.4 19.2 %collective-permute-start.14 = (bf16[2,3,96,192]{3,2,1,0:T(8,128)(2,1)}, bf16[2,3,96,192]{3,2,1,0:T(8,128)(2,1)S(1)}, u32[]{:S(2)}, u32[]{:S(2)}) collective-permute-start(bf16[2,3,96,192]{3,2,1,0:T(8,128)(2,1)} %get-tuple-element.262), channel_id=1, source_target_pairs={{0,1},{1,0},{2,3},{3,2},{4,5},{5,4},{6,7},{7,6},{8,9},{9,8},{10,11... | collective-permute-start | bytes 663560 | tf_op jit(solution)/shard_map/ppermute | solution.py:1255
  392.4 19.2 %collective-permute-start.15 = (bf16[2,3,96,192]{3,2,1,0:T(8,128)(2,1)}, bf16[2,3,96,192]{3,2,1,0:T(8,128)(2,1)S(1)}, u32[]{:S(2)}, u32[]{:S(2)}) collective-permute-start(bf16[2,3,96,192]{3,2,1,0:T(8,128)(2,1)} %get-tuple-element.263), channel_id=1, source_target_pairs={{0,2},{1,3},{2,0},{3,1},{4,6},{5,7},{6,4},{7,5},{8,10},{9,11},{10,... | collective-permute-start | bytes 663560 | tf_op jit(solution)/shard_map/ppermute | solution.py:1255
  393.6 18.0 %collective-permute-start.16 = (bf16[2,3,96,192]{3,2,1,0:T(8,128)(2,1)S(1)}, bf16[2,3,96,192]{3,2,1,0:T(8,128)(2,1)S(1)}, u32[]{:S(2)}, u32[]{:S(2)}) collective-permute-start(bf16[2,3,96,192]{3,2,1,0:T(8,128)(2,1)S(1)} %copy-done.32), channel_id=1, source_target_pairs={{0,3},{1,2},{2,1},{3,0},{4,7},{5,6},{6,5},{7,4},{8,11},{9,10},{10,... | collective-permute-start | bytes 663560 | tf_op jit(solution)/shard_map/ppermute | solution.py:1255
  416.5 27.3 %collective-permute-start.19 = (bf16[128,768]{1,0:T(8,128)(2,1)S(1)}, bf16[128,768]{1,0:T(8,128)(2,1)S(1)}, u32[]{:S(2)}, u32[]{:S(2)}) collective-permute-start(bf16[128,768]{1,0:T(8,128)(2,1)S(1)} %get-tuple-element.342), channel_id=1, source_target_pairs={{0,16},{4,20},{8,24},{12,28},{16,0},{20,4},{24,8},{28,12},{1,17},{... | collective-permute-start | bytes 589832 | tf_op jit(solution)/shard_map/ppermute | solution.py:1061
  419.9 23.9 %collective-permute-start.20 = (bf16[192,384]{1,0:T(8,128)(2,1)}, bf16[192,384]{1,0:T(8,128)(2,1)S(1)}, u32[]{:S(2)}, u32[]{:S(2)}) collective-permute-start(bf16[192,384]{1,0:T(8,128)(2,1)} %get-tuple-element.274), channel_id=1, source_target_pairs={{0,16},{4,20},{8,24},{12,28},{16,0},{20,4},{24,8},{28,12},{1,17},{... | collective-permute-start | bytes 442376 | tf_op jit(solution)/shard_map/ppermute | solution.py:1255
  424.9 18.9 %collective-permute-start.22 = (bf16[3,96,192]{2,1,0:T(8,128)(2,1)}, bf16[3,96,192]{2,1,0:T(8,128)(2,1)S(1)}, u32[]{:S(2)}, u32[]{:S(2)}) collective-permute-start(bf16[3,96,192]{2,1,0:T(8,128)(2,1)} %bitcast.112), channel_id=1, source_target_pairs={{0,4},{1,12},{2,20},{3,28},{4,5},{5,13},{6,21},{7,29},{8,6},{9,14}... | collective-permute-start | bytes 331784 | tf_op jit(solution)/shard_map/ppermute | solution.py:1372
  426.3 17.5 %collective-permute-start.21 = (bf16[3,96,192]{2,1,0:T(8,128)(2,1)}, bf16[3,96,192]{2,1,0:T(8,128)(2,1)S(1)}, u32[]{:S(2)}, u32[]{:S(2)}) collective-permute-start(bf16[3,96,192]{2,1,0:T(8,128)(2,1)} %bitcast.111), channel_id=1, source_target_pairs={{0,0},{1,8},{2,16},{3,24},{4,1},{5,9},{6,17},{7,25},{8,2},{9,10},{... | collective-permute-start | bytes 331784 | tf_op jit(solution)/shard_map/ppermute | solution.py:1372
  (46 other events, 379.5 us)
Sparse Core Ops, SparseCore 0:
  221.0 84.8 reduce-scatter.2
  335.6 85.9 reduce-scatter.4

commit v5 on v4

--- a/solution.py
+++ b/solution.py
@@ -576,7 +576,7 @@
     heads = width // HEAD_DIM
     stat_rows = (parts.shape[1] - width) // 2
     hidden = ffn_in.shape[1]
-    piece = 384
+    piece = 768
     steps = hidden // piece
     payload = width + 4 * stat_rows
 
@@ -947,29 +947,39 @@
     )(*[array for pair in pairs for array in pair])
 
 
-def sums_of(arrays, bit):
-    _, rows, width = arrays[0].shape
+def sums_of(lists, bit):
+    arrays = [array for one in lists for array in one]
 
     def kernel(s_ref, *refs):
-        for side in range(2):
-            terms = [refs[2 * i + side][0].astype(F32) for i in range(len(arrays))]
-            refs[2 * len(arrays) + side][...] = functools.reduce(jnp.add, terms).astype(BF16)
-
-    spec = lambda side: pl.BlockSpec((1, rows, width), lambda j, s: ((s[0] + side) % 2, 0, 0))
-    out = pl.BlockSpec((rows, width), lambda j, s: (0, 0))
-    return pl.pallas_call(
+        start = 0
+        for i, one in enumerate(lists):
+            for side in range(2):
+                terms = [refs[2 * (start + n) + side][0].astype(F32) for n in range(len(one))]
+                total = functools.reduce(jnp.add, terms)
+                refs[2 * (len(arrays) + i) + side][...] = total.astype(BF16)
+            start += len(one)
+
+    def spec(array, side):
+        return pl.BlockSpec((1,) + array.shape[1:], lambda j, s: ((s[0] + side) % 2, 0, 0))
+
+    outs = pl.pallas_call(
         kernel,
         grid_spec=pltpu.PrefetchScalarGridSpec(
             num_scalar_prefetch=1,
             grid=(1,),
-            in_specs=[spec(side) for _ in arrays for side in range(2)],
-            out_specs=[out] * 2,
-        ),
-        out_shape=[jax.ShapeDtypeStruct((rows, width), BF16)] * 2,
+            in_specs=[spec(array, side) for array in arrays for side in range(2)],
+            out_specs=[
+                pl.BlockSpec(one[0].shape[1:], lambda j, s: (0, 0)) for one in lists for _ in range(2)
+            ],
+        ),
+        out_shape=[
+            jax.ShapeDtypeStruct(one[0].shape[1:], BF16) for one in lists for _ in range(2)
+        ],
         compiler_params=params(),
         cost_estimate=estimate(flops=0, bytes_accessed=0, transcendentals=0),
         name="sums_of",
     )(bit, *[array for array in arrays for _ in range(2)])
+    return list(zip(outs[::2], outs[1::2]))
 
 
 def self_backward(projected, mixed, grads, prob, weight, groups):
@@ -1324,9 +1334,7 @@
         got_2 = moved(sent_2, "dp", 1)
     own_grads = self_backward(projected, sent_mix, own_mixed, self_prob, self_weight, groups)
     if staged:
-        own_grads, kept_1, got_1, kept_2, got_2, pieces = together(
-            own_grads, kept_1, got_1, kept_2, got_2, pieces
-        )
+        own_grads, kept_2, got_2, pieces = together(own_grads, kept_2, got_2, pieces)
     back = traded(own_grads)
     if staged:
         back_4 = sent_back(pieces[3])
@@ -1342,25 +1350,30 @@
             blocks,
         )
         gains = jnp.concatenate([gain_one, gain_two, gain_three], axis=0)
+        gains = gains + moved(gains, "dp", 1)
+        gains = gains + moved(gains, "dp", 2)
         back, back_4, kept_1, got_1, kept_2, got_2, parts_w, gains, key_low = together(
             back, back_4, kept_1, got_1, kept_2, got_2, parts_w, gains, key_low
         )
     own_grad = input_stage(back, padded_qkv, all_inputs, gain_rows[0], self_grad, slot, groups)
+    if staged:
+        own_grad, key_low = together(own_grad, key_low)
+    dec_parts = leaving(own_grad)
     if staged:
         late = traded(sums_for([(kept_1, got_1), (kept_2, got_2)], groups))
         parts_w = [parts_w[0]] + [moved(p, "dp", r) for r, p in enumerate(parts_w) if r]
-        gains = gains + moved(gains, "dp", 1)
-        gains = gains + moved(gains, "dp", 2)
+        gains_got = moved(gains, "blk", 1)
         (enc_own,) = row_grads(key_low[0], value_low[0], cross_kv, [0, enc_rows])
         enc_grad = both_queries(enc_own, [back_1, back_2, back_3, back_4], here)
-        own_grad, late, parts_w, gains, enc_grad = together(
-            own_grad, late, parts_w, gains, enc_grad
-        )
-    dec_parts = leaving(own_grad)
+        dec_parts, late, parts_w, gains, gains_got, enc_grad = together(
+            dec_parts, late, parts_w, gains, gains_got, enc_grad
+        )
+        gains = gains + gains_got
     if staged:
-        kept_j, sent_j = sums_of([late[g] for g in range(groups)], here)
+        (kept_j, sent_j), halves = sums_of(
+            [[late[g] for g in range(groups)], [p.reshape(seqs, -1, own) for p in parts_w]], here
+        )
         got_j = moved(sent_j, "blk", groups)
-        halves = sums_of([p.reshape(seqs, -1, own) for p in parts_w], here)
         got_w = []
         for step, piece in enumerate(halves):
             pairs = []
@@ -1370,13 +1383,10 @@
                     pairs.append((b * columns + d, (d * seqs + row) * columns + b % groups))
             piece = piece.reshape(3, width // blocks, own)
             got_w.append(lax.ppermute(piece, ("blk", "dp"), pairs))
-        gains = gains + moved(gains, "blk", 1)
         gains = gains + moved(gains, "blk", 2)
-        dec_parts, kept_j, got_j, got_w, gains = together(
-            dec_parts, kept_j, got_j, got_w, gains
-        )
+        dec_grad = returned(dec_parts)
+        dec_grad, kept_j, got_j, got_w, gains = together(dec_grad, kept_j, got_j, got_w, gains)
         gain_grads = gains + moved(gains, "blk", 4)
-        dec_grad = returned(dec_parts)
         qkv = sum(piece.astype(F32) for piece in got_w)
         ffn_in_own, ffn_out_own, kv_own, cross_out_own, cross_q_own, self_out_own = unpacked(
             hidden, (kept_j, got_j), width // blocks, width // columns

time: 465 us -> 459 us (0.987)
  Pallas kernels: 216 us -> 211 us
    ppermute x2, waiting for transfers between devices: 2.26 us -> 17.4 us  [body(): got_w.append(lax.ppermute(piece, ('blk', 'dp'), pairs))]
    ppermute x4, waiting for transfers between devices: 32.3 us -> 18.8 us  [sent_back(): return lax.ppermute(piece, 'blk', shifted(1))]
    unnamed x75 -> x71, local copies, waits for them, and re-layouts: 19.5 us -> 18.8 us
  transfers between devices with their start and end apart: 36 -> 36, of which waited for: 17 -> 15; matrix products, arithmetic and copies ran while one was open for 6% -> 6% of each run, Pallas kernels for 36% -> 36%
where the time goes in v5:
time: 459 us; the launch traced here: 453 us
  Pallas kernels  211 us (46%)
  waiting for transfers between devices  119 us (26%)
  starting transfers between devices  69.7 us (15%)
  local copies, waits for them, and re-layouts  32.5 us (7%)
  between operations  14.8 us (3%)
  other arithmetic  6.4 us (1%)
    pallas_call x2, Pallas kernels, cross_backward(): pl.pallas_call(kernel, grid=(heads // pair,), in_specs=[pl.BlockSpec((siz...  52 us
    all_to_all x7, waiting for transfers between devices, traded(): return lax.all_to_all(array, 'blk', 0, 0, axis_index_groups=members)  32.8 us
    ppermute x4, waiting for transfers between devices, exchange(): lax.ppermute(pieces(lax.rem(mine + step, seqs)), 'blk', shifted(step))  28.4 us
    pallas_call x1, Pallas kernels, cross_forward(): pl.pallas_call(kernel, grid=(heads,), in_specs=[pl.BlockSpec((HEAD_DIM, l...  28.4 us
    all_to_all x7, starting transfers between devices, traded(): return lax.all_to_all(array, 'blk', 0, 0, axis_index_groups=members)  27.3 us
    ppermute x4, waiting for transfers between devices, sent_back(): return lax.ppermute(piece, 'blk', shifted(1))  18.8 us
    unnamed x71, local copies, waits for them, and re-layouts  18.8 us
    ppermute x2, waiting for transfers between devices, body(): got_w.append(lax.ppermute(piece, ('blk', 'dp'), pairs))  17.4 us
  transfers between devices with their start and end apart: 36, of which 15 were waited for; matrix products, arithmetic and copies ran while one was open for 6% of the time, Pallas kernels for 36%

profile of v5, /device:TPU:0, one launch (start us, length us, event | category | flops | bytes accessed | tf_op | source)
XLA Modules:
  0.0 452.5 jit_solution(5514828385101397583)
XLA Ops:
  12.4 9.1 %collective-permute-done = bf16[128,768]{1,0:T(8,128)(2,1)S(1)} collective-permute-done((bf16[128,768]{1,0:T(8,128)(2,1)S(1)}, bf16[128,768]{1,0:T(8,128)(2,1)S(1)}, u32[]{:S(2)}, u32[]{:S(2)}) %collective-permute-start) | collective-permute-done | bytes 196640 | tf_op jit(solution)/shard_map/ppermute | solution.py:1071
  38.3 5.6 %project_rows.3.refs_1_.refs_4_.refs_2_ = bf16[2,768,896]{2,1,0:T(8,128)(2,1)} custom-call(bf16[896,768]{1,0:T(8,128)(2,1)} %dynamic-slice_bitcast_fusion.refs_0_, bf16[2,768,768]{2,1,0:T(8,128)(2,1)} %bitcast.76), custom_call_target="tpu_custom_call" | custom-call | flops 2 | bytes 1 | tf_op jit(solution)/shard_map/project_rows/pallas_call | solution.py:492
  49.9 6.1 %collective-permute-done.1.refs_0_.refs_1_ = bf16[384,768]{1,0:T(8,128)(2,1)S(1)} collective-permute-done((bf16[384,768]{1,0:T(8,128)(2,1)}, bf16[384,768]{1,0:T(8,128)(2,1)S(1)}, u32[]{:S(2)}, u32[]{:S(2)}) %collective-permute-start.1) | collective-permute-done | bytes 589856 | tf_op jit(solution)/shard_map/ppermute | solution.py:1118
  61.0 11.8 %self_forward.1 = (bf16[1024,768]{1,0:T(8,128)(2,1)}, bf16[3,192,1024]{2,1,0:T(8,128)(2,1)}, bf16[4,192,1024]{2,1,0:T(8,128)(2,1)}, bf16[3,1024,1024]{2,1,0:T(8,128)(2,1)}, f32[3,1,1024]{2,1,0:T(1,128)}) custom-call(bf16[1024,768]{1,0:T(8,128)(2,1)} %bitcast.79, f32[1,768]{1,0:T(1,128)} %get-tuple-element.352.g_ref, bf16[3,192,768]{2,1,0:T(8,128)(2,1)} %bitcast.84, ...), custom_call_target="tpu_custom_call" | custom-call | flops 3 | bytes 1 | tf_op jit(solution)/shard_map/self_forward/pallas_call | solution.py:447
  73.5 5.2 %all-to-all-start.1 = ((bf16[4,192,1024]{2,1,0:T(8,128)(2,1)}), bf16[4,192,1024]{2,1,0:T(8,128)(2,1)S(1)}, u32[]{:S(2)}, u32[]{:S(2)}) async-start(bf16[4,192,1024]{2,1,0:T(8,128)(2,1)} %get-tuple-element.158.o_ref), calls=%async_computation.1 | async-start | bytes 3145728 | tf_op jit(solution)/shard_map/all_to_all | solution.py:1094
  88.7 20.2 %all-to-all-done.1 = bf16[4,192,1024]{2,1,0:T(8,128)(2,1)S(1)} async-done(((bf16[4,192,1024]{2,1,0:T(8,128)(2,1)}), bf16[4,192,1024]{2,1,0:T(8,128)(2,1)S(1)}, u32[]{:S(2)}, u32[]{:S(2)}) %all-to-all-start.1) | async-done | bytes 1572896 | tf_op jit(solution)/shard_map/all_to_all | solution.py:1094
  110.1 8.2 %query_stage.1 = (bf16[768,1024]{1,0:T(8,128)(2,1)}, f32[256,768]{1,0:T(8,128)}, bf16[256,768]{1,0:T(8,128)(2,1)}) custom-call(s32[1]{0:T(128)} %bitcast.s_ref.n_ref, bf16[1024,768]{1,0:T(8,128)(2,1)} %bitcast.80, bf16[768,1024]{1,0:T(8,128)(2,1)} %bitcast.82, bf16[768,768]{1,0:T(8,128)(2,1)} %w_ref.7, f32[1,768]{1,0:T(1,128)} %get-tuple-element.351.g_ref, ...), custom_call_target="tpu_custom_call" | custom-call | flops 4 | bytes 1 | tf_op jit(solution)/shard_map/query_stage/pallas_call | solution.py:524
  123.6 28.4 %cross_forward.1 = (bf16[4,800,256]{2,1,0:T(8,128)(2,1)}, bf16[12,1792,1024]{2,1,0:T(8,128)(2,1)}, f32[12,1,1024]{2,1,0:T(1,128)}) custom-call(bf16[768,1024]{1,0:T(8,128)(2,1)} %get-tuple-element.161.refs_0_, bf16[2,768,896]{2,1,0:T(8,128)(2,1)} %project_rows.3.refs_1_.refs_4_.refs_2_, bf16[2,768,384]{2,1,0:T(8,128)(2,1)} %project_rows.4.refs_2_.refs_5_.refs_1_.refs_3_, ...), custom_call_target="tpu_custom_call" | custom-call | flops 22 | bytes 1 | tf_op jit(solution)/shard_map/cross_forward/pallas_call | solution.py:293
  157.6 19.3 %collective-permute-done.4 = bf16[128,768]{1,0:T(8,128)(2,1)S(1)} collective-permute-done((bf16[128,768]{1,0:T(8,128)(2,1)S(1)}, bf16[128,768]{1,0:T(8,128)(2,1)S(1)}, u32[]{:S(2)}, u32[]{:S(2)}) %collective-permute-start.4) | collective-permute-done | bytes 196640 | tf_op jit(solution)/shard_map/ppermute | solution.py:1071
  180.3 13.8 %token_stage.1 = (bf16[256,768]{1,0:T(8,128)(2,1)}, f32[256,768]{1,0:T(8,128)}, bf16[256,768]{1,0:T(8,128)(2,1)}, bf16[256,768]{1,0:T(8,128)(2,1)}, bf16[256,307...) custom-call(bf16[4,800,256]{2,1,0:T(8,128)(2,1)} %copy-done.5, ...), custom_call_target="tpu_custom_call" | custom-call | flops 4 | bytes 1 | tf_op jit(solution)/shard_map/token_stage/pallas_call | solution.py:650
  198.3 13.3 %early_weight_grads.1 = bf16[4,8,432,384]{3,2,1,0:T(8,128)(2,1)} custom-call(bf16[256,768]{1,0:T(8,128)(2,1)} %get-tuple-element.170.a_ref, bf16[256,3072]{1,0:T(8,128)(2,1)} %get-tuple-element.171.du_ref, bf16[256,3072]{1,0:T(8,128)(2,1)} %get-tuple-element.172.z_ref, bf16[256,768]{1,0:T(8,128)(2,1)} %pad_maximum_fusion.1.c_ref, ...), custom_call_target="tpu_custom_call" | custom-call | flops 2 | bytes 1 | tf_op jit(solution)/shard_map/early_weight_grads/pallas_call | solution.py:730
  211.6 6.3 %all-to-all-done.3.refs_6_.refs_7_.refs_4_.refs_5_ = bf16[4,832,256]{2,1,0:T(8,128)(2,1)S(1)} async-done(((bf16[4,832,256]{2,1,0:T(8,128)(2,1)}), bf16[4,832,256]{2,1,0:T(8,128)(2,1)S(1)}, u32[]{:S(2)}, u32[]{:S(2)}) %all-to-all-start.3) | async-done | bytes 1703968 | tf_op jit(solution)/shard_map/all_to_all | solution.py:1094
  220.3 26.3 %cross_backward.2 = (bf16[4,768,256]{2,1,0:T(8,128)(2,1)}, bf16[896,768]{1,0:T(8,128)(2,1)}, bf16[896,768]{1,0:T(8,128)(2,1)}) custom-call(bf16[768,1024]{1,0:T(8,128)(2,1)} %get-tuple-element.161.refs_0_, bf16[2,768,384]{2,1,0:T(8,128)(2,1)} %project_rows.4.refs_2_.refs_5_.refs_1_.refs_3_, bf16[2,768,512]{2,1,0:T(8,128)(2,1)} %project_rows.5.refs_3_.refs_6_.refs_2_.refs_4_, ...), custom_call_target="tpu_custom_call" | custom-call | flops 22 | bytes 1 | tf_op jit(solution)/shard_map/cross_backward/pallas_call | solution.py:391
  246.5 5.8 %row_grads.2 = (bf16[352,768]{1,0:T(8,128)(2,1)}, bf16[256,768]{1,0:T(8,128)(2,1)}, bf16[128,768]{1,0:T(8,128)(2,1)}, bf16[160,768]{1,0:T(8,128)(2,1)}) custom-call(bf16[896,768]{1,0:T(8,128)(2,1)} %get-tuple-element.202.k_ref.refs_5_, bf16[896,768]{1,0:T(8,128)(2,1)} %get-tuple-element.204.v_ref.refs_7_, bf16[2,768,768]{2,1,0:T(8,128)(2,1)} %w_ref.9), custom_call_target="tpu_custom_call" | custom-call | flops 1 | bytes 1 | tf_op jit(solution)/shard_map/row_grads/pallas_call | solution.py:148
  253.4 25.7 %cross_backward.3 = (bf16[4,768,256]{2,1,0:T(8,128)(2,1)}, bf16[896,768]{1,0:T(8,128)(2,1)}, bf16[896,768]{1,0:T(8,128)(2,1)}) custom-call(bf16[768,1024]{1,0:T(8,128)(2,1)} %get-tuple-element.161.refs_0_, bf16[2,768,896]{2,1,0:T(8,128)(2,1)} %project_rows.3.refs_1_.refs_4_.refs_2_, bf16[2,768,896]{2,1,0:T(8,128)(2,1)} %project_rows.3.refs_1_.refs_4_.refs_2_, ...), custom_call_target="tpu_custom_call" | custom-call | flops 22 | bytes 1 | tf_op jit(solution)/shard_map/cross_backward/pallas_call | solution.py:391
  285.1 11.0 %weight_chunks.2 = (bf16[16,96,384]{2,1,0:T(8,128)(2,1)}, bf16[16,96,384]{2,1,0:T(8,128)(2,1)}) custom-call(s32[1]{0:T(128)} %bitcast.24.c_ref, s32[1]{0:T(128)} %bitcast.s_ref.n_ref, bf16[896,768]{1,0:T(8,128)(2,1)} %dynamic-slice_bitcast_fusion.refs_0_, bf16[384,768]{1,0:T(8,128)(2,1)} %copy-done.12, bf16[128,768]{1,0:T(8,128)(2,1)} %copy-done.17, ...), custom_call_target="tpu_custom_call" | custom-call | flops 1 | bytes 1 | tf_op jit(solution)/shard_map/weight_chunks/pallas_call | solution.py:124
  296.1 11.5 %collective-permute-done.7.refs_1_ = bf16[256,768]{1,0:T(8,128)(2,1)S(1)} collective-permute-done((bf16[256,768]{1,0:T(8,128)(2,1)S(1)}, bf16[256,768]{1,0:T(8,128)(2,1)S(1)}, u32[]{:S(2)}, u32[]{:S(2)}) %collective-permute-start.7) | collective-permute-done | bytes 393248 | tf_op jit(solution)/shard_map/ppermute | solution.py:1251
  311.4 4.7 %mixed_stage.1 = (bf16[768,256]{1,0:T(8,128)(2,1)}, f32[256,768]{1,0:T(8,128)}, bf16[256,768]{1,0:T(8,128)(2,1)}, bf16[4,192,256]{2,1,0:T(8,128)(2,1)}, f32[1,768]{1,0:T(1,128)}) custom-call(bf16[4,768,256]{2,1,0:T(8,128)(2,1)} %copy-done.6, bf16[768,768]{1,0:T(8,128)(2,1)} %q_ref.1, f32[256,768]{1,0:T(8,128)} %get-tuple-element.168.h_ref, ...), custom_call_target="tpu_custom_call" | custom-call | flops 1 | bytes 1 | tf_op jit(solution)/shard_map/mixed_stage/pallas_call | solution.py:773
  332.4 9.7 %self_backward.1.d_ref = bf16[4,3,192,256]{3,2,1,0:T(8,128)(2,1)} custom-call(bf16[3,192,1024]{2,1,0:T(8,128)(2,1)} %get-tuple-element.208.q_ref.k_ref.v_ref, bf16[3,192,1024]{2,1,0:T(8,128)(2,1)} %get-tuple-element.208.q_ref.k_ref.v_ref, bf16[3,192,1024]{2,1,0:T(8,128)(2,1)} %get-tuple-element.208.q_ref.k_ref.v_ref, ...), custom_call_target="tpu_custom_call" | custom-call | flops 6 | bytes 1 | tf_op jit(solution)/shard_map/self_backward/pallas_call | solution.py:1010
  350.7 5.2 %own_weight_grads.1 = (bf16[2,3,96,192]{3,2,1,0:T(8,128)(2,1)}, bf16[2,3,96,192]{3,2,1,0:T(8,128)(2,1)}, bf16[2,3,96,192]{3,2,1,0:T(8,128)(2,1)}, bf16[2,3,96,192]{3,2,1,0:T(8,128)(2,1)}, f32[1,768]{1,0:T(1,128)}) custom-call(s32[1]{0:T(128)} %bitcast.30.c_ref, bf16[1024,768]{1,0:T(8,128)(2,1)} %get-tuple-element.246.a_ref, ...), custom_call_target="tpu_custom_call" | custom-call | flops 1 | bytes 1 | tf_op jit(solution)/shard_map/own_weight_grads/pallas_call | solution.py:903
  360.4 14.3 %collective-permute-done.15 = f32[3,768]{1,0:T(4,128)S(1)} collective-permute-done((f32[3,768]{1,0:T(4,128)S(1)}, f32[3,768]{1,0:T(4,128)S(1)}, u32[]{:S(2)}, u32[]{:S(2)}) %collective-permute-start.15) | collective-permute-done | bytes 9248 | tf_op jit(solution)/shard_map/ppermute | solution.py:1265
  387.9 5.5 %input_stage.1 = bf16[256,768]{1,0:T(8,128)(2,1)} custom-call(s32[1]{0:T(128)} %bitcast.s_ref.n_ref, bf16[4,3,192,256]{3,2,1,0:T(8,128)(2,1)} %copy-done.10, bf16[3,768,768]{2,1,0:T(8,128)(2,1)} %w_ref.8, bf16[1024,768]{1,0:T(8,128)(2,1)} %bitcast.81, f32[1,768]{1,0:T(1,128)} %get-tuple-element.352.g_ref, f32[256,768]{1,0:T(8,128)} %get-tuple-element.255.h_ref), custom_call_target="tpu_custom_call" | custom-call | flops 1 | bytes 1 | tf_op jit(solution)/shard_map/input_stage/pallas_call | solution.py:814
  400.9 5.9 %row_grads.3.own_ref = bf16[896,768]{1,0:T(8,128)(2,1)} custom-call(bf16[896,768]{1,0:T(8,128)(2,1)} %get-tuple-element.267.refs_4_.k_ref, bf16[896,768]{1,0:T(8,128)(2,1)} %get-tuple-element.203.refs_6_.v_ref, bf16[2,768,768]{2,1,0:T(8,128)(2,1)} %w_ref.9), custom_call_target="tpu_custom_call" | custom-call | flops 1 | bytes 1 | tf_op jit(solution)/shard_map/row_grads/pallas_call | solution.py:148
  422.8 17.4 %collective-permute-done.23 = bf16[3,96,192]{2,1,0:T(8,128)(2,1)S(1)} collective-permute-done((bf16[3,96,192]{2,1,0:T(8,128)(2,1)}, bf16[3,96,192]{2,1,0:T(8,128)(2,1)S(1)}, u32[]{:S(2)}, u32[]{:S(2)}) %collective-permute-start.23) | collective-permute-done | bytes 110624 | tf_op jit(solution)/shard_map/ppermute | solution.py:1385
  (186 shorter events, 147.5 us)
Async XLA Ops:
  22.8 37.1 %all-to-all-start = ((bf16[4,256,768]{2,1,0:T(8,128)(2,1)}), bf16[4,256,768]{2,1,0:T(8,128)(2,1)S(1)}, u32[]{:S(2)}, u32[]{:S(2)}) async-start(bf16[4,256,768]{2,1,0:T(8,128)(2,1)} %broadcast_in_dim.104), calls=%async_computation | async-start | bytes 3145728 | tf_op jit(solution)/shard_map/all_to_all | solution.py:1085
  28.7 27.2 %collective-permute-start.1 = (bf16[384,768]{1,0:T(8,128)(2,1)}, bf16[384,768]{1,0:T(8,128)(2,1)S(1)}, u32[]{:S(2)}, u32[]{:S(2)}) collective-permute-start(bf16[384,768]{1,0:T(8,128)(2,1)} %get-tuple-element.333), channel_id=1, source_target_pairs={{0,16},{4,20},{8,24},{12,28},{16,0},{20,4},{24,8},{28,12},{1,17},{... | collective-permute-start | bytes 1769480 | tf_op jit(solution)/shard_map/ppermute | solution.py:1118
  56.0 16.9 %collective-permute-start.2 = (bf16[128,768]{1,0:T(8,128)(2,1)S(1)}, bf16[128,768]{1,0:T(8,128)(2,1)S(1)}, u32[]{:S(2)}, u32[]{:S(2)}) collective-permute-start(bf16[128,768]{1,0:T(8,128)(2,1)S(1)} %dynamic-slice_bitcast_fusion.3), channel_id=1, source_target_pairs={{0,16},{4,20},{8,24},{12,28},{16,0},{20,4},{24,8},{28,12},{1,17},{... | collective-permute-start | bytes 589832 | tf_op jit(solution)/shard_map/ppermute | solution.py:1122
  73.5 35.4 %all-to-all-start.1 = ((bf16[4,192,1024]{2,1,0:T(8,128)(2,1)}), bf16[4,192,1024]{2,1,0:T(8,128)(2,1)S(1)}, u32[]{:S(2)}, u32[]{:S(2)}) async-start(bf16[4,192,1024]{2,1,0:T(8,128)(2,1)} %get-tuple-element.158.o_ref), calls=%async_computation.1 | async-start | bytes 3145728 | tf_op jit(solution)/shard_map/all_to_all | solution.py:1094
  78.9 39.3 %collective-permute-start.3 = (bf16[384,768]{1,0:T(8,128)(2,1)}, bf16[384,768]{1,0:T(8,128)(2,1)S(1)}, u32[]{:S(2)}, u32[]{:S(2)}) collective-permute-start(bf16[384,768]{1,0:T(8,128)(2,1)} %get-tuple-element.160), channel_id=1, source_target_pairs={{0,16},{4,20},{8,24},{12,28},{16,0},{20,4},{24,8},{28,12},{1,17},{... | collective-permute-start | bytes 1769480 | tf_op jit(solution)/shard_map/ppermute | solution.py:1122
  152.0 27.1 %all-to-all-start.2 = ((bf16[4,800,256]{2,1,0:T(8,128)(2,1)}), bf16[4,800,256]{2,1,0:T(8,128)(2,1)S(1)}, u32[]{:S(2)}, u32[]{:S(2)}) async-start(bf16[4,800,256]{2,1,0:T(8,128)(2,1)} %get-tuple-element.167), calls=%async_computation.2 | async-start | bytes 3276800 | tf_op jit(solution)/shard_map/all_to_all | solution.py:1094
  155.8 21.1 %collective-permute-start.4 = (bf16[128,768]{1,0:T(8,128)(2,1)S(1)}, bf16[128,768]{1,0:T(8,128)(2,1)S(1)}, u32[]{:S(2)}, u32[]{:S(2)}) collective-permute-start(bf16[128,768]{1,0:T(8,128)(2,1)S(1)} %dynamic-slice_bitcast_fusion.8), channel_id=1, source_target_pairs={{0,16},{4,20},{8,24},{12,28},{16,0},{20,4},{24,8},{28,12},{1,17},{... | collective-permute-start | bytes 589832 | tf_op jit(solution)/shard_map/ppermute | solution.py:1071
  194.1 23.7 %all-to-all-start.3 = ((bf16[4,832,256]{2,1,0:T(8,128)(2,1)}), bf16[4,832,256]{2,1,0:T(8,128)(2,1)S(1)}, u32[]{:S(2)}, u32[]{:S(2)}) async-start(bf16[4,832,256]{2,1,0:T(8,128)(2,1)} %get-tuple-element.169), calls=%async_computation.3 | async-start | bytes 3407872 | tf_op jit(solution)/shard_map/all_to_all | solution.py:1094
  197.7 112.6 %reduce-scatter.3.cloned.1.call-start = ((), (), s32[]{:S(2)}) async-start(), calls=%async_computation.10 | async-start | bytes 13271040 | tf_op jit(solution)/shard_map/reduce_scatter | solution.py:1229
  219.1 33.2 %collective-permute-start.5 = (bf16[128,768]{1,0:T(8,128)(2,1)S(1)}, bf16[128,768]{1,0:T(8,128)(2,1)S(1)}, u32[]{:S(2)}, u32[]{:S(2)}) collective-permute-start(bf16[128,768]{1,0:T(8,128)(2,1)S(1)} %get-tuple-element.348), channel_id=1, source_target_pairs={{0,16},{4,20},{8,24},{12,28},{16,0},{20,4},{24,8},{28,12},{1,17},{... | collective-permute-start | bytes 589832 | tf_op jit(solution)/shard_map/ppermute | solution.py:1071
  252.3 26.8 %collective-permute-start.6 = (bf16[352,768]{1,0:T(8,128)(2,1)}, bf16[352,768]{1,0:T(8,128)(2,1)}, u32[]{:S(2)}, u32[]{:S(2)}) collective-permute-start(bf16[352,768]{1,0:T(8,128)(2,1)} %get-tuple-element.190), channel_id=1, source_target_pairs={{0,16},{4,20},{8,24},{12,28},{16,0},{20,4},{24,8},{28,12},{1,17},{... | collective-permute-start | bytes 1622024 | tf_op jit(solution)/shard_map/ppermute | solution.py:1251
  279.1 31.2 %all-to-all-start.4 = ((bf16[4,768,256]{2,1,0:T(8,128)(2,1)}), bf16[4,768,256]{2,1,0:T(8,128)(2,1)S(1)}, u32[]{:S(2)}, u32[]{:S(2)}) async-start(bf16[4,768,256]{2,1,0:T(8,128)(2,1)} %get-tuple-element.194), calls=%async_computation.4 | async-start | bytes 3145728 | tf_op jit(solution)/shard_map/all_to_all | solution.py:1094
  283.0 24.6 %collective-permute-start.7 = (bf16[256,768]{1,0:T(8,128)(2,1)S(1)}, bf16[256,768]{1,0:T(8,128)(2,1)S(1)}, u32[]{:S(2)}, u32[]{:S(2)}) collective-permute-start(bf16[256,768]{1,0:T(8,128)(2,1)S(1)} %copy-done.28), channel_id=1, source_target_pairs={{0,16},{4,20},{8,24},{12,28},{16,0},{20,4},{24,8},{28,12},{1,17},{... | collective-permute-start | bytes 1179656 | tf_op jit(solution)/shard_map/ppermute | solution.py:1251
  319.6 121.4 %reduce-scatter.5.cloned.1.call-start = ((), (), s32[]{:S(2)}) async-start(), calls=%async_computation.11 | async-start | bytes 2985984 | tf_op jit(solution)/shard_map/reduce_scatter | solution.py:1304
  342.1 38.8 %all-to-all-start.6 = ((bf16[4,3,192,256]{3,2,1,0:T(8,128)(2,1)}), bf16[4,3,192,256]{3,2,1,0:T(8,128)(2,1)S(1)}, u32[]{:S(2)}, u32[]{:S(2)}) async-start(bf16[4,3,192,256]{3,2,1,0:T(8,128)(2,1)} %self_backward.1.d_ref), calls=%async_computation.7 | async-start | bytes 2359296 | tf_op jit(solution)/shard_map/all_to_all | solution.py:1094
  345.8 29.6 %collective-permute-start.12 = (bf16[8,96,384]{2,1,0:T(8,128)(2,1)}, bf16[8,96,384]{2,1,0:T(8,128)(2,1)}, u32[]{:S(2)}, u32[]{:S(2)}) collective-permute-start(bf16[8,96,384]{2,1,0:T(8,128)(2,1)} %get-tuple-element.241), channel_id=1, source_target_pairs={{0,2},{1,3},{2,0},{3,1},{4,6},{5,7},{6,4},{7,5},{8,10},{9,11},{10,... | collective-permute-start | bytes 1769480 | tf_op jit(solution)/shard_map/ppermute | solution.py:1265
  350.4 28.1 %collective-permute-start.13 = (bf16[8,96,384]{2,1,0:T(8,128)(2,1)}, bf16[8,96,384]{2,1,0:T(8,128)(2,1)S(1)}, u32[]{:S(2)}, u32[]{:S(2)}) collective-permute-start(bf16[8,96,384]{2,1,0:T(8,128)(2,1)} %get-tuple-element.245), channel_id=1, source_target_pairs={{0,2},{1,3},{2,0},{3,1},{4,6},{5,7},{6,4},{7,5},{8,10},{9,11},{10,... | collective-permute-start | bytes 1769480 | tf_op jit(solution)/shard_map/ppermute | solution.py:1265
  356.8 21.8 %collective-permute-start.11 = (bf16[160,768]{1,0:T(8,128)(2,1)S(1)}, bf16[160,768]{1,0:T(8,128)(2,1)S(1)}, u32[]{:S(2)}, u32[]{:S(2)}) collective-permute-start(bf16[160,768]{1,0:T(8,128)(2,1)S(1)} %copy-done.31), channel_id=1, source_target_pairs={{0,16},{4,20},{8,24},{12,28},{16,0},{20,4},{24,8},{28,12},{1,17},{... | collective-permute-start | bytes 737288 | tf_op jit(solution)/shard_map/ppermute | solution.py:1251
  358.6 16.1 %collective-permute-start.15 = (f32[3,768]{1,0:T(4,128)S(1)}, f32[3,768]{1,0:T(4,128)S(1)}, u32[]{:S(2)}, u32[]{:S(2)}) collective-permute-start(f32[3,768]{1,0:T(4,128)S(1)} %fusion.28), channel_id=1, source_target_pairs={{0,2},{1,3},{2,0},{3,1},{4,6},{5,7},{6,4},{7,5},{8,10},{9,11},{10,... | collective-permute-start | bytes 27656 | tf_op jit(solution)/shard_map/ppermute | solution.py:1265
  384.3 25.9 %all-to-all-start.7 = ((bf16[4,2,192,384]{3,2,1,0:T(8,128)(2,1)}), bf16[4,2,192,384]{3,2,1,0:T(8,128)(2,1)S(1)}, u32[]{:S(2)}, u32[]{:S(2)}) async-start(bf16[4,2,192,384]{3,2,1,0:T(8,128)(2,1)} %sums_for.1), calls=%async_computation.8 | async-start | bytes 2359296 | tf_op jit(solution)/shard_map/all_to_all | solution.py:1094
  393.4 16.7 %collective-permute-start.17 = (bf16[2,3,96,192]{3,2,1,0:T(8,128)(2,1)}, bf16[2,3,96,192]{3,2,1,0:T(8,128)(2,1)S(1)}, u32[]{:S(2)}, u32[]{:S(2)}) collective-permute-start(bf16[2,3,96,192]{3,2,1,0:T(8,128)(2,1)} %get-tuple-element.263), channel_id=1, source_target_pairs={{0,1},{1,0},{2,3},{3,2},{4,5},{5,4},{6,7},{7,6},{8,9},{9,8},{10,11... | collective-permute-start | bytes 663560 | tf_op jit(solution)/shard_map/ppermute | solution.py:1265
  393.5 16.6 %collective-permute-start.18 = (bf16[2,3,96,192]{3,2,1,0:T(8,128)(2,1)S(1)}, bf16[2,3,96,192]{3,2,1,0:T(8,128)(2,1)S(1)}, u32[]{:S(2)}, u32[]{:S(2)}) collective-permute-start(bf16[2,3,96,192]{3,2,1,0:T(8,128)(2,1)S(1)} %copy-done.30), channel_id=1, source_target_pairs={{0,2},{1,3},{2,0},{3,1},{4,6},{5,7},{6,4},{7,5},{8,10},{9,11},{10,... | collective-permute-start | bytes 663560 | tf_op jit(solution)/shard_map/ppermute | solution.py:1265
  416.0 24.2 %collective-permute-start.21 = (bf16[192,384]{1,0:T(8,128)(2,1)}, bf16[192,384]{1,0:T(8,128)(2,1)S(1)}, u32[]{:S(2)}, u32[]{:S(2)}) collective-permute-start(bf16[192,384]{1,0:T(8,128)(2,1)} %get-tuple-element.280), channel_id=1, source_target_pairs={{0,16},{4,20},{8,24},{12,28},{16,0},{20,4},{24,8},{28,12},{1,17},{... | collective-permute-start | bytes 442376 | tf_op jit(solution)/shard_map/ppermute | solution.py:1265
  421.4 18.9 %collective-permute-start.23 = (bf16[3,96,192]{2,1,0:T(8,128)(2,1)}, bf16[3,96,192]{2,1,0:T(8,128)(2,1)S(1)}, u32[]{:S(2)}, u32[]{:S(2)}) collective-permute-start(bf16[3,96,192]{2,1,0:T(8,128)(2,1)} %bitcast.111), channel_id=1, source_target_pairs={{0,4},{1,12},{2,20},{3,28},{4,5},{5,13},{6,21},{7,29},{8,6},{9,14}... | collective-permute-start | bytes 331784 | tf_op jit(solution)/shard_map/ppermute | solution.py:1385
  (44 other events, 363.2 us)
Sparse Core Ops, SparseCore 0:
  218.0 84.8 reduce-scatter.2
  332.4 94.5 reduce-scatter.4

commit v6 on v5

--- a/solution.py
+++ b/solution.py
@@ -231,6 +231,11 @@
         b_refs = refs[1 + 2 * parts : 1 + 3 * parts]
         o_ref, p_ref, m_ref, lse_ref = refs[1 + 3 * parts :]
         head = pl.program_id(0)
+
+        @pl.when(head == 0)
+        def clear():
+            lse_ref[...] = jnp.zeros_like(lse_ref)
+
         query = q_ref[...]
         aug_query = jnp.concatenate([query, jnp.ones((16, length), BF16)], axis=0)
         q_norm = jnp.max(jnp.sum(jnp.square(query.astype(F32)), axis=0, keepdims=True))
@@ -508,6 +513,8 @@
     length, width = inputs.shape
     tokens = length // groups
     rows = mixed.shape[0]
+    wide = 2 if groups % 2 == 0 else 1
+    chunk = wide * tokens
 
     def kernel(s_ref, x_ref, o_ref, w_ref, g_ref, q_ref, qc_ref, h_ref, a_ref):
         after = x_ref[...].astype(F32) + dot(o_ref[...], w_ref[...], 0, 0)
@@ -515,26 +522,28 @@
         scaled = dot(q_ref[...], low, 1, 1).astype(BF16)
         qc_ref[...] = (scaled.astype(F32) * 0.125).astype(BF16)
 
-        @pl.when(pl.program_id(0) == s_ref[0])
-        def keep():
-            h_ref[...] = after
-            a_ref[...] = low
+        for part in range(wide):
+
+            @pl.when(pl.program_id(0) * wide + part == s_ref[0])
+            def keep():
+                h_ref[...] = after[part * tokens : (part + 1) * tokens]
+                a_ref[...] = low[part * tokens : (part + 1) * tokens]
 
     whole = lambda *shape: pl.BlockSpec(shape, lambda i, s: (0,) * len(shape))
     return pl.pallas_call(
         kernel,
         grid_spec=pltpu.PrefetchScalarGridSpec(
             num_scalar_prefetch=1,
-            grid=(groups,),
+            grid=(groups // wide,),
             in_specs=[
-                pl.BlockSpec((tokens, width), lambda i, s: (i, 0)),
-                pl.BlockSpec((rows, tokens), lambda i, s: (0, i)),
+                pl.BlockSpec((chunk, width), lambda i, s: (i, 0)),
+                pl.BlockSpec((rows, chunk), lambda i, s: (0, i)),
                 whole(rows, width),
                 whole(1, width),
                 whole(width, width),
             ],
             out_specs=[
-                pl.BlockSpec((width, tokens), lambda i, s: (0, i)),
+                pl.BlockSpec((width, chunk), lambda i, s: (0, i)),
                 whole(tokens, width),
                 whole(tokens, width),
             ],
@@ -576,7 +585,7 @@
     heads = width // HEAD_DIM
     stat_rows = (parts.shape[1] - width) // 2
     hidden = ffn_in.shape[1]
-    piece = 768
+    piece = 1536
     steps = hidden // piece
     payload = width + 4 * stat_rows
 
@@ -1242,7 +1251,7 @@
             cross_query, subset, cross_prob, place, packed, local_top, earlier, width, groups
         )
 
-    shares = [0, 11, 19, 23, 28]
+    shares = [0, 12, 19, 23, 28]
     marks = [enc_rows * share // 28 for share in shares]
     part_grads, came_key, came_value = rows_backward(1, pairs[1:], None)
     pieces = row_grads(came_key, came_value, cross_kv, marks)

time: 459 us -> 461 us (level)
    ppermute x4, waiting for transfers between devices: 28.4 us -> 33.6 us  [exchange(): lax.ppermute(pieces(lax.rem(mine + step, seqs)), 'blk', shifted(step))]
  transfers between devices with their start and end apart: 36 -> 36, of which waited for: 15 -> 17; matrix products, arithmetic and copies ran while one was open for 6% -> 6% of each run, Pallas kernels for 36% -> 36%
where the time goes in v6:
time: 461 us; the launch traced here: 455 us
  Pallas kernels  210 us (46%)
  waiting for transfers between devices  122 us (26%)
  starting transfers between devices  69.7 us (15%)
  local copies, waits for them, and re-layouts  32.5 us (7%)
  between operations  14.8 us (3%)
  other arithmetic  6.41 us (1%)
    pallas_call x2, Pallas kernels, cross_backward(): pl.pallas_call(kernel, grid=(heads // pair,), in_specs=[pl.BlockSpec((siz...  52.1 us
    ppermute x4, waiting for transfers between devices, exchange(): lax.ppermute(pieces(lax.rem(mine + step, seqs)), 'blk', shifted(step))  33.6 us
    all_to_all x7, waiting for transfers between devices, traded(): return lax.all_to_all(array, 'blk', 0, 0, axis_index_groups=members)  32.8 us
    pallas_call x1, Pallas kernels, cross_forward(): pl.pallas_call(kernel, grid=(heads,), in_specs=[pl.BlockSpec((HEAD_DIM, l...  28.5 us
    all_to_all x7, starting transfers between devices, traded(): return lax.all_to_all(array, 'blk', 0, 0, axis_index_groups=members)  28.3 us
    unnamed x71, local copies, waits for them, and re-layouts  18.8 us
    ppermute x4, waiting for transfers between devices, sent_back(): return lax.ppermute(piece, 'blk', shifted(1))  18.6 us
    ppermute x2, waiting for transfers between devices, body(): got_w.append(lax.ppermute(piece, ('blk', 'dp'), pairs))  15.5 us
  transfers between devices with their start and end apart: 36, of which 17 were waited for; matrix products, arithmetic and copies ran while one was open for 6% of the time, Pallas kernels for 36%

profile of v6, /device:TPU:0, one launch (start us, length us, event | category | flops | bytes accessed | tf_op | source)
XLA Modules:
  0.0 455.2 jit_solution(16154908188602270415)
XLA Ops:
  12.4 9.1 %collective-permute-done = bf16[128,768]{1,0:T(8,128)(2,1)S(1)} collective-permute-done((bf16[128,768]{1,0:T(8,128)(2,1)S(1)}, bf16[128,768]{1,0:T(8,128)(2,1)S(1)}, u32[]{:S(2)}, u32[]{:S(2)}) %collective-permute-start) | collective-permute-done | bytes 196640 | tf_op jit(solution)/shard_map/ppermute | solution.py:1080
  38.3 5.6 %project_rows.3.refs_1_.refs_4_.refs_2_ = bf16[2,768,896]{2,1,0:T(8,128)(2,1)} custom-call(bf16[896,768]{1,0:T(8,128)(2,1)} %dynamic-slice_bitcast_fusion.refs_0_, bf16[2,768,768]{2,1,0:T(8,128)(2,1)} %bitcast.76), custom_call_target="tpu_custom_call" | custom-call | flops 2 | bytes 1 | tf_op jit(solution)/shard_map/project_rows/pallas_call | solution.py:497
  49.9 6.1 %collective-permute-done.1.refs_0_.refs_1_ = bf16[384,768]{1,0:T(8,128)(2,1)S(1)} collective-permute-done((bf16[384,768]{1,0:T(8,128)(2,1)}, bf16[384,768]{1,0:T(8,128)(2,1)S(1)}, u32[]{:S(2)}, u32[]{:S(2)}) %collective-permute-start.1) | collective-permute-done | bytes 589856 | tf_op jit(solution)/shard_map/ppermute | solution.py:1127
  61.0 11.8 %self_forward.1 = (bf16[1024,768]{1,0:T(8,128)(2,1)}, bf16[3,192,1024]{2,1,0:T(8,128)(2,1)}, bf16[4,192,1024]{2,1,0:T(8,128)(2,1)}, bf16[3,1024,1024]{2,1,0:T(8,128)(2,1)}, f32[3,1,1024]{2,1,0:T(1,128)}) custom-call(bf16[1024,768]{1,0:T(8,128)(2,1)} %bitcast.79, f32[1,768]{1,0:T(1,128)} %get-tuple-element.352.g_ref, bf16[3,192,768]{2,1,0:T(8,128)(2,1)} %bitcast.84, ...), custom_call_target="tpu_custom_call" | custom-call | flops 3 | bytes 1 | tf_op jit(solution)/shard_map/self_forward/pallas_call | solution.py:452
  73.5 5.1 %all-to-all-start.1 = ((bf16[4,192,1024]{2,1,0:T(8,128)(2,1)}), bf16[4,192,1024]{2,1,0:T(8,128)(2,1)S(1)}, u32[]{:S(2)}, u32[]{:S(2)}) async-start(bf16[4,192,1024]{2,1,0:T(8,128)(2,1)} %get-tuple-element.158.o_ref), calls=%async_computation.1 | async-start | bytes 3145728 | tf_op jit(solution)/shard_map/all_to_all | solution.py:1103
  88.6 20.2 %all-to-all-done.1 = bf16[4,192,1024]{2,1,0:T(8,128)(2,1)S(1)} async-done(((bf16[4,192,1024]{2,1,0:T(8,128)(2,1)}), bf16[4,192,1024]{2,1,0:T(8,128)(2,1)S(1)}, u32[]{:S(2)}, u32[]{:S(2)}) %all-to-all-start.1) | async-done | bytes 1572896 | tf_op jit(solution)/shard_map/all_to_all | solution.py:1103
  110.0 7.5 %query_stage.1 = (bf16[768,1024]{1,0:T(8,128)(2,1)}, f32[256,768]{1,0:T(8,128)}, bf16[256,768]{1,0:T(8,128)(2,1)}) custom-call(s32[1]{0:T(128)} %bitcast.s_ref.n_ref, bf16[1024,768]{1,0:T(8,128)(2,1)} %bitcast.80, bf16[768,1024]{1,0:T(8,128)(2,1)} %bitcast.82, bf16[768,768]{1,0:T(8,128)(2,1)} %w_ref.7, f32[1,768]{1,0:T(1,128)} %get-tuple-element.351.g_ref, ...), custom_call_target="tpu_custom_call" | custom-call | flops 4 | bytes 1 | tf_op jit(solution)/shard_map/query_stage/pallas_call | solution.py:533
  122.9 28.5 %cross_forward.1 = (bf16[4,800,256]{2,1,0:T(8,128)(2,1)}, bf16[12,1792,1024]{2,1,0:T(8,128)(2,1)}, f32[12,1,1024]{2,1,0:T(1,128)}) custom-call(bf16[768,1024]{1,0:T(8,128)(2,1)} %get-tuple-element.161.refs_0_, bf16[2,768,896]{2,1,0:T(8,128)(2,1)} %project_rows.3.refs_1_.refs_4_.refs_2_, bf16[2,768,384]{2,1,0:T(8,128)(2,1)} %project_rows.4.refs_2_.refs_5_.refs_1_.refs_3_, ...), custom_call_target="tpu_custom_call" | custom-call | flops 22 | bytes 1 | tf_op jit(solution)/shard_map/cross_forward/pallas_call | solution.py:298
  157.3 19.3 %collective-permute-done.4 = bf16[128,768]{1,0:T(8,128)(2,1)S(1)} collective-permute-done((bf16[128,768]{1,0:T(8,128)(2,1)S(1)}, bf16[128,768]{1,0:T(8,128)(2,1)S(1)}, u32[]{:S(2)}, u32[]{:S(2)}) %collective-permute-start.4) | collective-permute-done | bytes 196640 | tf_op jit(solution)/shard_map/ppermute | solution.py:1080
  179.9 13.8 %token_stage.1 = (bf16[256,768]{1,0:T(8,128)(2,1)}, f32[256,768]{1,0:T(8,128)}, bf16[256,768]{1,0:T(8,128)(2,1)}, bf16[256,768]{1,0:T(8,128)(2,1)}, bf16[256,307...) custom-call(bf16[4,800,256]{2,1,0:T(8,128)(2,1)} %copy-done.5, ...), custom_call_target="tpu_custom_call" | custom-call | flops 4 | bytes 1 | tf_op jit(solution)/shard_map/token_stage/pallas_call | solution.py:659
  197.8 13.3 %early_weight_grads.1 = bf16[4,8,432,384]{3,2,1,0:T(8,128)(2,1)} custom-call(bf16[256,768]{1,0:T(8,128)(2,1)} %get-tuple-element.170.a_ref, bf16[256,3072]{1,0:T(8,128)(2,1)} %get-tuple-element.171.du_ref, bf16[256,3072]{1,0:T(8,128)(2,1)} %get-tuple-element.172.z_ref, bf16[256,768]{1,0:T(8,128)(2,1)} %pad_maximum_fusion.1.c_ref, ...), custom_call_target="tpu_custom_call" | custom-call | flops 2 | bytes 1 | tf_op jit(solution)/shard_map/early_weight_grads/pallas_call | solution.py:739
  211.1 6.3 %all-to-all-done.3.refs_6_.refs_7_.refs_4_.refs_5_ = bf16[4,832,256]{2,1,0:T(8,128)(2,1)S(1)} async-done(((bf16[4,832,256]{2,1,0:T(8,128)(2,1)}), bf16[4,832,256]{2,1,0:T(8,128)(2,1)S(1)}, u32[]{:S(2)}, u32[]{:S(2)}) %all-to-all-start.3) | async-done | bytes 1703968 | tf_op jit(solution)/shard_map/all_to_all | solution.py:1103
  219.9 26.4 %cross_backward.2 = (bf16[4,768,256]{2,1,0:T(8,128)(2,1)}, bf16[896,768]{1,0:T(8,128)(2,1)}, bf16[896,768]{1,0:T(8,128)(2,1)}) custom-call(bf16[768,1024]{1,0:T(8,128)(2,1)} %get-tuple-element.161.refs_0_, bf16[2,768,384]{2,1,0:T(8,128)(2,1)} %project_rows.4.refs_2_.refs_5_.refs_1_.refs_3_, bf16[2,768,512]{2,1,0:T(8,128)(2,1)} %project_rows.5.refs_3_.refs_6_.refs_2_.refs_4_, ...), custom_call_target="tpu_custom_call" | custom-call | flops 22 | bytes 1 | tf_op jit(solution)/shard_map/cross_backward/pallas_call | solution.py:396
  246.3 5.8 %row_grads.2 = (bf16[384,768]{1,0:T(8,128)(2,1)}, bf16[224,768]{1,0:T(8,128)(2,1)}, bf16[128,768]{1,0:T(8,128)(2,1)}, bf16[160,768]{1,0:T(8,128)(2,1)}) custom-call(bf16[896,768]{1,0:T(8,128)(2,1)} %get-tuple-element.202.k_ref.refs_5_, bf16[896,768]{1,0:T(8,128)(2,1)} %get-tuple-element.204.v_ref.refs_7_, bf16[2,768,768]{2,1,0:T(8,128)(2,1)} %w_ref.9), custom_call_target="tpu_custom_call" | custom-call | flops 1 | bytes 1 | tf_op jit(solution)/shard_map/row_grads/pallas_call | solution.py:148
  253.0 25.7 %cross_backward.3 = (bf16[4,768,256]{2,1,0:T(8,128)(2,1)}, bf16[896,768]{1,0:T(8,128)(2,1)}, bf16[896,768]{1,0:T(8,128)(2,1)}) custom-call(bf16[768,1024]{1,0:T(8,128)(2,1)} %get-tuple-element.161.refs_0_, bf16[2,768,896]{2,1,0:T(8,128)(2,1)} %project_rows.3.refs_1_.refs_4_.refs_2_, bf16[2,768,896]{2,1,0:T(8,128)(2,1)} %project_rows.3.refs_1_.refs_4_.refs_2_, ...), custom_call_target="tpu_custom_call" | custom-call | flops 22 | bytes 1 | tf_op jit(solution)/shard_map/cross_backward/pallas_call | solution.py:396
  284.8 11.0 %weight_chunks.2 = (bf16[16,96,384]{2,1,0:T(8,128)(2,1)}, bf16[16,96,384]{2,1,0:T(8,128)(2,1)}) custom-call(s32[1]{0:T(128)} %bitcast.24.c_ref, s32[1]{0:T(128)} %bitcast.s_ref.n_ref, bf16[896,768]{1,0:T(8,128)(2,1)} %dynamic-slice_bitcast_fusion.refs_0_, bf16[384,768]{1,0:T(8,128)(2,1)} %copy-done.12, bf16[128,768]{1,0:T(8,128)(2,1)} %copy-done.17, ...), custom_call_target="tpu_custom_call" | custom-call | flops 1 | bytes 1 | tf_op jit(solution)/shard_map/weight_chunks/pallas_call | solution.py:124
  295.8 10.4 %collective-permute-done.7.refs_1_ = bf16[224,768]{1,0:T(8,128)(2,1)S(1)} collective-permute-done((bf16[224,768]{1,0:T(8,128)(2,1)S(1)}, bf16[224,768]{1,0:T(8,128)(2,1)S(1)}, u32[]{:S(2)}, u32[]{:S(2)}) %collective-permute-start.7) | collective-permute-done | bytes 344096 | tf_op jit(solution)/shard_map/ppermute | solution.py:1260
  331.2 9.7 %self_backward.1.d_ref = bf16[4,3,192,256]{3,2,1,0:T(8,128)(2,1)} custom-call(bf16[3,192,1024]{2,1,0:T(8,128)(2,1)} %get-tuple-element.208.q_ref.k_ref.v_ref, bf16[3,192,1024]{2,1,0:T(8,128)(2,1)} %get-tuple-element.208.q_ref.k_ref.v_ref, bf16[3,192,1024]{2,1,0:T(8,128)(2,1)} %get-tuple-element.208.q_ref.k_ref.v_ref, ...), custom_call_target="tpu_custom_call" | custom-call | flops 6 | bytes 1 | tf_op jit(solution)/shard_map/self_backward/pallas_call | solution.py:1019
  349.6 5.3 %own_weight_grads.1 = (bf16[2,3,96,192]{3,2,1,0:T(8,128)(2,1)}, bf16[2,3,96,192]{3,2,1,0:T(8,128)(2,1)}, bf16[2,3,96,192]{3,2,1,0:T(8,128)(2,1)}, bf16[2,3,96,192]{3,2,1,0:T(8,128)(2,1)}, f32[1,768]{1,0:T(1,128)}) custom-call(s32[1]{0:T(128)} %bitcast.30.c_ref, bf16[1024,768]{1,0:T(8,128)(2,1)} %get-tuple-element.246.a_ref, ...), custom_call_target="tpu_custom_call" | custom-call | flops 1 | bytes 1 | tf_op jit(solution)/shard_map/own_weight_grads/pallas_call | solution.py:912
  359.1 14.5 %collective-permute-done.15 = f32[3,768]{1,0:T(4,128)S(1)} collective-permute-done((f32[3,768]{1,0:T(4,128)S(1)}, f32[3,768]{1,0:T(4,128)S(1)}, u32[]{:S(2)}, u32[]{:S(2)}) %collective-permute-start.15) | collective-permute-done | bytes 9248 | tf_op jit(solution)/shard_map/ppermute | solution.py:1274
  387.5 5.5 %input_stage.1 = bf16[256,768]{1,0:T(8,128)(2,1)} custom-call(s32[1]{0:T(128)} %bitcast.s_ref.n_ref, bf16[4,3,192,256]{3,2,1,0:T(8,128)(2,1)} %copy-done.10, bf16[3,768,768]{2,1,0:T(8,128)(2,1)} %w_ref.8, bf16[1024,768]{1,0:T(8,128)(2,1)} %bitcast.81, f32[1,768]{1,0:T(1,128)} %get-tuple-element.352.g_ref, f32[256,768]{1,0:T(8,128)} %get-tuple-element.255.h_ref), custom_call_target="tpu_custom_call" | custom-call | flops 1 | bytes 1 | tf_op jit(solution)/shard_map/input_stage/pallas_call | solution.py:823
  400.5 5.9 %row_grads.3.own_ref = bf16[896,768]{1,0:T(8,128)(2,1)} custom-call(bf16[896,768]{1,0:T(8,128)(2,1)} %get-tuple-element.267.refs_4_.k_ref, bf16[896,768]{1,0:T(8,128)(2,1)} %get-tuple-element.203.refs_6_.v_ref, bf16[2,768,768]{2,1,0:T(8,128)(2,1)} %w_ref.9), custom_call_target="tpu_custom_call" | custom-call | flops 1 | bytes 1 | tf_op jit(solution)/shard_map/row_grads/pallas_call | solution.py:148
  409.7 5.2 %collective-permute-done.16 = bf16[128,768]{1,0:T(8,128)(2,1)S(1)} collective-permute-done((bf16[128,768]{1,0:T(8,128)(2,1)S(1)}, bf16[128,768]{1,0:T(8,128)(2,1)S(1)}, u32[]{:S(2)}, u32[]{:S(2)}) %collective-permute-start.16) | collective-permute-done | bytes 196640 | tf_op jit(solution)/shard_map/ppermute | solution.py:1080
  427.4 15.5 %collective-permute-done.23 = bf16[3,96,192]{2,1,0:T(8,128)(2,1)S(1)} collective-permute-done((bf16[3,96,192]{2,1,0:T(8,128)(2,1)}, bf16[3,96,192]{2,1,0:T(8,128)(2,1)S(1)}, u32[]{:S(2)}, u32[]{:S(2)}) %collective-permute-start.23) | collective-permute-done | bytes 110624 | tf_op jit(solution)/shard_map/ppermute | solution.py:1394
  (186 shorter events, 153.1 us)
Async XLA Ops:
  22.8 37.1 %all-to-all-start = ((bf16[4,256,768]{2,1,0:T(8,128)(2,1)}), bf16[4,256,768]{2,1,0:T(8,128)(2,1)S(1)}, u32[]{:S(2)}, u32[]{:S(2)}) async-start(bf16[4,256,768]{2,1,0:T(8,128)(2,1)} %broadcast_in_dim.104), calls=%async_computation | async-start | bytes 3145728 | tf_op jit(solution)/shard_map/all_to_all | solution.py:1094
  28.7 27.2 %collective-permute-start.1 = (bf16[384,768]{1,0:T(8,128)(2,1)}, bf16[384,768]{1,0:T(8,128)(2,1)S(1)}, u32[]{:S(2)}, u32[]{:S(2)}) collective-permute-start(bf16[384,768]{1,0:T(8,128)(2,1)} %get-tuple-element.333), channel_id=1, source_target_pairs={{0,16},{4,20},{8,24},{12,28},{16,0},{20,4},{24,8},{28,12},{1,17},{... | collective-permute-start | bytes 1769480 | tf_op jit(solution)/shard_map/ppermute | solution.py:1127
  73.5 35.3 %all-to-all-start.1 = ((bf16[4,192,1024]{2,1,0:T(8,128)(2,1)}), bf16[4,192,1024]{2,1,0:T(8,128)(2,1)S(1)}, u32[]{:S(2)}, u32[]{:S(2)}) async-start(bf16[4,192,1024]{2,1,0:T(8,128)(2,1)} %get-tuple-element.158.o_ref), calls=%async_computation.1 | async-start | bytes 3145728 | tf_op jit(solution)/shard_map/all_to_all | solution.py:1103
  78.8 38.6 %collective-permute-start.3 = (bf16[384,768]{1,0:T(8,128)(2,1)}, bf16[384,768]{1,0:T(8,128)(2,1)S(1)}, u32[]{:S(2)}, u32[]{:S(2)}) collective-permute-start(bf16[384,768]{1,0:T(8,128)(2,1)} %get-tuple-element.160), channel_id=1, source_target_pairs={{0,16},{4,20},{8,24},{12,28},{16,0},{20,4},{24,8},{28,12},{1,17},{... | collective-permute-start | bytes 1769480 | tf_op jit(solution)/shard_map/ppermute | solution.py:1131
  151.4 27.3 %all-to-all-start.2 = ((bf16[4,800,256]{2,1,0:T(8,128)(2,1)}), bf16[4,800,256]{2,1,0:T(8,128)(2,1)S(1)}, u32[]{:S(2)}, u32[]{:S(2)}) async-start(bf16[4,800,256]{2,1,0:T(8,128)(2,1)} %get-tuple-element.167), calls=%async_computation.2 | async-start | bytes 3276800 | tf_op jit(solution)/shard_map/all_to_all | solution.py:1103
  155.4 21.1 %collective-permute-start.4 = (bf16[128,768]{1,0:T(8,128)(2,1)S(1)}, bf16[128,768]{1,0:T(8,128)(2,1)S(1)}, u32[]{:S(2)}, u32[]{:S(2)}) collective-permute-start(bf16[128,768]{1,0:T(8,128)(2,1)S(1)} %dynamic-slice_bitcast_fusion.8), channel_id=1, source_target_pairs={{0,16},{4,20},{8,24},{12,28},{16,0},{20,4},{24,8},{28,12},{1,17},{... | collective-permute-start | bytes 589832 | tf_op jit(solution)/shard_map/ppermute | solution.py:1080
  193.7 23.7 %all-to-all-start.3 = ((bf16[4,832,256]{2,1,0:T(8,128)(2,1)}), bf16[4,832,256]{2,1,0:T(8,128)(2,1)S(1)}, u32[]{:S(2)}, u32[]{:S(2)}) async-start(bf16[4,832,256]{2,1,0:T(8,128)(2,1)} %get-tuple-element.169), calls=%async_computation.3 | async-start | bytes 3407872 | tf_op jit(solution)/shard_map/all_to_all | solution.py:1103
  197.3 111.5 %reduce-scatter.3.cloned.1.call-start = ((), (), s32[]{:S(2)}) async-start(), calls=%async_computation.10 | async-start | bytes 13271040 | tf_op jit(solution)/shard_map/reduce_scatter | solution.py:1238
  218.7 33.3 %collective-permute-start.5 = (bf16[128,768]{1,0:T(8,128)(2,1)S(1)}, bf16[128,768]{1,0:T(8,128)(2,1)S(1)}, u32[]{:S(2)}, u32[]{:S(2)}) collective-permute-start(bf16[128,768]{1,0:T(8,128)(2,1)S(1)} %get-tuple-element.348), channel_id=1, source_target_pairs={{0,16},{4,20},{8,24},{12,28},{16,0},{20,4},{24,8},{28,12},{1,17},{... | collective-permute-start | bytes 589832 | tf_op jit(solution)/shard_map/ppermute | solution.py:1080
  252.0 27.0 %collective-permute-start.6 = (bf16[384,768]{1,0:T(8,128)(2,1)}, bf16[384,768]{1,0:T(8,128)(2,1)}, u32[]{:S(2)}, u32[]{:S(2)}) collective-permute-start(bf16[384,768]{1,0:T(8,128)(2,1)} %get-tuple-element.190), channel_id=1, source_target_pairs={{0,16},{4,20},{8,24},{12,28},{16,0},{20,4},{24,8},{28,12},{1,17},{... | collective-permute-start | bytes 1769480 | tf_op jit(solution)/shard_map/ppermute | solution.py:1260
  279.0 29.7 %all-to-all-start.4 = ((bf16[4,768,256]{2,1,0:T(8,128)(2,1)}), bf16[4,768,256]{2,1,0:T(8,128)(2,1)S(1)}, u32[]{:S(2)}, u32[]{:S(2)}) async-start(bf16[4,768,256]{2,1,0:T(8,128)(2,1)} %get-tuple-element.194), calls=%async_computation.4 | async-start | bytes 3145728 | tf_op jit(solution)/shard_map/all_to_all | solution.py:1103
  282.9 23.3 %collective-permute-start.7 = (bf16[224,768]{1,0:T(8,128)(2,1)S(1)}, bf16[224,768]{1,0:T(8,128)(2,1)S(1)}, u32[]{:S(2)}, u32[]{:S(2)}) collective-permute-start(bf16[224,768]{1,0:T(8,128)(2,1)S(1)} %copy-done.28), channel_id=1, source_target_pairs={{0,16},{4,20},{8,24},{12,28},{16,0},{20,4},{24,8},{28,12},{1,17},{... | collective-permute-start | bytes 1032200 | tf_op jit(solution)/shard_map/ppermute | solution.py:1260
  319.1 124.6 %reduce-scatter.5.cloned.1.call-start = ((), (), s32[]{:S(2)}) async-start(), calls=%async_computation.11 | async-start | bytes 2985984 | tf_op jit(solution)/shard_map/reduce_scatter | solution.py:1313
  340.9 39.6 %all-to-all-start.6 = ((bf16[4,3,192,256]{3,2,1,0:T(8,128)(2,1)}), bf16[4,3,192,256]{3,2,1,0:T(8,128)(2,1)S(1)}, u32[]{:S(2)}, u32[]{:S(2)}) async-start(bf16[4,3,192,256]{3,2,1,0:T(8,128)(2,1)} %self_backward.1.d_ref), calls=%async_computation.7 | async-start | bytes 2359296 | tf_op jit(solution)/shard_map/all_to_all | solution.py:1103
  344.7 29.6 %collective-permute-start.12 = (bf16[8,96,384]{2,1,0:T(8,128)(2,1)}, bf16[8,96,384]{2,1,0:T(8,128)(2,1)}, u32[]{:S(2)}, u32[]{:S(2)}) collective-permute-start(bf16[8,96,384]{2,1,0:T(8,128)(2,1)} %get-tuple-element.241), channel_id=1, source_target_pairs={{0,2},{1,3},{2,0},{3,1},{4,6},{5,7},{6,4},{7,5},{8,10},{9,11},{10,... | collective-permute-start | bytes 1769480 | tf_op jit(solution)/shard_map/ppermute | solution.py:1274
  349.0 29.2 %collective-permute-start.13 = (bf16[8,96,384]{2,1,0:T(8,128)(2,1)}, bf16[8,96,384]{2,1,0:T(8,128)(2,1)S(1)}, u32[]{:S(2)}, u32[]{:S(2)}) collective-permute-start(bf16[8,96,384]{2,1,0:T(8,128)(2,1)} %get-tuple-element.245), channel_id=1, source_target_pairs={{0,2},{1,3},{2,0},{3,1},{4,6},{5,7},{6,4},{7,5},{8,10},{9,11},{10,... | collective-permute-start | bytes 1769480 | tf_op jit(solution)/shard_map/ppermute | solution.py:1274
  355.6 22.5 %collective-permute-start.11 = (bf16[160,768]{1,0:T(8,128)(2,1)S(1)}, bf16[160,768]{1,0:T(8,128)(2,1)S(1)}, u32[]{:S(2)}, u32[]{:S(2)}) collective-permute-start(bf16[160,768]{1,0:T(8,128)(2,1)S(1)} %copy-done.31), channel_id=1, source_target_pairs={{0,16},{4,20},{8,24},{12,28},{16,0},{20,4},{24,8},{28,12},{1,17},{... | collective-permute-start | bytes 737288 | tf_op jit(solution)/shard_map/ppermute | solution.py:1260
  383.9 31.1 %all-to-all-start.7 = ((bf16[4,2,192,384]{3,2,1,0:T(8,128)(2,1)}), bf16[4,2,192,384]{3,2,1,0:T(8,128)(2,1)S(1)}, u32[]{:S(2)}, u32[]{:S(2)}) async-start(bf16[4,2,192,384]{3,2,1,0:T(8,128)(2,1)} %sums_for.1), calls=%async_computation.8 | async-start | bytes 2359296 | tf_op jit(solution)/shard_map/all_to_all | solution.py:1103
  393.0 22.0 %collective-permute-start.17 = (bf16[2,3,96,192]{3,2,1,0:T(8,128)(2,1)}, bf16[2,3,96,192]{3,2,1,0:T(8,128)(2,1)S(1)}, u32[]{:S(2)}, u32[]{:S(2)}) collective-permute-start(bf16[2,3,96,192]{3,2,1,0:T(8,128)(2,1)} %get-tuple-element.263), channel_id=1, source_target_pairs={{0,1},{1,0},{2,3},{3,2},{4,5},{5,4},{6,7},{7,6},{8,9},{9,8},{10,11... | collective-permute-start | bytes 663560 | tf_op jit(solution)/shard_map/ppermute | solution.py:1274
  393.0 21.9 %collective-permute-start.18 = (bf16[2,3,96,192]{3,2,1,0:T(8,128)(2,1)S(1)}, bf16[2,3,96,192]{3,2,1,0:T(8,128)(2,1)S(1)}, u32[]{:S(2)}, u32[]{:S(2)}) collective-permute-start(bf16[2,3,96,192]{3,2,1,0:T(8,128)(2,1)S(1)} %copy-done.30), channel_id=1, source_target_pairs={{0,2},{1,3},{2,0},{3,1},{4,6},{5,7},{6,4},{7,5},{8,10},{9,11},{10,... | collective-permute-start | bytes 663560 | tf_op jit(solution)/shard_map/ppermute | solution.py:1274
  394.5 20.4 %collective-permute-start.19 = (bf16[2,3,96,192]{3,2,1,0:T(8,128)(2,1)S(1)}, bf16[2,3,96,192]{3,2,1,0:T(8,128)(2,1)S(1)}, u32[]{:S(2)}, u32[]{:S(2)}) collective-permute-start(bf16[2,3,96,192]{3,2,1,0:T(8,128)(2,1)S(1)} %copy-done.29), channel_id=1, source_target_pairs={{0,3},{1,2},{2,1},{3,0},{4,7},{5,6},{6,5},{7,4},{8,11},{9,10},{10,... | collective-permute-start | bytes 663560 | tf_op jit(solution)/shard_map/ppermute | solution.py:1274
  395.9 19.0 %collective-permute-start.16 = (bf16[128,768]{1,0:T(8,128)(2,1)S(1)}, bf16[128,768]{1,0:T(8,128)(2,1)S(1)}, u32[]{:S(2)}, u32[]{:S(2)}) collective-permute-start(bf16[128,768]{1,0:T(8,128)(2,1)S(1)} %get-tuple-element.344), channel_id=1, source_target_pairs={{0,16},{4,20},{8,24},{12,28},{16,0},{20,4},{24,8},{28,12},{1,17},{... | collective-permute-start | bytes 589832 | tf_op jit(solution)/shard_map/ppermute | solution.py:1080
  420.4 22.5 %collective-permute-start.21 = (bf16[192,384]{1,0:T(8,128)(2,1)}, bf16[192,384]{1,0:T(8,128)(2,1)S(1)}, u32[]{:S(2)}, u32[]{:S(2)}) collective-permute-start(bf16[192,384]{1,0:T(8,128)(2,1)} %get-tuple-element.280), channel_id=1, source_target_pairs={{0,16},{4,20},{8,24},{12,28},{16,0},{20,4},{24,8},{28,12},{1,17},{... | collective-permute-start | bytes 442376 | tf_op jit(solution)/shard_map/ppermute | solution.py:1274
  425.4 17.5 %collective-permute-start.23 = (bf16[3,96,192]{2,1,0:T(8,128)(2,1)}, bf16[3,96,192]{2,1,0:T(8,128)(2,1)S(1)}, u32[]{:S(2)}, u32[]{:S(2)}) collective-permute-start(bf16[3,96,192]{2,1,0:T(8,128)(2,1)} %bitcast.111), channel_id=1, source_target_pairs={{0,4},{1,12},{2,20},{3,28},{4,5},{5,13},{6,21},{7,29},{8,6},{9,14}... | collective-permute-start | bytes 331784 | tf_op jit(solution)/shard_map/ppermute | solution.py:1394
  (44 other events, 365.0 us)
Sparse Core Ops, SparseCore 0:
  217.6 84.8 reduce-scatter.2
  331.2 88.2 reduce-scatter.4
